TPU v7x, 32 devices: a whole 2x2x4 slice. The times are simulated.
32 devices in a mesh: dp: 8 (over z, x), tensor: 4 (over y, core).
Axes of the slice: x: 2, y: 2, z: 4, core: 2. Of those that a mesh axis runs over, the one named last changes fastest.
Arguments:
- coords: float32 [6, 6144], P(None, 'dp'), may hold values from 0 to 2.5, as said below
- model_ids: int32 [6144], P('dp'), may hold values from 0 to 3
- cells: int32 [6144], P('dp'), may hold values from 0 to 65535
- valid: int32 [6144], P('dp'), may hold values 0 or 1
- slowness_grid: float32 [4, 512, 128], replicated, may hold values from 0.2 to 6
- master_blocks: float32 [2, 2, 512, 512], P(None, None, 'dp', 'tensor'), may hold values from -0.25 to 0.25
- small_params: float32 [12, 512], P(None, 'tensor'), may hold values from -1.5 to 1.5
- moment_blocks: float32 [2, 2, 512, 512], P(None, None, 'dp', 'tensor'), may hold values from -1 to 1
- moment_small: float32 [12, 512], P(None, 'tensor'), may hold values from -6 to 6
- average_blocks: float32 [2, 2, 512, 512], P(None, None, 'dp', 'tensor'), may hold values from -0.25 to 0.25
- average_small: float32 [12, 512], P(None, 'tensor'), may hold values from -4 to 4
Outputs:
- loss: float32 [], replicated
- grad_blocks: float32 [2, 2, 512, 512], P(None, None, 'dp', 'tensor')
- grad_small: float32 [12, 512], P(None, 'tensor')
- bias_grads: float32 [4, 512], P(None, 'tensor')
- new_moment_blocks: float32 [2, 2, 512, 512], P(None, None, 'dp', 'tensor')
- new_moment_small: float32 [12, 512], P(None, 'tensor')
- new_master_blocks: float32 [2, 2, 512, 512], P(None, None, 'dp', 'tensor')
- new_small: float32 [12, 512], P(None, 'tensor')
- new_average_blocks: float32 [2, 2, 512, 512], P(None, None, 'dp', 'tensor')
- new_average_small: float32 [12, 512], P(None, 'tensor')
- low_blocks: bfloat16 [2, 2, 512, 512], P(None, None, 'dp', 'tensor')
Inputs may be any that keep to these rules, and one draw needn't show every extreme that they name: `coords`: rows 0 to 2 are a source in the unit cube; the receiver's first coordinate exceeds the source's by 0.5 or more.
All inputs are finite; a program needn't handle non-finite values. No bound on the sum of `valid` on one device may be relied on, other than what follows from the above.
Results may differ from a plain program's by a relative error of at most 0.012.
Values may be sent and summed in bfloat16 or wider, within the bound.
A program may use at most 128 MiB of HBM per device.

v0:
```python
import jax
import jax.numpy as jnp
from jax import lax
from jax.sharding import PartitionSpec as P

LAYERS = 2
MICRO = 3


highest = lax.Precision.HIGHEST
momentum_coef = 0.5
average_decay = 0.5
spread_rate = 0.5
norm_epsilon = 1e-12


def elu(values):
    return jnp.where(values > 0, values, jnp.expm1(jnp.minimum(values, 0.0)))


def slope_of(values):
    return jnp.where(values > 0, 1.0, jnp.exp(jnp.minimum(values, 0.0)))


def curve_of(values):
    return jnp.where(values > 0, 0.0, jnp.exp(jnp.minimum(values, 0.0)))


def layer_forward(streams, w_in, w_out, bias_in, bias_out, widen, narrow):
    acts_low = widen(streams.astype(jnp.bfloat16))
    pre_all = jnp.einsum("sdb,dh->shb", acts_low, w_in, preferred_element_type=jnp.float32)
    value_pre = pre_all[0] + bias_in[:, None]
    slopes = slope_of(value_pre)
    hidden = jnp.concatenate([elu(value_pre)[None], slopes[None] * pre_all[1:]], 0).astype(
        jnp.bfloat16
    )
    partial_sum = jnp.einsum("shb,oh->sob", hidden, w_out, preferred_element_type=jnp.float32)
    branch = narrow(partial_sum)
    updated = streams + branch
    updated = updated.at[0].add(bias_out[:, None])
    return (updated, (acts_low, pre_all, hidden))


def layer_backward(grad_acts, saved_fwd, w_in, w_out, bias_in, expand, shrink):
    acts_low, pre_all, hidden = saved_fwd
    value_pre = pre_all[0] + bias_in[:, None]
    slopes = slope_of(value_pre)
    curves = curve_of(value_pre)
    grad_branch = expand(grad_acts.astype(jnp.bfloat16))
    grad_hidden = jnp.einsum("sob,oh->shb", grad_branch, w_out, preferred_element_type=jnp.float32)
    grad_value = grad_hidden[0] * slopes + jnp.sum(grad_hidden[1:] * pre_all[1:], 0) * curves
    grad_pre = jnp.concatenate([grad_value[None], grad_hidden[1:] * slopes[None]], 0).astype(
        jnp.bfloat16
    )
    grad_bias_in = jnp.sum(grad_value, 1)
    grad_bias_out = jnp.sum(grad_acts[0], 1)
    grad_w_out = jnp.einsum("sob,shb->oh", grad_branch, hidden, preferred_element_type=jnp.float32)
    grad_w_in = jnp.einsum("sdb,shb->dh", acts_low, grad_pre, preferred_element_type=jnp.float32)
    grad_input = jnp.einsum("shb,dh->sdb", grad_pre, w_in, preferred_element_type=jnp.float32)
    return (grad_acts + shrink(grad_input), grad_w_in, grad_w_out, grad_bias_in, grad_bias_out)


def micro_grads(weights, small, coord_rows, model_rows, cell_rows, mask_rows, grid, link_fns):
    widen, narrow, head_sum, expand, shrink = link_fns
    first_rows = small[0:6]
    inner_pre = (
        jnp.einsum("jb,jf->fb", coord_rows, first_rows, precision=highest) + small[6][:, None]
    )
    slopes = slope_of(inner_pre)
    streams = jnp.concatenate([elu(inner_pre)[None], slopes[None] * first_rows[3:6][:, :, None]], 0)
    kept_list = []
    for layer_index in range(LAYERS):
        streams, saved_fwd = layer_forward(
            streams,
            weights[layer_index, 0],
            weights[layer_index, 1],
            small[7 + layer_index],
            small[7 + LAYERS + layer_index],
            widen,
            narrow,
        )
        kept_list.append(saved_fwd)
    out_row = small[7 + 2 * LAYERS]
    projected = head_sum(jnp.einsum("sfb,f->sb", streams, out_row, precision=highest))
    separation = coord_rows[3:6] - coord_rows[0:3]
    distance = jnp.sqrt(jnp.sum(separation * separation, 0))
    direction_unit = separation / distance
    factor_tau = projected[0]
    sign_tau = jnp.sign(factor_tau)
    grad_time = direction_unit * jnp.abs(factor_tau) + distance * sign_tau * projected[1:]
    square = jnp.sum(grad_time * grad_time, 0)
    row_index = cell_rows // grid.shape[2]
    column_index = cell_rows % grid.shape[2]
    picked_rows = grid[model_rows, row_index]
    columns = lax.broadcasted_iota(jnp.int32, picked_rows.shape, 1)
    true_slow = jnp.sum(jnp.where(columns == column_index[:, None], picked_rows, 0.0), 1)
    error_rows = square - true_slow * true_slow
    total_err = jnp.sum(mask_rows * jnp.abs(error_rows))
    count_valid = jnp.sum(mask_rows)
    seed_sign = mask_rows * jnp.sign(error_rows)
    grad_gt = 2.0 * grad_time * seed_sign
    grad_tau = sign_tau * jnp.sum(direction_unit * grad_gt, 0)
    grad_proj = jnp.concatenate([grad_tau[None], distance * sign_tau * grad_gt], 0)
    grad_out_row = jnp.einsum("sfb,sb->f", streams, grad_proj, precision=highest)
    grad_acts = out_row[None, :, None] * grad_proj[:, None, :]
    weight_grads = []
    bias_in_grads = []
    bias_out_grads = []
    for layer_index in reversed(range(LAYERS)):
        grad_acts, grad_w_in, grad_w_out, grad_bias_in, grad_bias_out = layer_backward(
            grad_acts,
            kept_list[layer_index],
            weights[layer_index, 0],
            weights[layer_index, 1],
            small[7 + layer_index],
            expand,
            shrink,
        )
        weight_grads.insert(0, jnp.stack([grad_w_in, grad_w_out]))
        bias_in_grads.insert(0, grad_bias_in)
        bias_out_grads.insert(0, grad_bias_out)
    curves = curve_of(inner_pre)
    grad_inner = (
        grad_acts[0] * slopes + jnp.sum(grad_acts[1:] * first_rows[3:6][:, :, None], 0) * curves
    )
    grad_first = jnp.einsum("jb,fb->jf", coord_rows, grad_inner, precision=highest)
    grad_first = grad_first.at[3:6].add(jnp.sum(grad_acts[1:] * slopes[None], 2))
    grad_small = jnp.concatenate(
        [
            grad_first,
            jnp.sum(grad_inner, 1)[None],
            jnp.stack(bias_in_grads),
            jnp.stack(bias_out_grads),
            grad_out_row[None],
        ],
        0,
    )
    return (jnp.stack(weight_grads), grad_small, total_err, count_valid)


def body(
    coords,
    model_ids,
    cells,
    valid,
    slowness_grid,
    master_blocks,
    small_params,
    moment_blocks,
    moment_small,
    average_blocks,
    average_small,
):
    n_data = lax.axis_size("dp")
    step_rows = coords.shape[1] // MICRO
    shard_low = master_blocks.astype(jnp.bfloat16)
    mask_all = valid.astype(jnp.float32)

    def widen(values):
        return lax.all_gather(values, "tensor", axis=1, tiled=True)

    def narrow(values):
        return lax.psum_scatter(values, "tensor", scatter_dimension=1, tiled=True)

    def head_sum(values):
        return lax.psum(values, "tensor")

    def expand(values):
        return lax.all_gather(values, "tensor", axis=1, tiled=True)

    def shrink(values):
        return lax.psum_scatter(
            values.astype(jnp.bfloat16), "tensor", scatter_dimension=1, tiled=True
        ).astype(jnp.float32)

    link_fns = (widen, narrow, head_sum, expand, shrink)
    shard_sum = jnp.zeros(master_blocks.shape, jnp.float32)
    small_sum = jnp.zeros(small_params.shape, jnp.float32)
    total_err = jnp.zeros((), jnp.float32)
    count_valid = jnp.zeros((), jnp.float32)
    for micro_index in range(MICRO):
        start = micro_index * step_rows
        coord_rows = lax.dynamic_slice_in_dim(coords, start, step_rows, 1)
        model_rows = lax.dynamic_slice_in_dim(model_ids, start, step_rows, 0)
        cell_rows = lax.dynamic_slice_in_dim(cells, start, step_rows, 0)
        mask_rows = lax.dynamic_slice_in_dim(mask_all, start, step_rows, 0)
        weights = lax.all_gather(shard_low, "dp", axis=2, tiled=True)
        grad_blocks, grad_small, micro_total, micro_count = micro_grads(
            weights,
            small_params,
            coord_rows,
            model_rows,
            cell_rows,
            mask_rows,
            slowness_grid,
            link_fns,
        )
        total_err = total_err + micro_total
        count_valid = count_valid + micro_count
        grad_blocks, grad_small = (grad_blocks, grad_small)
        shard_sum = shard_sum + lax.psum_scatter(
            grad_blocks.astype(jnp.bfloat16), "dp", scatter_dimension=2, tiled=True
        ).astype(jnp.float32)
        small_sum = small_sum + grad_small
    small_sum, total_err, count_valid = lax.psum((small_sum, total_err, count_valid), "dp")
    loss = total_err / count_valid
    grad_blocks = shard_sum / count_valid
    grad_small = small_sum / count_valid
    bias_grads = grad_small[7 : 7 + 2 * LAYERS]
    new_moment_blocks = momentum_coef * moment_blocks + grad_blocks
    new_moment_small = momentum_coef * moment_small + grad_small
    dir_blocks = grad_blocks + momentum_coef * new_moment_blocks
    dir_small = grad_small + momentum_coef * new_moment_small
    weight_sq = jnp.concatenate(
        [
            jnp.sum(master_blocks * master_blocks, (2, 3)).reshape(-1),
            (jnp.sum(small_params * small_params) / n_data)[None],
        ]
    )
    dir_sq = jnp.concatenate(
        [
            jnp.sum(dir_blocks * dir_blocks, (2, 3)).reshape(-1),
            (jnp.sum(dir_small * dir_small) / n_data)[None],
        ]
    )
    weight_sq, dir_sq = lax.psum((weight_sq, dir_sq), ("dp", "tensor"))
    step_rate = spread_rate * jnp.sqrt(weight_sq) / jnp.sqrt(dir_sq + norm_epsilon)
    rate_blocks = step_rate[:-1].reshape(LAYERS, 2)
    new_master_blocks = master_blocks - rate_blocks[:, :, None, None] * dir_blocks
    new_small = small_params - step_rate[-1] * dir_small
    new_average_blocks = average_decay * average_blocks + (1.0 - average_decay) * new_master_blocks
    new_average_small = average_decay * average_small + (1.0 - average_decay) * new_small
    return (
        loss,
        grad_blocks,
        grad_small,
        bias_grads,
        new_moment_blocks,
        new_moment_small,
        new_master_blocks,
        new_small,
        new_average_blocks,
        new_average_small,
        new_master_blocks.astype(jnp.bfloat16),
    )


def solution(mesh):
    in_specs = (
        P(None, "dp"),
        P("dp"),
        P("dp"),
        P("dp"),
        P(),
        P(None, None, "dp", "tensor"),
        P(None, "tensor"),
        P(None, None, "dp", "tensor"),
        P(None, "tensor"),
        P(None, None, "dp", "tensor"),
        P(None, "tensor"),
    )
    out_specs = (
        P(),
        P(None, None, "dp", "tensor"),
        P(None, "tensor"),
        P(None, "tensor"),
        P(None, None, "dp", "tensor"),
        P(None, "tensor"),
        P(None, None, "dp", "tensor"),
        P(None, "tensor"),
        P(None, None, "dp", "tensor"),
        P(None, "tensor"),
        P(None, None, "dp", "tensor"),
    )
    return jax.shard_map(body, mesh=mesh, in_specs=in_specs, out_specs=out_specs, check_vma=False)
```

profile of v0, /device:TPU:0, one launch (start us, length us, event | category | flops | bytes accessed | tf_op | source)
XLA Modules:
  0.0 894.2 jit_solution(7646677067643106769)
XLA Ops:
  16.7 33.2 %all_gather.42 = bf16[2,2,512,128]{3,2,1,0:T(8,128)(2,1)S(1)} all-gather(bf16[2,2,64,128]{3,2,1,0:T(8,128)(2,1)S(1)} %get-tuple-element.201), channel_id=1, replica_groups=mesh['dp'=8,'tensor'=4] {'dp'}, dimensions={2}, use_global_device_ids=true | all-gather | bytes 589824 | tf_op jit(solution)/shard_map/all_gather | solution.py:187
  54.6 15.9 %all-gather.17.cloned.1.call-done = bf16[4,512,256]{2,1,0:T(8,128)(2,1)} async-done(((bf16[4,128,256]{2,1,0:T(8,128)(2,1)}), bf16[4,512,256]{2,1,0:T(8,128)(2,1)}) %all-gather.17.cloned.1.call-update) | async-done | bytes 1048592 | tf_op jit(solution)/shard_map/all_gather | solution.py:160
  79.4 2.6 convolution_bitcast_fusion.3
  86.4 22.9 %reduce-scatter.24.cloned.1.call-done = f32[4,128,256]{2,1,0:T(8,128)} async-done(((f32[4,512,256]{2,1,0:T(8,128)}), f32[4,128,256]{2,1,0:T(8,128)}) %reduce-scatter.24.cloned.1.call-update) | async-done | bytes 524304 | tf_op jit(solution)/shard_map/reduce_scatter | solution.py:163
  111.4 31.9 %reduce-scatter.20.cloned.1.call-done = f32[4,128,256]{2,1,0:T(8,128)} async-done(((f32[4,512,256]{2,1,0:T(8,128)}), f32[4,128,256]{2,1,0:T(8,128)}) %reduce-scatter.20.cloned.1.call-update) | async-done | bytes 524304 | tf_op jit(solution)/shard_map/reduce_scatter | solution.py:163
  145.4 31.8 %reduce-scatter.16.cloned.1.call-done = f32[4,128,256]{2,1,0:T(8,128)} async-done(((f32[4,512,256]{2,1,0:T(8,128)}), f32[4,128,256]{2,1,0:T(8,128)}) %reduce-scatter.16.cloned.1.call-update) | async-done | bytes 524304 | tf_op jit(solution)/shard_map/reduce_scatter | solution.py:163
  186.5 13.1 %all-gather.23.cloned.1.call-done = bf16[4,512,256]{2,1,0:T(8,128)(2,1)} async-done(((bf16[4,128,256]{2,1,0:T(8,128)(2,1)}), bf16[4,512,256]{2,1,0:T(8,128)(2,1)}) %all-gather.23.cloned.1.call-update) | async-done | bytes 1048592 | tf_op jit(solution)/shard_map/all_gather | solution.py:160
  202.0 16.0 %all-gather.15.cloned.1.call-done = bf16[4,512,256]{2,1,0:T(8,128)(2,1)} async-done(((bf16[4,128,256]{2,1,0:T(8,128)(2,1)}), bf16[4,512,256]{2,1,0:T(8,128)(2,1)}) %all-gather.15.cloned.1.call-update) | async-done | bytes 1048592 | tf_op jit(solution)/shard_map/all_gather | solution.py:160
  222.2 14.2 %all-gather.19.cloned.1.call-done = bf16[4,512,256]{2,1,0:T(8,128)(2,1)} async-done(((bf16[4,128,256]{2,1,0:T(8,128)(2,1)}), bf16[4,512,256]{2,1,0:T(8,128)(2,1)}) %all-gather.19.cloned.1.call-update) | async-done | bytes 1048592 | tf_op jit(solution)/shard_map/all_gather | solution.py:160
  244.9 2.6 convolution_bitcast_fusion.2
  249.3 2.6 convolution_bitcast_fusion.4
  262.4 12.3 %reduce-scatter.26.cloned.1.call-done = f32[4,128,256]{2,1,0:T(8,128)} async-done(((f32[4,512,256]{2,1,0:T(8,128)}), f32[4,128,256]{2,1,0:T(8,128)}) %reduce-scatter.26.cloned.1.call-update) | async-done | bytes 524304 | tf_op jit(solution)/shard_map/reduce_scatter | solution.py:163
  276.0 32.7 %reduce-scatter.22.cloned.1.call-done = f32[4,128,256]{2,1,0:T(8,128)} async-done(((f32[4,512,256]{2,1,0:T(8,128)}), f32[4,128,256]{2,1,0:T(8,128)}) %reduce-scatter.22.cloned.1.call-update) | async-done | bytes 524304 | tf_op jit(solution)/shard_map/reduce_scatter | solution.py:163
  310.6 32.1 %reduce-scatter.18.cloned.1.call-done = f32[4,128,256]{2,1,0:T(8,128)} async-done(((f32[4,512,256]{2,1,0:T(8,128)}), f32[4,128,256]{2,1,0:T(8,128)}) %reduce-scatter.18.cloned.1.call-update) | async-done | bytes 524304 | tf_op jit(solution)/shard_map/reduce_scatter | solution.py:163
  348.8 10.1 %all-reduce.2 = (f32[4,256]{1,0:T(4,128)S(1)}, f32[4,256]{1,0:T(4,128)S(1)}, f32[4,256]{1,0:T(4,128)S(1)}) all-reduce(f32[4,256]{1,0:T(4,128)S(1)} %bitcast.458, f32[4,256]{1,0:T(4,128)S(1)} %bitcast.457, f32[4,256]{1,0:T(4,128)S(1)} %bitcast.456), channel_id=1, replica_groups=mesh['dp'=8,'tensor'=4] {'tensor'}, use_global_device_ids=true, to_apply=%region_17.18 | all-reduce | flops 3072 | bytes 24576 | tf_op jit(solution)/shard_map/psum | solution.py:166
  363.1 17.3 %all-gather.33.cloned.1.call-done = bf16[4,512,256]{2,1,0:T(8,128)(2,1)} async-done(((bf16[4,128,256]{2,1,0:T(8,128)(2,1)}), bf16[4,512,256]{2,1,0:T(8,128)(2,1)}) %all-gather.33.cloned.1.call-update) | async-done | bytes 1048592 | tf_op jit(solution)/shard_map/all_gather | solution.py:169
  383.6 15.0 %all-gather.29.cloned.1.call-done = bf16[4,512,256]{2,1,0:T(8,128)(2,1)} async-done(((bf16[4,128,256]{2,1,0:T(8,128)(2,1)}), bf16[4,512,256]{2,1,0:T(8,128)(2,1)}) %all-gather.29.cloned.1.call-update) | async-done | bytes 1048592 | tf_op jit(solution)/shard_map/all_gather | solution.py:169
  406.2 22.5 %reduce-scatter.32.cloned.1.call-done = bf16[4,128,256]{2,1,0:T(8,128)(2,1)} async-done(((bf16[4,512,256]{2,1,0:T(8,128)(2,1)}), bf16[4,128,256]{2,1,0:T(8,128)(2,1)}) %reduce-scatter.32.cloned.1.call-update) | async-done | bytes 262160 | tf_op jit(solution)/shard_map/reduce_scatter | solution.py:172
  428.7 27.5 %reduce-scatter.36.cloned.1.call-done = bf16[4,128,256]{2,1,0:T(8,128)(2,1)} async-done(((bf16[4,512,256]{2,1,0:T(8,128)(2,1)}), bf16[4,128,256]{2,1,0:T(8,128)(2,1)}) %reduce-scatter.36.cloned.1.call-update) | async-done | bytes 262160 | tf_op jit(solution)/shard_map/reduce_scatter | solution.py:172
  460.0 15.5 %all-gather.35.cloned.1.call-done = bf16[4,512,256]{2,1,0:T(8,128)(2,1)} async-done(((bf16[4,128,256]{2,1,0:T(8,128)(2,1)}), bf16[4,512,256]{2,1,0:T(8,128)(2,1)}) %all-gather.35.cloned.1.call-update) | async-done | bytes 1048592 | tf_op jit(solution)/shard_map/all_gather | solution.py:169
  478.9 14.8 %all-gather.31.cloned.1.call-done = bf16[4,512,256]{2,1,0:T(8,128)(2,1)} async-done(((bf16[4,128,256]{2,1,0:T(8,128)(2,1)}), bf16[4,512,256]{2,1,0:T(8,128)(2,1)}) %all-gather.31.cloned.1.call-update) | async-done | bytes 1048592 | tf_op jit(solution)/shard_map/all_gather | solution.py:169
  499.4 12.6 %all-gather.25.cloned.1.call-done = bf16[4,512,256]{2,1,0:T(8,128)(2,1)} async-done(((bf16[4,128,256]{2,1,0:T(8,128)(2,1)}), bf16[4,512,256]{2,1,0:T(8,128)(2,1)}) %all-gather.25.cloned.1.call-update) | async-done | bytes 1048592 | tf_op jit(solution)/shard_map/all_gather | solution.py:169
  520.2 19.1 %reduce-scatter.42.cloned.1.call-done = bf16[4,128,256]{2,1,0:T(8,128)(2,1)} async-done(((bf16[4,512,256]{2,1,0:T(8,128)(2,1)}), bf16[4,128,256]{2,1,0:T(8,128)(2,1)}) %reduce-scatter.42.cloned.1.call-update) | async-done | bytes 262160 | tf_op jit(solution)/shard_map/reduce_scatter | solution.py:172
  539.3 27.6 %reduce-scatter.28.cloned.1.call-done = bf16[4,128,256]{2,1,0:T(8,128)(2,1)} async-done(((bf16[4,512,256]{2,1,0:T(8,128)(2,1)}), bf16[4,128,256]{2,1,0:T(8,128)(2,1)}) %reduce-scatter.28.cloned.1.call-update) | async-done | bytes 262160 | tf_op jit(solution)/shard_map/reduce_scatter | solution.py:172
  566.9 27.5 %reduce-scatter.44.cloned.1.call-done = bf16[4,128,256]{2,1,0:T(8,128)(2,1)} async-done(((bf16[4,512,256]{2,1,0:T(8,128)(2,1)}), bf16[4,128,256]{2,1,0:T(8,128)(2,1)}) %reduce-scatter.44.cloned.1.call-update) | async-done | bytes 262160 | tf_op jit(solution)/shard_map/reduce_scatter | solution.py:172
  594.4 3.1 broadcast_multiply_fusion.1
  604.2 10.2 %all-gather.27.cloned.1.call-done = bf16[4,512,256]{2,1,0:T(8,128)(2,1)} async-done(((bf16[4,128,256]{2,1,0:T(8,128)(2,1)}), bf16[4,512,256]{2,1,0:T(8,128)(2,1)}) %all-gather.27.cloned.1.call-update) | async-done | bytes 1048592 | tf_op jit(solution)/shard_map/all_gather | solution.py:169
  663.8 22.5 %all-reduce.1 = (f32[]{:T(128)}, f32[]{:T(128)}, f32[12,128]{1,0:T(8,128)S(1)}) all-reduce(f32[]{:T(128)S(6)} %add.439, f32[]{:T(128)S(6)} %add.441, f32[12,128]{1,0:T(8,128)S(1)} %add_add_fusion), channel_id=1, replica_groups=mesh['dp'=8,'tensor'=4] {'dp'}, use_global_device_ids=true, to_apply=%region_21.22 | all-reduce | flops 1538 | bytes 12304 | tf_op jit(solution)/shard_map/psum | solution.py:205
  689.6 21.2 %reduce-scatter.38.cloned.1.call-done = bf16[2,2,64,128]{3,2,1,0:T(8,128)(2,1)} async-done(((bf16[2,2,512,128]{3,2,1,0:T(8,128)(2,1)}), bf16[2,2,64,128]{3,2,1,0:T(8,128)(2,1)}) %reduce-scatter.38.cloned.1.call-update) | async-done | bytes 65552 | tf_op jit(solution)/shard_map/reduce_scatter | solution.py:201
  710.8 65.0 %reduce-scatter.34.cloned.1.call-done = bf16[2,2,64,128]{3,2,1,0:T(8,128)(2,1)} async-done(((bf16[2,2,512,128]{3,2,1,0:T(8,128)(2,1)}), bf16[2,2,64,128]{3,2,1,0:T(8,128)(2,1)}) %reduce-scatter.34.cloned.1.call-update) | async-done | bytes 65552 | tf_op jit(solution)/shard_map/reduce_scatter | solution.py:201
  775.8 64.6 %reduce-scatter.30.cloned.1.call-done = bf16[2,2,64,128]{3,2,1,0:T(8,128)(2,1)} async-done(((bf16[2,2,512,128]{3,2,1,0:T(8,128)(2,1)}), bf16[2,2,64,128]{3,2,1,0:T(8,128)(2,1)}) %reduce-scatter.30.cloned.1.call-update) | async-done | bytes 65552 | tf_op jit(solution)/shard_map/reduce_scatter | solution.py:201
  842.8 40.0 %all-reduce = (f32[5]{0:T(128)S(1)}, f32[5]{0:T(128)S(1)}) all-reduce(f32[5]{0:T(128)S(1)} %pad_maximum_fusion.46, f32[5]{0:T(128)S(1)} %pad_maximum_fusion.45), channel_id=1, replica_groups=mesh['dp'=8,'tensor'=4] {'dp','tensor'}, use_global_device_ids=true, to_apply=%region_71.72 | all-reduce | flops 10 | bytes 80 | tf_op jit(solution)/shard_map/psum | solution.py:226
  (529 shorter events, 170.2 us)
Async XLA Ops:
  7.2 245.2 %copy-start = (f32[4,512,128]{2,1,0:T(8,128)S(1)}, f32[4,512,128]{2,1,0:T(8,128)}, u32[]{:S(2)}) copy-start(f32[4,512,128]{2,1,0:T(8,128)} %param.33) | copy-start | bytes 3145732
  7.2 42.7 %all-gather.21.cloned.1.call-start = ((), (), s32[]{:S(2)}) async-start(), calls=%async_computation.23 | async-start | bytes 1310720 | tf_op jit(solution)/shard_map/all_gather | solution.py:160
  9.4 230.6 %copy-start.116 = (f32[128]{0:T(128)}, f32[128]{0:T(128)S(1)}, u32[]{:S(2)}) copy-start(f32[128]{0:T(128)S(1)} %get-tuple-element.220) | copy-start | bytes 1540
  14.3 37.9 %all-gather.13.cloned.1.call-start = ((), (), s32[]{:S(2)}) async-start(), calls=%async_computation.15 | async-start | bytes 1310720 | tf_op jit(solution)/shard_map/all_gather | solution.py:160
  15.1 55.4 %all-gather.17.cloned.1.call-start = ((), (), s32[]{:S(2)}) async-start(), calls=%async_computation.19 | async-start | bytes 1310720 | tf_op jit(solution)/shard_map/all_gather | solution.py:160
  15.9 93.4 %reduce-scatter.24.cloned.1.call-start = ((), (), s32[]{:S(2)}) async-start(), calls=%async_computation.24 | async-start | bytes 2621440 | tf_op jit(solution)/shard_map/reduce_scatter | solution.py:163
  77.7 65.6 %reduce-scatter.20.cloned.1.call-start = ((), (), s32[]{:S(2)}) async-start(), calls=%async_computation.20 | async-start | bytes 2621440 | tf_op jit(solution)/shard_map/reduce_scatter | solution.py:163
  82.1 95.1 %reduce-scatter.16.cloned.1.call-start = ((), (), s32[]{:S(2)}) async-start(), calls=%async_computation.16 | async-start | bytes 2621440 | tf_op jit(solution)/shard_map/reduce_scatter | solution.py:163
  86.4 113.3 %all-gather.23.cloned.1.call-start = ((), (), s32[]{:S(2)}) async-start(), calls=%async_computation.25 | async-start | bytes 1310720 | tf_op jit(solution)/shard_map/all_gather | solution.py:160
  182.8 35.3 %all-gather.15.cloned.1.call-start = ((), (), s32[]{:S(2)}) async-start(), calls=%async_computation.17 | async-start | bytes 1310720 | tf_op jit(solution)/shard_map/all_gather | solution.py:160
  184.6 51.8 %all-gather.19.cloned.1.call-start = ((), (), s32[]{:S(2)}) async-start(), calls=%async_computation.21 | async-start | bytes 1310720 | tf_op jit(solution)/shard_map/all_gather | solution.py:160
  186.5 88.2 %reduce-scatter.26.cloned.1.call-start = ((), (), s32[]{:S(2)}) async-start(), calls=%async_computation.26 | async-start | bytes 2621440 | tf_op jit(solution)/shard_map/reduce_scatter | solution.py:163
  243.1 65.6 %reduce-scatter.22.cloned.1.call-start = ((), (), s32[]{:S(2)}) async-start(), calls=%async_computation.22 | async-start | bytes 2621440 | tf_op jit(solution)/shard_map/reduce_scatter | solution.py:163
  247.5 95.2 %reduce-scatter.18.cloned.1.call-start = ((), (), s32[]{:S(2)}) async-start(), calls=%async_computation.18 | async-start | bytes 2621440 | tf_op jit(solution)/shard_map/reduce_scatter | solution.py:163
  252.0 128.4 %all-gather.33.cloned.1.call-start = ((), (), s32[]{:S(2)}) async-start(), calls=%async_computation.35 | async-start | bytes 1310720 | tf_op jit(solution)/shard_map/all_gather | solution.py:169
  362.5 36.1 %all-gather.29.cloned.1.call-start = ((), (), s32[]{:S(2)}) async-start(), calls=%async_computation.31 | async-start | bytes 1310720 | tf_op jit(solution)/shard_map/all_gather | solution.py:169
  363.1 65.6 %reduce-scatter.32.cloned.1.call-start = ((), (), s32[]{:S(2)}) async-start(), calls=%async_computation.32 | async-start | bytes 1310720 | tf_op jit(solution)/shard_map/reduce_scatter | solution.py:172
  403.6 52.5 %reduce-scatter.36.cloned.1.call-start = ((), (), s32[]{:S(2)}) async-start(), calls=%async_computation.36 | async-start | bytes 1310720 | tf_op jit(solution)/shard_map/reduce_scatter | solution.py:172
  406.0 69.5 %all-gather.35.cloned.1.call-start = ((), (), s32[]{:S(2)}) async-start(), calls=%async_computation.37 | async-start | bytes 1310720 | tf_op jit(solution)/shard_map/all_gather | solution.py:169
  458.6 35.1 %all-gather.31.cloned.1.call-start = ((), (), s32[]{:S(2)}) async-start(), calls=%async_computation.33 | async-start | bytes 1310720 | tf_op jit(solution)/shard_map/all_gather | solution.py:169
  459.2 52.8 %all-gather.25.cloned.1.call-start = ((), (), s32[]{:S(2)}) async-start(), calls=%async_computation.27 | async-start | bytes 1310720 | tf_op jit(solution)/shard_map/all_gather | solution.py:169
  460.0 79.3 %reduce-scatter.42.cloned.1.call-start = ((), (), s32[]{:S(2)}) async-start(), calls=%async_computation.40 | async-start | bytes 1310720 | tf_op jit(solution)/shard_map/reduce_scatter | solution.py:172
  499.4 67.6 %reduce-scatter.28.cloned.1.call-start = ((), (), s32[]{:S(2)}) async-start(), calls=%async_computation.28 | async-start | bytes 1310720 | tf_op jit(solution)/shard_map/reduce_scatter | solution.py:172
  517.5 76.9 %reduce-scatter.44.cloned.1.call-start = ((), (), s32[]{:S(2)}) async-start(), calls=%async_computation.41 | async-start | bytes 1310720 | tf_op jit(solution)/shard_map/reduce_scatter | solution.py:172
  519.9 94.5 %all-gather.27.cloned.1.call-start = ((), (), s32[]{:S(2)}) async-start(), calls=%async_computation.29 | async-start | bytes 1310720 | tf_op jit(solution)/shard_map/all_gather | solution.py:169
  597.5 60.3 %reduce-scatter.40.cloned.1.call-start = ((), (), s32[]{:S(2)}) async-start(), calls=%async_computation.39 | async-start | bytes 1310720 | tf_op jit(solution)/shard_map/reduce_scatter | solution.py:172
  620.0 90.8 %reduce-scatter.38.cloned.1.call-start = ((), (), s32[]{:S(2)}) async-start(), calls=%async_computation.38 | async-start | bytes 589824 | tf_op jit(solution)/shard_map/reduce_scatter | solution.py:201
  637.5 138.3 %reduce-scatter.34.cloned.1.call-start = ((), (), s32[]{:S(2)}) async-start(), calls=%async_computation.34 | async-start | bytes 589824 | tf_op jit(solution)/shard_map/reduce_scatter | solution.py:201
  646.7 193.7 %reduce-scatter.30.cloned.1.call-start = ((), (), s32[]{:S(2)}) async-start(), calls=%async_computation.30 | async-start | bytes 589824 | tf_op jit(solution)/shard_map/reduce_scatter | solution.py:201
  659.2 224.3 %copy-start.68 = (f32[2,2,64,128]{3,2,1,0:T(8,128)S(1)}, f32[2,2,64,128]{3,2,1,0:T(8,128)}, u32[]{:S(2)}) copy-start(f32[2,2,64,128]{3,2,1,0:T(8,128)} %param.34) | copy-start | bytes 393220
  659.3 226.9 %copy-start.1 = (f32[4,512,128]{2,1,0:T(8,128)S(1)}, f32[4,512,128]{2,1,0:T(8,128)}, u32[]{:S(2)}) copy-start(f32[4,512,128]{2,1,0:T(8,128)} %param.33) | copy-start | bytes 3145732
  660.9 224.0 %copy-start.132 = (f32[12,128]{1,0:T(8,128)S(1)}, f32[12,128]{1,0:T(8,128)}, u32[]{:S(2)}) copy-start(f32[12,128]{1,0:T(8,128)} %param.39) | copy-start | bytes 18436
  (148 other events, 2133.2 us)
Sparse Core Ops, SparseCore 0:
  14.4 19.4 all-gather.20
  35.4 16.7 all-gather.12
  53.8 16.7 all-gather.16
  77.9 31.4 reduce-scatter.23
  111.9 31.3 reduce-scatter.19
  145.7 31.4 reduce-scatter.15
  182.9 16.7 all-gather.22
  201.3 16.7 all-gather.14
  219.7 16.7 all-gather.18
  243.2 31.4 reduce-scatter.25
  277.2 31.4 reduce-scatter.21
  311.2 31.3 reduce-scatter.17
  362.6 17.7 all-gather.32
  381.8 16.7 all-gather.28
  403.8 24.8 reduce-scatter.31
  431.2 24.8 reduce-scatter.35
  458.8 16.7 all-gather.34
  476.9 16.7 all-gather.30
  495.2 16.7 all-gather.24
  514.4 24.8 reduce-scatter.41
  542.0 24.8 reduce-scatter.27
  569.5 24.9 reduce-scatter.43
  597.7 16.7 all-gather.26
  620.1 24.7 reduce-scatter.39
  648.3 62.4 reduce-scatter.37
  714.4 61.3 reduce-scatter.33
  779.0 61.3 reduce-scatter.29
where the time goes:
time: 897 us; the launch traced here: 894 us
  waiting for transfers between devices  586 us (65%)
  blocking collectives  106 us (12%)
  other arithmetic  82.1 us (9%)
  matrix products  69.5 us (8%)
  local copies, waits for them, and re-layouts  25.1 us (3%)
  between operations  23.9 us (3%)
    reduce_scatter x6, waiting for transfers between devices, narrow(): return lax.psum_scatter(values, 'tensor', scatter_dimension=1, tiled=True)  164 us
    reduce_scatter x3, waiting for transfers between devices, body(): lax.psum_scatter(grad_blocks.astype(jnp.bfloat16), 'dp', scatter_dimensio...  151 us
    reduce_scatter x6, waiting for transfers between devices, shrink(): lax.psum_scatter(values.astype(jnp.bfloat16), 'tensor', scatter_dimension...  124 us
    all_gather x6, waiting for transfers between devices, expand(): return lax.all_gather(values, 'tensor', axis=1, tiled=True)  85.3 us
    all_gather x6, waiting for transfers between devices, widen(): return lax.all_gather(values, 'tensor', axis=1, tiled=True)  60 us
    psum x1, blocking collectives, body(): weight_sq, dir_sq = lax.psum((weight_sq, dir_sq), ('dp', 'tensor'))  40 us
    all_gather x1, blocking collectives, body(): weights = lax.all_gather(shard_low, 'dp', axis=2, tiled=True)  33.2 us
    psum x1, blocking collectives, body(): lax.psum((small_sum, total_err, count_valid), 'dp')  22.5 us
  transfers between devices with their start and end apart: 27, of which 25 were waited for; matrix products, arithmetic and copies ran while one was open for 13% of the time, Pallas kernels for 0%

commit v1 on v0

v1 whole, which is shorter than its diff:
```python
import functools

import jax
import jax.numpy as jnp
from jax import lax
from jax.experimental import pallas as pl
from jax.experimental.pallas import tpu as pltpu
from jax.sharding import PartitionSpec as P

LAYERS = 2
MATS = 2 * LAYERS
SMALL = 12
MESH = pl.DeviceIdType.MESH
F32 = jnp.float32
BF16 = jnp.bfloat16

momentum_coef = 0.5
average_decay = 0.5
spread_rate = 0.5
norm_epsilon = 1e-12

FAR_LAST = 3


def nn(left, right):
    return lax.dot_general(left, right, (((1,), (0,)), ((), ())), preferred_element_type=F32)


def nt(left, right):
    return lax.dot_general(left, right, (((1,), (1,)), ((), ())), preferred_element_type=F32)


def tn(left, right):
    return lax.dot_general(left, right, (((0,), (0,)), ((), ())), preferred_element_type=F32)


def sign_of(v):
    return jnp.where(v > 0, 1.0, jnp.where(v < 0, -1.0, 0.0))


def kernel(
    dims,
    coords_hbm,
    model_hbm,
    cells_hbm,
    valid_hbm,
    grid_hbm,
    master_hbm,
    small_hbm,
    moment_hbm,
    msmall_hbm,
    gsum,
    sred,
    tot,
    coords,
    model,
    cells,
    valid,
    grid,
    master,
    moment,
    msmall,
    spbuf,
    columns,
    wbuf,
    streams,
    acts,
    pre,
    hidden,
    grad,
    gbranch,
    gpre,
    inner,
    gsend,
    gcore,
    gone,
    gslot_g,
    gtwo_g,
    gslot_z,
    gtwo_z,
    gback_g,
    sgsend,
    sgcore,
    sgone,
    sgslot_g,
    sgtwo,
    sgslot_z,
    arslot_g,
    artwo,
    arslot_z,
    in_sem,
    w_send,
    w_recv,
    g_send,
    g_recv,
    s_send,
    s_recv,
):
    A, B, C, R, cw, Pn, D = dims
    n_t = 2 * C
    G = C * B
    dp = lax.axis_index("dp")
    t = lax.axis_index("tensor")
    a, b = dp // B, dp % B
    y, c = t // 2, t % 2
    g = y * B + b

    def device(a_, g_, c_):
        return (a_ * B + g_ % B, (g_ // B) * 2 + c_)

    far = [(a + k) % A for k in range(1, A)]
    near = [(g + k) % G for k in range(1, G)]
    z_devices = [device(o, g, c) for o in far]
    g_devices = [device(a, o, c) for o in near]
    core_device = device(a, g, 1 - c)
    group = [(o, 1 - c) for o in near]
    q_devices = g_devices + [device(a, o, cc) for o, cc in group] + [core_device]
    q_slots = [o * 2 + c for o in near] + [o * 2 + cc for o, cc in group] + [g * 2 + 1 - c]
    NQ = 2 * G
    FAR, NEAR, CORE = 0, A - 1, A + G - 2

    S1 = 1
    S2 = S1 + G - 1
    S3 = S2 + A - 1
    S4 = S3 + NQ - 1
    S5 = S4 + n_t - 1

    sends = []

    def remote(src, dst, ssem, rsem, device_id):
        copy = pltpu.make_async_remote_copy(
            src_ref=src,
            dst_ref=dst,
            send_sem=ssem,
            recv_sem=rsem,
            device_id=device_id,
            device_id_type=MESH,
        )
        copy.start()
        sends.append(copy)
        return copy

    def arrived(copies):
        for copy in copies:
            copy.wait_recv()

    local = []
    for i, (src, dst) in enumerate(
        [
            (master_hbm, master),
            (small_hbm, spbuf.at[t]),
            (coords_hbm, coords),
            (model_hbm, model),
            (cells_hbm, cells),
            (valid_hbm, valid),
            (grid_hbm, grid),
            (moment_hbm, moment),
            (msmall_hbm, msmall),
        ]
    ):
        copy = pltpu.make_async_copy(src, dst, in_sem.at[i])
        copy.start()
        local.append(copy)

    barrier = pltpu.get_barrier_semaphore()
    peers = z_devices + q_devices
    for d in peers:
        pl.semaphore_signal(barrier, inc=1, device_id=d, device_id_type=MESH)

    local[0].wait()
    for m in range(MATS):
        wbuf[m, c, y, a, b] = master[m // 2, m % 2].astype(BF16)
    local[1].wait()
    pl.semaphore_wait(barrier, len(peers))

    def w_far(m, src_of):
        return [
            remote(src_of(m), src_of(m), w_send.at[m, FAR + k], w_recv.at[m, FAR + k], d)
            for k, d in enumerate(z_devices)
        ]

    def w_near(m, src_of):
        return [
            remote(src_of(m), src_of(m), w_send.at[m, NEAR + k], w_recv.at[m, NEAR + k], d)
            for k, d in enumerate(g_devices)
        ]

    def own(m):
        return wbuf.at[m, c, y, a, b]

    def line(m):
        return wbuf.at[m, c, y, :, b]

    def plane(m):
        return wbuf.at[m, c, :, a]

    def w_core(m):
        return [remote(wbuf.at[m, c], wbuf.at[m, c], w_send.at[m, CORE], w_recv.at[m, CORE], core_device)]

    def owner_t(o, cc):
        return (o // B) * 2 + cc

    first = {}
    normal = [m for m in range(MATS) if m != FAR_LAST]
    sp_copies = []
    for k in range(1, n_t):
        o = (t + k) % n_t
        sp_copies.append(
            remote(spbuf.at[t], spbuf.at[t], s_send.at[S4 + k - 1], s_recv.at[S4 + k - 1], (dp, o))
        )
    for i, m in enumerate(normal):
        first[m] = w_far(m, own)
        if i == 0:
            first[FAR_LAST] = w_near(FAR_LAST, own)

    for copy in local[2:7]:
        copy.wait()
    cols = grid.shape[2]
    shift = (cols - 1).bit_length()
    cell = cells[...].reshape(1, -1)
    row_id = model[...].reshape(1, -1) * grid.shape[1] + (cell >> shift)
    col_id = cell & (cols - 1)
    PB = row_id.shape[1]
    packed = jnp.concatenate(
        [
            coords[...],
            row_id.astype(F32),
            col_id.astype(F32),
            valid[...].reshape(1, -1).astype(F32),
            jnp.zeros((128 - 9, PB), F32),
        ],
        0,
    )
    columns[...] = packed.T
    mine = columns[pl.ds(pl.multiple_of(t * Pn, 8), Pn), :]
    xs = [mine[:, j : j + 1] for j in range(6)]
    mask = mine[:, 8:9]
    row_of = mine[:, 6:7].astype(jnp.int32)
    col_of = mine[:, 7:8].astype(jnp.int32)
    table = grid[...].reshape(-1, cols)
    onehot = (
        lax.broadcasted_iota(jnp.int32, (Pn, table.shape[0]), 1) == row_of
    ).astype(BF16)
    high = table.astype(BF16)
    rest = table - high.astype(F32)
    middle = rest.astype(BF16)
    lowest = (rest - middle.astype(F32)).astype(BF16)
    picked = nn(onehot, high) + nn(onehot, middle) + nn(onehot, lowest)
    lane = lax.broadcasted_iota(jnp.int32, (Pn, cols), 1)
    truth = jnp.sum(jnp.where(lane == col_of, picked, 0.0), 1, keepdims=True)
    seps = [xs[3 + k] - xs[k] for k in range(3)]
    distance = jnp.sqrt(seps[0] * seps[0] + seps[1] * seps[1] + seps[2] * seps[2])
    units = [s / distance for s in seps]

    arrived(sp_copies)

    def small_row(i):
        return jnp.concatenate([spbuf[tt, i : i + 1, :] for tt in range(n_t)], 1)

    first_rows = [small_row(j) for j in range(6)]
    z0 = small_row(6) + xs[0] * first_rows[0]
    for j in range(1, 6):
        z0 = z0 + xs[j] * first_rows[j]
    inner[...] = z0
    e0 = jnp.exp(jnp.minimum(z0, 0.0))
    slope0 = jnp.where(z0 > 0, 1.0, e0)
    streams[0] = jnp.where(z0 > 0, z0, e0 - 1.0)
    acts[0, 0] = streams[0].astype(BF16)
    for k in range(3):
        streams[1 + k] = slope0 * first_rows[3 + k]
        acts[0, 1 + k] = streams[1 + k].astype(BF16)

    second = {}
    arrived(first[FAR_LAST])
    second[FAR_LAST] = w_far(FAR_LAST, plane)
    for m in normal:
        arrived(first[m])
        second[m] = w_near(m, line)

    third = {}

    def weight(m):
        return jnp.concatenate([wbuf[m, tt % 2, tt // 2].reshape(D, cw) for tt in range(n_t)], 1)

    M = 4 * Pn

    def block_in(l):
        pre[l] = nn(acts[l].reshape(M, D), weight(2 * l)).reshape(4, Pn, D)
        z = pre[l, 0] + small_row(7 + l)
        e = jnp.exp(jnp.minimum(z, 0.0))
        slope = jnp.where(z > 0, 1.0, e)
        hidden[l, 0] = jnp.where(z > 0, z, e - 1.0).astype(BF16)
        for k in range(1, 4):
            hidden[l, k] = (slope * pre[l, k]).astype(BF16)

    def block_out(l):
        branch = nt(hidden[l].reshape(M, D), weight(2 * l + 1)).reshape(4, Pn, D)
        for s in range(4):
            new = streams[s] + branch[s]
            if s == 0:
                new = new + small_row(7 + LAYERS + l)
            streams[s] = new
            if l + 1 < LAYERS:
                acts[l + 1, s] = new.astype(BF16)

    def fetch(m):
        arrived(second[m])
        third[m] = w_core(m)

    for m in range(MATS):
        fetch(m)
        arrived(third[m])
        if m % 2 == 0:
            block_in(m // 2)
        else:
            block_out(m // 2)

    out_row = small_row(7 + 2 * LAYERS)
    proj = [jnp.sum(streams[s] * out_row, 1, keepdims=True) for s in range(4)]
    tau = proj[0]
    sign_tau = sign_of(tau)
    abs_tau = jnp.abs(tau)
    grad_time = [units[k] * abs_tau + distance * sign_tau * proj[1 + k] for k in range(3)]
    square = grad_time[0] * grad_time[0] + grad_time[1] * grad_time[1] + grad_time[2] * grad_time[2]
    error = square - truth * truth
    total_err = jnp.sum(mask * jnp.abs(error), axis=0, keepdims=True)
    count = jnp.sum(mask, axis=0, keepdims=True)
    seed = mask * sign_of(error)
    g_time = [2.0 * grad_time[k] * seed for k in range(3)]
    g_tau = sign_tau * (units[0] * g_time[0] + units[1] * g_time[1] + units[2] * g_time[2])
    g_proj = [g_tau] + [distance * sign_tau * g_time[k] for k in range(3)]
    g_out_row = jnp.sum(
        streams[0] * g_proj[0] + streams[1] * g_proj[1] + streams[2] * g_proj[2] + streams[3] * g_proj[3],
        axis=0,
        keepdims=True,
    )
    for s in range(4):
        value = g_proj[s] * out_row
        grad[s] = value
        gbranch[s] = value.astype(BF16)

    flying = {}

    def start_core(m, value):
        low = value.astype(BF16)
        for tt in range(n_t):
            gsend[m, tt % 2, tt // 2] = low[:, tt * cw : (tt + 1) * cw].reshape(A, B, R, cw)
        flying[m] = [
            remote(gsend.at[m, 1 - c], gcore.at[m], g_send.at[m, CORE], g_recv.at[m, CORE], core_device)
        ]

    def core_sum(m):
        arrived(flying[m])
        return (gsend[m, c].astype(F32) + gcore[m].astype(F32)).astype(BF16)

    def slot_sum(ref, count_of):
        value = ref[0].astype(F32)
        for i in range(1, count_of):
            value = value + ref[i].astype(F32)
        return value

    def start_near(m):
        gone[m] = core_sum(m)
        gslot_g[m, g] = gone[m, y, :, b]
        flying[m] = [
            remote(
                gone.at[m, o // B, :, o % B],
                gslot_g.at[m, g],
                g_send.at[m, NEAR + k],
                g_recv.at[m, NEAR + k],
                g_devices[k],
            )
            for k, o in enumerate(near)
        ]

    def start_far(m):
        arrived(flying[m])
        gtwo_g[m] = slot_sum(gslot_g.at[m], G).astype(BF16)
        gslot_z[m, a] = gtwo_g[m, a]
        flying[m] = [
            remote(gtwo_g.at[m, o], gslot_z.at[m, a], g_send.at[m, FAR + k], g_recv.at[m, FAR + k], z_devices[k])
            for k, o in enumerate(far)
        ]

    def start_far_first(m):
        gone[m] = core_sum(m)
        gtwo_z[a] = gone[m, :, a]
        flying[m] = [
            remote(
                gone.at[m, :, o], gtwo_z.at[a], g_send.at[m, FAR + k], g_recv.at[m, FAR + k], z_devices[k]
            )
            for k, o in enumerate(far)
        ]

    def start_near_last(m):
        arrived(flying[m])
        total = slot_sum(gtwo_z, A).astype(BF16)
        for i in range(G):
            gback_g[0, i] = total[i // B, i % B]
        gback_g[1, g] = gback_g[0, g]
        flying[m] = [
            remote(gback_g.at[0, o], gback_g.at[1, g], g_send.at[m, NEAR + k], g_recv.at[m, NEAR + k], g_devices[k])
            for k, o in enumerate(near)
        ]

    bias_in = [None] * LAYERS
    bias_out = [None] * LAYERS

    def back_out(l):
        bias_out[l] = jnp.sum(grad[0], axis=0, keepdims=True)
        gb = gbranch[...].reshape(M, D)
        start_core(2 * l + 1, tn(gb, hidden[l].reshape(M, D)))

    def back_in(l):
        gb = gbranch[...].reshape(M, D)
        gh = nn(gb, weight(2 * l + 1)).reshape(4, Pn, D)
        z = pre[l, 0] + small_row(7 + l)
        e = jnp.exp(jnp.minimum(z, 0.0))
        slope = jnp.where(z > 0, 1.0, e)
        curve = jnp.where(z > 0, 0.0, e)
        gz = gh[0] * slope + curve * (gh[1] * pre[l, 1] + gh[2] * pre[l, 2] + gh[3] * pre[l, 3])
        bias_in[l] = jnp.sum(gz, axis=0, keepdims=True)
        gpre[0] = gz.astype(BF16)
        for k in range(1, 4):
            gpre[k] = (gh[k] * slope).astype(BF16)
        start_core(2 * l, tn(acts[l].reshape(M, D), gpre[...].reshape(M, D)))

    def back_through(l):
        back = nt(gpre[...].reshape(M, D), weight(2 * l)).reshape(4, Pn, D)
        for s in range(4):
            value = grad[s] + back[s]
            grad[s] = value
            if l > 0:
                gbranch[s] = value.astype(BF16)

    def forward_first(m):
        if m == FAR_LAST:
            start_far_first(m)
        else:
            start_near(m)

    back_out(1)
    back_in(1)
    forward_first(3)
    back_through(1)
    back_out(0)
    forward_first(2)
    back_in(0)
    forward_first(1)
    back_through(0)
    forward_first(0)

    z0 = inner[...]
    e0 = jnp.exp(jnp.minimum(z0, 0.0))
    slope0 = jnp.where(z0 > 0, 1.0, e0)
    curve0 = jnp.where(z0 > 0, 0.0, e0)
    first_rows = [small_row(j) for j in range(6)]
    g_inner = grad[0] * slope0 + curve0 * (
        grad[1] * first_rows[3] + grad[2] * first_rows[4] + grad[3] * first_rows[5]
    )
    rows = [jnp.sum(xs[j] * g_inner, axis=0, keepdims=True) for j in range(6)]
    for k in range(3):
        rows[3 + k] = rows[3 + k] + jnp.sum(grad[1 + k] * slope0, axis=0, keepdims=True)
    rows.append(jnp.sum(g_inner, axis=0, keepdims=True))
    rows = rows + bias_in + bias_out + [g_out_row]

    lanes = lax.broadcasted_iota(jnp.int32, (1, cw), 1)
    weight_sq = jnp.zeros((1, cw), F32)
    for m in range(MATS):
        part = jnp.sum(master[m // 2, m % 2] * master[m // 2, m % 2], keepdims=True)
        weight_sq = jnp.where(lanes == m, part, weight_sq)
    own_small = spbuf[t]
    weight_sq = jnp.where(lanes == MATS, jnp.sum(own_small * own_small, keepdims=True) / (A * B), weight_sq)
    tail = [
        jnp.broadcast_to(total_err, (1, cw)),
        jnp.broadcast_to(count, (1, cw)),
        weight_sq,
        jnp.zeros((1, cw), F32),
    ]
    for tt in range(n_t):
        sgsend[tt % 2, tt // 2] = jnp.concatenate([r[:, tt * cw : (tt + 1) * cw] for r in rows] + tail, 0)
    sg = [remote(sgsend.at[1 - c], sgcore, s_send.at[0], s_recv.at[0], core_device)]
    arrived(sg)
    sgone[...] = sgsend[c] + sgcore[...]
    sgslot_g[g] = sgone[y]
    sg = [
        remote(sgone.at[o // B], sgslot_g.at[g], s_send.at[S1 + k], s_recv.at[S1 + k], g_devices[k])
        for k, o in enumerate(near)
    ]

    start_near_last(FAR_LAST)
    for m in reversed(normal):
        start_far(m)
    arrived(sg)
    sgtwo[...] = slot_sum(sgslot_g, G)
    sgslot_z[a] = sgtwo[...]
    sg = [
        remote(sgtwo, sgslot_z.at[a], s_send.at[S2 + k], s_recv.at[S2 + k], z_devices[k]) for k in range(A - 1)
    ]

    for copy in local[7:]:
        copy.wait()
    arrived(flying[FAR_LAST])
    for i in range(MATS):
        m = MATS - 1 - i
        if m == FAR_LAST:
            gsum[m] = slot_sum(gback_g.at[1], G)
        else:
            arrived(flying[m])
            gsum[m] = slot_sum(gslot_z.at[m], A)
    arrived(sg)
    sred[...] = slot_sum(sgslot_z, A)
    counted = sred[SMALL + 1 : SMALL + 2, 0:1]
    tile_rows = lax.broadcasted_iota(jnp.int32, (8, 128), 0)
    parts = jnp.zeros((8, 128), F32)
    for m in range(MATS):
        gr = gsum[m] / counted
        direction = gr + momentum_coef * (momentum_coef * moment[m // 2, m % 2] + gr)
        parts = jnp.where(tile_rows == m, jnp.sum(direction * direction, keepdims=True), parts)
    gr = sred[0:SMALL, :] / counted
    direction = gr + momentum_coef * (momentum_coef * msmall[...] + gr)
    parts = jnp.where(
        tile_rows == MATS, jnp.sum(direction * direction, keepdims=True) / (A * B), parts
    )
    me = g * 2 + c
    arslot_g[me] = parts
    ar = [
        remote(arslot_g.at[me], arslot_g.at[me], s_send.at[S3 + k], s_recv.at[S3 + k], d)
        for k, d in enumerate(q_devices)
    ]
    arrived(ar)
    artwo[...] = slot_sum(arslot_g, NQ)
    arslot_z[a] = artwo[...]
    ar = [
        remote(artwo, arslot_z.at[a], s_send.at[S5 + k], s_recv.at[S5 + k], d) for k, d in enumerate(z_devices)
    ]
    arrived(ar)
    tot[...] = slot_sum(arslot_z, A)

    for copy in sends:
        copy.wait_send()


def body(
    axes,
    coords,
    model_ids,
    cells,
    valid,
    slowness_grid,
    master_blocks,
    small_params,
    moment_blocks,
    moment_small,
    average_blocks,
    average_small,
):
    n_dp, n_t = axes
    A = 4 if n_dp % 4 == 0 else n_dp
    B = n_dp // A
    C = n_t // 2
    G = C * B
    R, cw = master_blocks.shape[2:]
    D = R * n_dp
    PB = coords.shape[1]
    Pn = PB // n_t
    dims = (A, B, C, R, cw, Pn, D)
    anywhere = pl.BlockSpec(memory_space=pl.ANY)
    vmem = pl.BlockSpec(memory_space=pltpu.VMEM)
    S = SMALL + 4
    args = (
        coords,
        model_ids,
        cells,
        valid,
        slowness_grid,
        master_blocks,
        small_params,
        moment_blocks,
        moment_small,
    )
    V = pltpu.VMEM
    gsum, sred, tot = pl.pallas_call(
        functools.partial(kernel, dims),
        out_shape=(
            jax.ShapeDtypeStruct((MATS, R, cw), F32),
            jax.ShapeDtypeStruct((S, cw), F32),
            jax.ShapeDtypeStruct((8, 128), F32),
        ),
        in_specs=[anywhere] * len(args),
        out_specs=(vmem,) * 3,
        scratch_shapes=[
            V(coords.shape, F32),
            V((PB,), jnp.int32),
            V((PB,), jnp.int32),
            V((PB,), jnp.int32),
            V(slowness_grid.shape, F32),
            V(master_blocks.shape, F32),
            V(master_blocks.shape, F32),
            V(small_params.shape, F32),
            V((n_t, SMALL, cw), F32),
            V((PB, 128), F32),
            V((MATS, 2, C, A, B, R, cw), BF16),
            V((4, Pn, D), F32),
            V((LAYERS, 4, Pn, D), BF16),
            V((LAYERS, 4, Pn, D), F32),
            V((LAYERS, 4, Pn, D), BF16),
            V((4, Pn, D), F32),
            V((4, Pn, D), BF16),
            V((4, Pn, D), BF16),
            V((Pn, D), F32),
            V((MATS, 2, C, A, B, R, cw), BF16),
            V((MATS, C, A, B, R, cw), BF16),
            V((MATS, C, A, B, R, cw), BF16),
            V((MATS, G, A, R, cw), BF16),
            V((MATS, A, R, cw), BF16),
            V((MATS, A, R, cw), BF16),
            V((A, C, B, R, cw), BF16),
            V((2, G, R, cw), BF16),
            V((2, C, S, cw), F32),
            V((C, S, cw), F32),
            V((C, S, cw), F32),
            V((G, S, cw), F32),
            V((S, cw), F32),
            V((A, S, cw), F32),
            V((2 * G, 8, 128), F32),
            V((8, 128), F32),
            V((A, 8, 128), F32),
            pltpu.SemaphoreType.DMA((len(args),)),
            pltpu.SemaphoreType.DMA((MATS, A + G - 1)),
            pltpu.SemaphoreType.DMA((MATS, A + G - 1)),
            pltpu.SemaphoreType.DMA((MATS, A + G - 1)),
            pltpu.SemaphoreType.DMA((MATS, A + G - 1)),
            pltpu.SemaphoreType.DMA((G + 2 * A + 2 * G + n_t,)),
            pltpu.SemaphoreType.DMA((G + 2 * A + 2 * G + n_t,)),
        ],
        compiler_params=pltpu.CompilerParams(
            collective_id=0, has_side_effects=True, vmem_limit_bytes=60 << 20
        ),
    )(*args)

    total_err = sred[SMALL, 0]
    count_valid = sred[SMALL + 1, 0]
    weight_sq = sred[SMALL + 2, 0 : MATS + 1]
    dir_sq = tot[0 : MATS + 1, 0]
    loss = total_err / count_valid
    grad_blocks = gsum.reshape(master_blocks.shape) / count_valid
    grad_small = sred[0:SMALL] / count_valid
    bias_grads = grad_small[7 : 7 + 2 * LAYERS]
    new_moment_blocks = momentum_coef * moment_blocks + grad_blocks
    new_moment_small = momentum_coef * moment_small + grad_small
    dir_blocks = grad_blocks + momentum_coef * new_moment_blocks
    dir_small = grad_small + momentum_coef * new_moment_small
    step_rate = spread_rate * jnp.sqrt(weight_sq) / jnp.sqrt(dir_sq + norm_epsilon)
    rate_blocks = step_rate[:-1].reshape(LAYERS, 2)
    new_master_blocks = master_blocks - rate_blocks[:, :, None, None] * dir_blocks
    new_small = small_params - step_rate[-1] * dir_small
    new_average_blocks = average_decay * average_blocks + (1.0 - average_decay) * new_master_blocks
    new_average_small = average_decay * average_small + (1.0 - average_decay) * new_small
    return (
        loss,
        grad_blocks,
        grad_small,
        bias_grads,
        new_moment_blocks,
        new_moment_small,
        new_master_blocks,
        new_small,
        new_average_blocks,
        new_average_small,
        new_master_blocks.astype(BF16),
    )


def solution(mesh):
    blocks = P(None, None, "dp", "tensor")
    small = P(None, "tensor")
    in_specs = (
        P(None, "dp"),
        P("dp"),
        P("dp"),
        P("dp"),
        P(),
        blocks,
        small,
        blocks,
        small,
        blocks,
        small,
    )
    out_specs = (P(), blocks, small, small, blocks, small, blocks, small, blocks, small, blocks)
    axes = (mesh.shape["dp"], mesh.shape["tensor"])
    return jax.shard_map(
        functools.partial(body, axes), mesh=mesh, in_specs=in_specs, out_specs=out_specs, check_vma=False
    )
```

time: 897 us -> 63.5 us (0.07)
  waiting for transfers between devices: 586 us -> 0 us
  blocking collectives: 106 us -> 0 us
  other arithmetic: 82.1 us -> 5.74 us
  matrix products: 69.5 us -> 0 us
  Pallas kernels: 0 us -> 52.2 us
  local copies, waits for them, and re-layouts: 25.1 us -> 2.03 us
  between operations: 23.9 us -> 3.2 us
    reduce_scatter x15 -> x0, waiting for transfers between devices: 439 us -> none  [the longest x6 164 us: narrow(): return lax.psum_scatter(values, 'tensor', scatter_dimension=1, tiled=True)]
    all_gather x12 -> x0, waiting for transfers between devices: 145 us -> none  [the longest x6 85.3 us: expand(): return lax.all_gather(values, 'tensor', axis=1, tiled=True)]
    psum x3 -> x0, blocking collectives: 72.6 us -> none  [the longest x1 40 us: body(): weight_sq, dir_sq = lax.psum((weight_sq, dir_sq), ('dp', 'tensor'))]
    dot_general x48 -> x0, matrix products: 69.5 us -> none  [the longest x6 14 us: layer_forward(): jnp.einsum('shb,oh->sob', hidden, w_out, preferred_element_type=jnp.float32)]
    pallas_call x0 -> x1, Pallas kernels: none -> 52.2 us  [body(): pl.pallas_call(functools.partial(kernel, dims), out_shape=(jax.ShapeDtype...]
    all_gather x1 -> x0, blocking collectives: 33.2 us -> none  [body(): weights = lax.all_gather(shard_low, 'dp', axis=2, tiled=True)]
    reduce_sum x28 -> x0, other arithmetic: 27.2 us -> none  [the longest x6 8.02 us: layer_backward(): grad_bias_out = jnp.sum(grad_acts[0], 1)]
    another operation x25 -> x0, other arithmetic: 18.8 us -> none
  transfers between devices with their start and end apart: 27 -> 0, of which waited for: 25 -> 0; matrix products, arithmetic and copies ran while one was open for 13% -> 0% of each run, Pallas kernels for 0% -> 0%
where the time goes in v1:
time: 63.5 us; the launch traced here: 63.2 us
  Pallas kernels  52.2 us (82%)
  other arithmetic  5.74 us (9%)
  between operations  3.2 us (5%)
  local copies, waits for them, and re-layouts  2.03 us (3%)
    pallas_call x1, Pallas kernels, body(): pl.pallas_call(functools.partial(kernel, dims), out_shape=(jax.ShapeDtype...  52.2 us
    add x1, other arithmetic, body(): average_decay * average_small + (1.0 - average_decay) * new_small  1.94 us
    div x1, other arithmetic, body(): grad_blocks = gsum.reshape(master_blocks.shape) / count_valid  1.61 us

profile of v1, /device:TPU:0, one launch (start us, length us, event | category | flops | bytes accessed | tf_op | source)
XLA Modules:
  0.0 63.2 jit_solution(3002611897902735437)
XLA Ops:
  0.6 52.2 %shard_map.194 = (f32[4,64,128]{2,1,0:T(8,128)}, f32[16,128]{1,0:T(8,128)}, f32[8,128]{1,0:T(8,128)}) custom-call(f32[6,768]{1,0:T(8,128)} %coords_hbm.1, s32[768]{0:T(1024)} %model_hbm.1, s32[768]{0:T(1024)} %cells_hbm.1, s32[768]{0:T(1024)} %valid_hbm.1, f32[4,512,128]{2,1,0:T(8,128)} %grid_hbm.1, f32[2,2,64,128]{3,2,1,0:T(8,128)} %master_hbm.1, ...), custom_call_target="tpu_custom_call" | custom-call | tf_op jit(solution)/shard_map/pallas_call | solution.py:583
  52.9 0.0 copy-start.8
  52.9 0.8 %rsqrt_reduce_fusion = f32[5]{0:T(128)S(1)} fusion(f32[8,128]{1,0:T(8,128)} %get-tuple-element.16), kind=kLoop, calls=%fused_computation.8 | loop fusion | flops 5 | bytes 40 | tf_op jit(solution)/shard_map/sqrt | solution.py:654
  53.7 0.0 copy-done.8
  53.7 0.6 slice.31
  54.3 0.0 copy-start.5
  54.3 0.0 copy-start.6
  54.3 0.0 copy-start.9
  54.3 0.1 mul.46
  54.4 0.5 fusion.1
  56.2 0.0 copy-start.2
  56.3 0.0 copy-start.3
  56.3 1.6 %broadcast_divide_fusion = f32[4,64,128]{2,1,0:T(8,128)S(1)} fusion(f32[4,64,128]{2,1,0:T(8,128)} %get-tuple-element.15, f32[]{:T(128)} %bitcast.1), kind=kLoop, calls=%fused_computation.3 | loop fusion | flops 32768 | bytes 262148 | tf_op jit(solution)/shard_map/div | solution.py:647
  57.9 0.0 copy-start.1
  57.9 0.0 copy-done.5
  57.9 0.0 copy-done.6
  57.9 0.0 copy-done.9
  57.9 1.9 %add_multiply_fusion.1 = (f32[12,128]{1,0:T(8,128)}, f32[12,128]{1,0:T(8,128)}, f32[12,128]{1,0:T(8,128)}, f32[12,128]{1,0:T(8,128)S(1)}) fusion(f32[12,128]{1,0:T(8,128)S(1)} %copy-done.9, f32[12,128]{1,0:T(8,128)S(1)} %copy-done.5, f32[]{:T(128)} %bitcast.4, f32[12,128]{1,0:T(8,128)S(1)} %copy-done.6, f32[]{:T(128)} %bitcast.1, f32[16,128]{1,0:T(8,128)S(1)} %copy-done.8), kind=kLoop, calls=%fused_computation.4 | loop fusion | flops 13824 | bytes 49160 | tf_op jit(solution)/shard_map/add | solution.py:659
  59.9 0.0 copy-start.7
  59.9 0.6 slice.32
  60.4 0.0 copy-done.2
  60.4 0.0 copy-done.3
  60.5 0.0 copy-start.4
  60.5 0.7 %fusion = (bf16[2,2,64,128]{3,2,1,0:T(8,128)(2,1)}, f32[2,2,64,128]{3,2,1,0:T(8,128)S(1)}, f32[2,2,64,128]{3,2,1,0:T(8,128)}) fusion(f32[2,2,64,128]{3,2,1,0:T(8,128)S(1)} %copy-done.2, f32[2,2,64,128]{3,2,1,0:T(8,128)S(1)} %bitcast.7, f32[2,2]{1,0:T(2,128)S(1)} %mul.46, f32[2,2,64,128]{3,2,1,0:T(8,128)S(1)} %copy-done.3), kind=kLoop, calls=%fused_computation.10 | loop fusion | flops 229376 | bytes 720912 | tf_op jit(solution)/shard_map/convert_element_type | solution.py:671
  61.2 0.0 copy-done.1
  61.2 0.0 copy-done.7
  61.2 0.0 copy-start
  61.2 0.2 copy-done.4
  61.4 0.7 %add_multiply_fusion = f32[2,2,64,128]{3,2,1,0:T(8,128)} fusion(f32[2,2,64,128]{3,2,1,0:T(8,128)S(1)} %copy-done.4, f32[2,2,64,128]{3,2,1,0:T(8,128)S(1)} %get-tuple-element.18), kind=kLoop, calls=%fused_computation | loop fusion | flops 65536 | bytes 393216 | tf_op jit(solution)/shard_map/add | solution.py:658
  62.1 0.0 copy-done
  (1 shorter events, 0.0 us)
Async XLA Ops:
  52.9 0.8 %copy-start.8 = (f32[16,128]{1,0:T(8,128)S(1)}, f32[16,128]{1,0:T(8,128)}, u32[]{:S(2)}) copy-start(f32[16,128]{1,0:T(8,128)} %get-tuple-element.14) | copy-start | bytes 24580
  54.3 3.6 %copy-start.5 = (f32[12,128]{1,0:T(8,128)S(1)}, f32[12,128]{1,0:T(8,128)}, u32[]{:S(2)}) copy-start(f32[12,128]{1,0:T(8,128)} %small_hbm.1) | copy-start | bytes 18436
  54.3 3.6 %copy-start.6 = (f32[12,128]{1,0:T(8,128)S(1)}, f32[12,128]{1,0:T(8,128)}, u32[]{:S(2)}) copy-start(f32[12,128]{1,0:T(8,128)} %msmall_hbm.1) | copy-start | bytes 18436
  54.3 3.6 %copy-start.9 = (f32[12,128]{1,0:T(8,128)S(1)}, f32[12,128]{1,0:T(8,128)}, u32[]{:S(2)}) copy-start(f32[12,128]{1,0:T(8,128)} %param.21) | copy-start | bytes 18436
  56.2 4.2 %copy-start.2 = (f32[2,2,64,128]{3,2,1,0:T(8,128)S(1)}, f32[2,2,64,128]{3,2,1,0:T(8,128)}, u32[]{:S(2)}) copy-start(f32[2,2,64,128]{3,2,1,0:T(8,128)} %master_hbm.1) | copy-start | bytes 393220
  56.3 4.2 %copy-start.3 = (f32[2,2,64,128]{3,2,1,0:T(8,128)S(1)}, f32[2,2,64,128]{3,2,1,0:T(8,128)}, u32[]{:S(2)}) copy-start(f32[2,2,64,128]{3,2,1,0:T(8,128)} %moment_hbm.1) | copy-start | bytes 393220
  57.9 3.3 %copy-start.1 = (f32[4,64,128]{2,1,0:T(8,128)}, f32[4,64,128]{2,1,0:T(8,128)S(1)}, u32[]{:S(2)}) copy-start(f32[4,64,128]{2,1,0:T(8,128)S(1)} %broadcast_divide_fusion) | copy-start | bytes 393220
  59.9 1.3 %copy-start.7 = (f32[12,128]{1,0:T(8,128)}, f32[12,128]{1,0:T(8,128)S(1)}, u32[]{:S(2)}) copy-start(f32[12,128]{1,0:T(8,128)S(1)} %get-tuple-element.23) | copy-start | bytes 18436
  60.5 1.0 %copy-start.4 = (f32[2,2,64,128]{3,2,1,0:T(8,128)S(1)}, f32[2,2,64,128]{3,2,1,0:T(8,128)}, u32[]{:S(2)}) copy-start(f32[2,2,64,128]{3,2,1,0:T(8,128)} %param.20) | copy-start | bytes 393220
  61.2 0.9 %copy-start = (f32[2,2,64,128]{3,2,1,0:T(8,128)}, f32[2,2,64,128]{3,2,1,0:T(8,128)S(1)}, u32[]{:S(2)}) copy-start(f32[2,2,64,128]{3,2,1,0:T(8,128)S(1)} %get-tuple-element.18) | copy-start | bytes 393220

commit v2 on v1

--- a/solution.py
+++ b/solution.py
@@ -19,7 +19,16 @@
 spread_rate = 0.5
 norm_epsilon = 1e-12
 
-FAR_LAST = 3
+TURNED = 2
+
+
+def partner(i, k, size):
+    bit = 1
+    while bit < size:
+        if (k // bit) % 2:
+            i = i + bit - 2 * bit * ((i // bit) % 2)
+        bit *= 2
+    return i
 
 
 def nn(left, right):
@@ -49,9 +58,19 @@
     small_hbm,
     moment_hbm,
     msmall_hbm,
-    gsum,
-    sred,
-    tot,
+    average_hbm,
+    asmall_hbm,
+    loss_b,
+    grad_b,
+    grad_s,
+    bias_b,
+    moment_b,
+    moment_s,
+    master_b,
+    master_s,
+    average_b,
+    average_s,
+    low_b,
     coords,
     model,
     cells,
@@ -60,8 +79,11 @@
     master,
     moment,
     msmall,
+    average,
+    asmall,
     spbuf,
     columns,
+    sred,
     wbuf,
     streams,
     acts,
@@ -74,11 +96,13 @@
     gsend,
     gcore,
     gone,
-    gslot_g,
-    gtwo_g,
+    gslot_n,
+    gtwo,
     gslot_z,
-    gtwo_z,
-    gback_g,
+    gown,
+    tslot_z,
+    tback,
+    tslot_n,
     sgsend,
     sgcore,
     sgone,
@@ -89,10 +113,19 @@
     artwo,
     arslot_z,
     in_sem,
-    w_send,
-    w_recv,
-    g_send,
-    g_recv,
+    wz_send,
+    wz_recv,
+    wn_send,
+    wn_recv,
+    wt_send,
+    wc_send,
+    wc_recv,
+    gz_send,
+    gz_recv,
+    gn_send,
+    gn_recv,
+    gc_send,
+    gc_recv,
     s_send,
     s_recv,
 ):
@@ -108,8 +141,8 @@
     def device(a_, g_, c_):
         return (a_ * B + g_ % B, (g_ // B) * 2 + c_)
 
-    far = [(a + k) % A for k in range(1, A)]
-    near = [(g + k) % G for k in range(1, G)]
+    far = [partner(a, k, A) for k in range(1, A)]
+    near = [partner(g, k, G) for k in range(1, G)]
     z_devices = [device(o, g, c) for o in far]
     g_devices = [device(a, o, c) for o in near]
     core_device = device(a, g, 1 - c)
@@ -117,7 +150,6 @@
     q_devices = g_devices + [device(a, o, cc) for o, cc in group] + [core_device]
     q_slots = [o * 2 + c for o in near] + [o * 2 + cc for o, cc in group] + [g * 2 + 1 - c]
     NQ = 2 * G
-    FAR, NEAR, CORE = 0, A - 1, A + G - 2
 
     S1 = 1
     S2 = S1 + G - 1
@@ -156,6 +188,8 @@
             (grid_hbm, grid),
             (moment_hbm, moment),
             (msmall_hbm, msmall),
+            (average_hbm, average),
+            (asmall_hbm, asmall),
         ]
     ):
         copy = pltpu.make_async_copy(src, dst, in_sem.at[i])
@@ -173,45 +207,53 @@
     local[1].wait()
     pl.semaphore_wait(barrier, len(peers))
 
-    def w_far(m, src_of):
+    def piece(m, o, z):
+        return wbuf.at[m, c, o // B, z, o % B]
+
+    def line(m, o):
+        return wbuf.at[m, c, o // B, :, o % B]
+
+    def plane(m, z):
+        return wbuf.at[m, c, :, z]
+
+    def await_bytes(ref, rsem, d):
+        pltpu.make_async_remote_copy(
+            src_ref=ref, dst_ref=ref, send_sem=s_send.at[0], recv_sem=rsem, device_id=d, device_id_type=MESH
+        ).wait_recv()
+
+    def w_far(m, ref):
         return [
-            remote(src_of(m), src_of(m), w_send.at[m, FAR + k], w_recv.at[m, FAR + k], d)
-            for k, d in enumerate(z_devices)
+            remote(ref, ref, wz_send.at[m, k], wz_recv.at[m, k], d) for k, d in enumerate(z_devices)
         ]
 
-    def w_near(m, src_of):
+    def w_near(m, ref, j):
         return [
-            remote(src_of(m), src_of(m), w_send.at[m, NEAR + k], w_recv.at[m, NEAR + k], d)
-            for k, d in enumerate(g_devices)
+            remote(ref, ref, wn_send.at[m, j, k], wn_recv.at[m, k], d) for k, d in enumerate(g_devices)
         ]
 
-    def own(m):
-        return wbuf.at[m, c, y, a, b]
-
-    def line(m):
-        return wbuf.at[m, c, y, :, b]
-
-    def plane(m):
-        return wbuf.at[m, c, :, a]
-
-    def w_core(m):
-        return [remote(wbuf.at[m, c], wbuf.at[m, c], w_send.at[m, CORE], w_recv.at[m, CORE], core_device)]
-
-    def owner_t(o, cc):
-        return (o // B) * 2 + cc
-
-    first = {}
-    normal = [m for m in range(MATS) if m != FAR_LAST]
+    def w_far_turned(ref, j):
+        for k, d in enumerate(z_devices):
+            remote(ref, ref, wt_send.at[j, k], wz_recv.at[TURNED, k], d)
+
+    def w_core(m, ref, j):
+        remote(ref, ref, wc_send.at[m, j], wc_recv.at[m], core_device)
+
+    straight = [m for m in range(MATS) if m != TURNED]
     sp_copies = []
     for k in range(1, n_t):
         o = (t + k) % n_t
         sp_copies.append(
             remote(spbuf.at[t], spbuf.at[t], s_send.at[S4 + k - 1], s_recv.at[S4 + k - 1], (dp, o))
         )
-    for i, m in enumerate(normal):
-        first[m] = w_far(m, own)
+    first = {}
+    for i, m in enumerate(straight):
+        first[m] = w_far(m, piece(m, g, a))
         if i == 0:
-            first[FAR_LAST] = w_near(FAR_LAST, own)
+            first[TURNED] = w_near(TURNED, piece(TURNED, g, a), 0)
+    for i, m in enumerate(straight):
+        w_near(m, piece(m, g, a), 0)
+        if i == 0:
+            w_far_turned(piece(TURNED, g, a), 0)
 
     for copy in local[2:7]:
         copy.wait()
@@ -270,14 +312,22 @@
         streams[1 + k] = slope0 * first_rows[3 + k]
         acts[0, 1 + k] = streams[1 + k].astype(BF16)
 
-    second = {}
-    arrived(first[FAR_LAST])
-    second[FAR_LAST] = w_far(FAR_LAST, plane)
-    for m in normal:
-        arrived(first[m])
-        second[m] = w_near(m, line)
-
-    third = {}
+    def pass_on(m):
+        for k in range(A - 1):
+            first[m][k].wait_recv()
+            w_near(m, piece(m, g, far[k]), k + 1)
+        w_core(m, line(m, g), 0)
+
+    def pass_on_turned():
+        for k in range(G - 1):
+            first[TURNED][k].wait_recv()
+            w_far_turned(piece(TURNED, near[k], a), k + 1)
+        w_core(TURNED, plane(TURNED, a), 0)
+
+    pass_on(straight[0])
+    pass_on_turned()
+    for m in straight[1:]:
+        pass_on(m)
 
     def weight(m):
         return jnp.concatenate([wbuf[m, tt % 2, tt // 2].reshape(D, cw) for tt in range(n_t)], 1)
@@ -304,12 +354,21 @@
                 acts[l + 1, s] = new.astype(BF16)
 
     def fetch(m):
-        arrived(second[m])
-        third[m] = w_core(m)
+        if m == TURNED:
+            for k in range(A - 1):
+                await_bytes(plane(m, far[k]), wz_recv.at[m, k], z_devices[k])
+                w_core(m, plane(m, far[k]), k + 1)
+        else:
+            for k in range(G - 1):
+                await_bytes(line(m, near[k]), wn_recv.at[m, k], g_devices[k])
+                w_core(m, line(m, near[k]), k + 1)
+
+    def fetched(m):
+        await_bytes(wbuf.at[m, c], wc_recv.at[m], core_device)
 
     for m in range(MATS):
         fetch(m)
-        arrived(third[m])
+        fetched(m)
         if m % 2 == 0:
             block_in(m // 2)
         else:
@@ -339,77 +398,90 @@
         grad[s] = value
         gbranch[s] = value.astype(BF16)
 
-    flying = {}
+    pieces = [(far[k], k) for k in reversed(range(A - 1))] + [(a, None)]
 
     def start_core(m, value):
         low = value.astype(BF16)
         for tt in range(n_t):
-            gsend[m, tt % 2, tt // 2] = low[:, tt * cw : (tt + 1) * cw].reshape(A, B, R, cw)
+            block = low[:, tt * cw : (tt + 1) * cw].reshape(A, B, R, cw)
+            for i in range(B):
+                gsend[m, tt % 2, :, (tt // 2) * B + i] = block[:, i]
+        return [
+            remote(
+                gsend.at[m, 1 - c, z], gcore.at[m, z], gc_send.at[m, j], gc_recv.at[m, j], core_device
+            )
+            for j, (z, k) in enumerate(pieces)
+        ]
+
+    def core_sum(m, j):
+        z = pieces[j][0]
+        flying[m][j].wait_recv()
+        gone[m, z] = (gsend[m, c, z].astype(F32) + gcore[m, z].astype(F32)).astype(BF16)
+
+    def slot_sum(ref, count_of, value=None):
+        for i in range(count_of):
+            term = ref[i].astype(F32)
+            value = term if value is None else value + term
+        return value
+
+    def start_near(m):
+        for j, (z, _) in enumerate(pieces):
+            core_sum(m, j)
+            for k, o in enumerate(near):
+                remote(
+                    gone.at[m, z, o], gslot_n.at[m, j, k], gn_send.at[m, j, k], gn_recv.at[m, j], g_devices[k]
+                )
+
+    def start_far(m):
+        flying[m] = []
+        for j, (z, k) in enumerate(pieces):
+            if G > 1:
+                await_bytes(gslot_n.at[m, j], gn_recv.at[m, j], core_device)
+            total = slot_sum(gslot_n.at[m, j], G - 1, gone[m, z, g].astype(F32))
+            if k is None:
+                gown[m] = total
+            else:
+                gtwo[m, k] = total.astype(BF16)
+                flying[m].append(
+                    remote(gtwo.at[m, k], gslot_z.at[m, k], gz_send.at[m, k], gz_recv.at[m, k], z_devices[k])
+                )
+
+    def finish(m):
+        if m == TURNED:
+            return slot_sum(tslot_n, G - 1, gown[m])
+        return slot_sum(gslot_z.at[m], A - 1, gown[m])
+
+    def start_far_turned():
+        m = TURNED
+        copies = []
+        for j, (z, k) in enumerate(pieces):
+            core_sum(m, j)
+            if k is not None:
+                copies.append(
+                    remote(gone.at[m, z], tslot_z.at[k], gz_send.at[m, k], gz_recv.at[m, k], z_devices[k])
+                )
+        flying[m] = copies
+
+    def start_near_turned():
+        m = TURNED
+        arrived(flying[m])
+        tback[...] = slot_sum(tslot_z, A - 1, gone[m, a].astype(F32))
+        gown[m] = tback[g]
+        tlow = gone.at[m, a]
+        tlow[...] = tback[...].astype(BF16)
         flying[m] = [
-            remote(gsend.at[m, 1 - c], gcore.at[m], g_send.at[m, CORE], g_recv.at[m, CORE], core_device)
-        ]
-
-    def core_sum(m):
-        arrived(flying[m])
-        return (gsend[m, c].astype(F32) + gcore[m].astype(F32)).astype(BF16)
-
-    def slot_sum(ref, count_of):
-        value = ref[0].astype(F32)
-        for i in range(1, count_of):
-            value = value + ref[i].astype(F32)
-        return value
-
-    def start_near(m):
-        gone[m] = core_sum(m)
-        gslot_g[m, g] = gone[m, y, :, b]
-        flying[m] = [
-            remote(
-                gone.at[m, o // B, :, o % B],
-                gslot_g.at[m, g],
-                g_send.at[m, NEAR + k],
-                g_recv.at[m, NEAR + k],
-                g_devices[k],
-            )
+            remote(tlow.at[o], tslot_n.at[k], gn_send.at[m, 0, k], gn_recv.at[m, k], g_devices[k])
             for k, o in enumerate(near)
         ]
 
-    def start_far(m):
-        arrived(flying[m])
-        gtwo_g[m] = slot_sum(gslot_g.at[m], G).astype(BF16)
-        gslot_z[m, a] = gtwo_g[m, a]
-        flying[m] = [
-            remote(gtwo_g.at[m, o], gslot_z.at[m, a], g_send.at[m, FAR + k], g_recv.at[m, FAR + k], z_devices[k])
-            for k, o in enumerate(far)
-        ]
-
-    def start_far_first(m):
-        gone[m] = core_sum(m)
-        gtwo_z[a] = gone[m, :, a]
-        flying[m] = [
-            remote(
-                gone.at[m, :, o], gtwo_z.at[a], g_send.at[m, FAR + k], g_recv.at[m, FAR + k], z_devices[k]
-            )
-            for k, o in enumerate(far)
-        ]
-
-    def start_near_last(m):
-        arrived(flying[m])
-        total = slot_sum(gtwo_z, A).astype(BF16)
-        for i in range(G):
-            gback_g[0, i] = total[i // B, i % B]
-        gback_g[1, g] = gback_g[0, g]
-        flying[m] = [
-            remote(gback_g.at[0, o], gback_g.at[1, g], g_send.at[m, NEAR + k], g_recv.at[m, NEAR + k], g_devices[k])
-            for k, o in enumerate(near)
-        ]
-
+    flying = {}
     bias_in = [None] * LAYERS
     bias_out = [None] * LAYERS
 
     def back_out(l):
         bias_out[l] = jnp.sum(grad[0], axis=0, keepdims=True)
         gb = gbranch[...].reshape(M, D)
-        start_core(2 * l + 1, tn(gb, hidden[l].reshape(M, D)))
+        flying[2 * l + 1] = start_core(2 * l + 1, tn(gb, hidden[l].reshape(M, D)))
 
     def back_in(l):
         gb = gbranch[...].reshape(M, D)
@@ -423,7 +495,7 @@
         gpre[0] = gz.astype(BF16)
         for k in range(1, 4):
             gpre[k] = (gh[k] * slope).astype(BF16)
-        start_core(2 * l, tn(acts[l].reshape(M, D), gpre[...].reshape(M, D)))
+        flying[2 * l] = start_core(2 * l, tn(acts[l].reshape(M, D), gpre[...].reshape(M, D)))
 
     def back_through(l):
         back = nt(gpre[...].reshape(M, D), weight(2 * l)).reshape(4, Pn, D)
@@ -433,22 +505,16 @@
             if l > 0:
                 gbranch[s] = value.astype(BF16)
 
-    def forward_first(m):
-        if m == FAR_LAST:
-            start_far_first(m)
-        else:
-            start_near(m)
-
     back_out(1)
     back_in(1)
-    forward_first(3)
+    start_near(3)
     back_through(1)
     back_out(0)
-    forward_first(2)
+    start_far_turned()
     back_in(0)
-    forward_first(1)
+    start_near(1)
     back_through(0)
-    forward_first(0)
+    start_near(0)
 
     z0 = inner[...]
     e0 = jnp.exp(jnp.minimum(z0, 0.0))
@@ -488,9 +554,10 @@
         for k, o in enumerate(near)
     ]
 
-    start_near_last(FAR_LAST)
-    for m in reversed(normal):
-        start_far(m)
+    start_far(3)
+    start_near_turned()
+    start_far(1)
+    start_far(0)
     arrived(sg)
     sgtwo[...] = slot_sum(sgslot_g, G)
     sgslot_z[a] = sgtwo[...]
@@ -500,27 +567,32 @@
 
     for copy in local[7:]:
         copy.wait()
-    arrived(flying[FAR_LAST])
-    for i in range(MATS):
-        m = MATS - 1 - i
-        if m == FAR_LAST:
-            gsum[m] = slot_sum(gback_g.at[1], G)
-        else:
-            arrived(flying[m])
-            gsum[m] = slot_sum(gslot_z.at[m], A)
+    for m in (3, 1, TURNED, 0):
+        arrived(flying[m])
+        grad_b[m // 2, m % 2] = finish(m)
     arrived(sg)
     sred[...] = slot_sum(sgslot_z, A)
     counted = sred[SMALL + 1 : SMALL + 2, 0:1]
     tile_rows = lax.broadcasted_iota(jnp.int32, (8, 128), 0)
     parts = jnp.zeros((8, 128), F32)
+
+    def step(gradient, momentum):
+        new = momentum_coef * momentum + gradient
+        return new, gradient + momentum_coef * new
+
     for m in range(MATS):
-        gr = gsum[m] / counted
-        direction = gr + momentum_coef * (momentum_coef * moment[m // 2, m % 2] + gr)
+        at = (m // 2, m % 2)
+        gr = grad_b[at] / counted
+        new, direction = step(gr, moment[at])
+        grad_b[at] = gr
+        moment_b[at] = new
         parts = jnp.where(tile_rows == m, jnp.sum(direction * direction, keepdims=True), parts)
     gr = sred[0:SMALL, :] / counted
-    direction = gr + momentum_coef * (momentum_coef * msmall[...] + gr)
+    new, dir_small = step(gr, msmall[...])
+    grad_s[...] = gr
+    moment_s[...] = new
     parts = jnp.where(
-        tile_rows == MATS, jnp.sum(direction * direction, keepdims=True) / (A * B), parts
+        tile_rows == MATS, jnp.sum(dir_small * dir_small, keepdims=True) / (A * B), parts
     )
     me = g * 2 + c
     arslot_g[me] = parts
@@ -528,17 +600,47 @@
         remote(arslot_g.at[me], arslot_g.at[me], s_send.at[S3 + k], s_recv.at[S3 + k], d)
         for k, d in enumerate(q_devices)
     ]
+    loss_b[...] = sred[SMALL : SMALL + 1, 0:1] / counted
+    bias_b[...] = grad_s[7 : 7 + 2 * LAYERS, :]
     arrived(ar)
     artwo[...] = slot_sum(arslot_g, NQ)
     arslot_z[a] = artwo[...]
     ar = [
-        remote(artwo, arslot_z.at[a], s_send.at[S5 + k], s_recv.at[S5 + k], d) for k, d in enumerate(z_devices)
+        remote(artwo, arslot_z.at[a], s_send.at[S5 + k], s_recv.at[S5 + k], d)
+        for k, d in enumerate(z_devices)
     ]
     arrived(ar)
-    tot[...] = slot_sum(arslot_z, A)
+    dir_sq = slot_sum(arslot_z, A)
+
+    def rate_of(m):
+        size = sred[SMALL + 2 : SMALL + 3, m : m + 1]
+        return spread_rate * jnp.sqrt(size) / jnp.sqrt(dir_sq[m : m + 1, 0:1] + norm_epsilon)
+
+    for m in range(MATS):
+        at = (m // 2, m % 2)
+        direction = grad_b[at] + momentum_coef * moment_b[at]
+        new = master[at] - rate_of(m) * direction
+        master_b[at] = new
+        average_b[at] = average_decay * average[at] + (1.0 - average_decay) * new
+        low_b[at] = new.astype(BF16)
+    new = own_small - rate_of(MATS) * dir_small
+    master_s[...] = new
+    average_s[...] = average_decay * asmall[...] + (1.0 - average_decay) * new
 
     for copy in sends:
         copy.wait_send()
+
+
+def write_out(*refs):
+    sems = refs[-1]
+    count = (len(refs) - 1) // 2
+    copies = [
+        pltpu.make_async_copy(refs[i], refs[count + i], sems.at[i]) for i in range(count)
+    ]
+    for copy in copies:
+        copy.start()
+    for copy in copies:
+        copy.wait()
 
 
 def body(
@@ -565,7 +667,7 @@
     PB = coords.shape[1]
     Pn = PB // n_t
     dims = (A, B, C, R, cw, Pn, D)
-    anywhere = pl.BlockSpec(memory_space=pl.ANY)
+    anywhere = pl.BlockSpec(memory_space=pltpu.HBM)
     vmem = pl.BlockSpec(memory_space=pltpu.VMEM)
     S = SMALL + 4
     args = (
@@ -578,17 +680,31 @@
         small_params,
         moment_blocks,
         moment_small,
+        average_blocks,
+        average_small,
     )
     V = pltpu.VMEM
-    gsum, sred, tot = pl.pallas_call(
+    DMA = pltpu.SemaphoreType.DMA
+    block = (master_blocks.shape, F32)
+    short = (small_params.shape, F32)
+    shapes = [
+        ((1, 1), F32),
+        block,
+        short,
+        ((2 * LAYERS, cw), F32),
+        block,
+        short,
+        block,
+        short,
+        block,
+        short,
+        (master_blocks.shape, BF16),
+    ]
+    results = pl.pallas_call(
         functools.partial(kernel, dims),
-        out_shape=(
-            jax.ShapeDtypeStruct((MATS, R, cw), F32),
-            jax.ShapeDtypeStruct((S, cw), F32),
-            jax.ShapeDtypeStruct((8, 128), F32),
-        ),
+        out_shape=tuple(V(*shape) for shape in shapes),
         in_specs=[anywhere] * len(args),
-        out_specs=(vmem,) * 3,
+        out_specs=(vmem,) * len(shapes),
         scratch_shapes=[
             V(coords.shape, F32),
             V((PB,), jnp.int32),
@@ -598,8 +714,11 @@
             V(master_blocks.shape, F32),
             V(master_blocks.shape, F32),
             V(small_params.shape, F32),
+            V(master_blocks.shape, F32),
+            V(small_params.shape, F32),
             V((n_t, SMALL, cw), F32),
             V((PB, 128), F32),
+            V((S, cw), F32),
             V((MATS, 2, C, A, B, R, cw), BF16),
             V((4, Pn, D), F32),
             V((LAYERS, 4, Pn, D), BF16),
@@ -609,14 +728,16 @@
             V((4, Pn, D), BF16),
             V((4, Pn, D), BF16),
             V((Pn, D), F32),
-            V((MATS, 2, C, A, B, R, cw), BF16),
-            V((MATS, C, A, B, R, cw), BF16),
-            V((MATS, C, A, B, R, cw), BF16),
-            V((MATS, G, A, R, cw), BF16),
-            V((MATS, A, R, cw), BF16),
-            V((MATS, A, R, cw), BF16),
-            V((A, C, B, R, cw), BF16),
-            V((2, G, R, cw), BF16),
+            V((MATS, 2, A, G, R, cw), BF16),
+            V((MATS, A, G, R, cw), BF16),
+            V((MATS, A, G, R, cw), BF16),
+            V((MATS, A, G - 1, R, cw), BF16),
+            V((MATS, A - 1, R, cw), BF16),
+            V((MATS, A - 1, R, cw), BF16),
+            V((MATS, R, cw), F32),
+            V((A - 1, G, R, cw), BF16),
+            V((G, R, cw), F32),
+            V((G - 1, R, cw), BF16),
             V((2, C, S, cw), F32),
             V((C, S, cw), F32),
             V((C, S, cw), F32),
@@ -627,10 +748,19 @@
             V((8, 128), F32),
             V((A, 8, 128), F32),
             pltpu.SemaphoreType.DMA((len(args),)),
-            pltpu.SemaphoreType.DMA((MATS, A + G - 1)),
-            pltpu.SemaphoreType.DMA((MATS, A + G - 1)),
-            pltpu.SemaphoreType.DMA((MATS, A + G - 1)),
-            pltpu.SemaphoreType.DMA((MATS, A + G - 1)),
+            DMA((MATS, A - 1)),
+            DMA((MATS, A - 1)),
+            DMA((MATS, A, G - 1)),
+            DMA((MATS, G - 1)),
+            DMA((G, A - 1)),
+            DMA((MATS, max(A, G))),
+            DMA((MATS,)),
+            DMA((MATS, A - 1)),
+            DMA((MATS, A - 1)),
+            DMA((MATS, A, G - 1)),
+            DMA((MATS, max(A, G - 1))),
+            DMA((MATS, A)),
+            DMA((MATS, A)),
             pltpu.SemaphoreType.DMA((G + 2 * A + 2 * G + n_t,)),
             pltpu.SemaphoreType.DMA((G + 2 * A + 2 * G + n_t,)),
         ],
@@ -639,37 +769,15 @@
         ),
     )(*args)
 
-    total_err = sred[SMALL, 0]
-    count_valid = sred[SMALL + 1, 0]
-    weight_sq = sred[SMALL + 2, 0 : MATS + 1]
-    dir_sq = tot[0 : MATS + 1, 0]
-    loss = total_err / count_valid
-    grad_blocks = gsum.reshape(master_blocks.shape) / count_valid
-    grad_small = sred[0:SMALL] / count_valid
-    bias_grads = grad_small[7 : 7 + 2 * LAYERS]
-    new_moment_blocks = momentum_coef * moment_blocks + grad_blocks
-    new_moment_small = momentum_coef * moment_small + grad_small
-    dir_blocks = grad_blocks + momentum_coef * new_moment_blocks
-    dir_small = grad_small + momentum_coef * new_moment_small
-    step_rate = spread_rate * jnp.sqrt(weight_sq) / jnp.sqrt(dir_sq + norm_epsilon)
-    rate_blocks = step_rate[:-1].reshape(LAYERS, 2)
-    new_master_blocks = master_blocks - rate_blocks[:, :, None, None] * dir_blocks
-    new_small = small_params - step_rate[-1] * dir_small
-    new_average_blocks = average_decay * average_blocks + (1.0 - average_decay) * new_master_blocks
-    new_average_small = average_decay * average_small + (1.0 - average_decay) * new_small
-    return (
-        loss,
-        grad_blocks,
-        grad_small,
-        bias_grads,
-        new_moment_blocks,
-        new_moment_small,
-        new_master_blocks,
-        new_small,
-        new_average_blocks,
-        new_average_small,
-        new_master_blocks.astype(BF16),
-    )
+    results = pl.pallas_call(
+        write_out,
+        out_shape=tuple(jax.ShapeDtypeStruct(*shape) for shape in shapes),
+        in_specs=[vmem] * len(shapes),
+        out_specs=(anywhere,) * len(shapes),
+        scratch_shapes=[pltpu.SemaphoreType.DMA((len(shapes),))],
+        compiler_params=pltpu.CompilerParams(vmem_limit_bytes=4 << 20),
+    )(*results)
+    return (results[0].reshape(()),) + tuple(results[1:])
 
 
 def solution(mesh):

time: 63.5 us -> 52.3 us (0.82)
  other arithmetic: 5.74 us -> 0 us
  between operations: 3.2 us -> 0.66 us
  local copies, waits for them, and re-layouts: 2.03 us -> 0 us
  Pallas kernels: 52.2 us -> 51.5 us
    add x2 -> x0, other arithmetic: 2.61 us -> none  [the longest x1 1.94 us: body(): average_decay * average_small + (1.0 - average_decay) * new_small]
    slice x3 -> x0, local copies, waits for them, and re-layouts: 1.68 us -> none  [the longest x1 0.59 us: body(): new_small = small_params - step_rate[-1] * dir_small]
    div x2 -> x0, other arithmetic: 1.62 us -> none  [the longest x1 1.61 us: body(): grad_blocks = gsum.reshape(master_blocks.shape) / count_valid]
    sqrt x1 -> x0, other arithmetic: 0.8 us -> none  [body(): jnp.sqrt(dir_sq + norm_epsilon)]
    pallas_call x1 -> x2, Pallas kernels: 52.2 us -> 51.5 us  [the longest x1 49.9 us: body(): pl.pallas_call(functools.partial(kernel, dims), out_shape=tuple((V(*shape...]
    convert_element_type x1 -> x0, other arithmetic: 0.72 us -> none  [body(): new_master_blocks.astype(BF16)]
where the time goes in v2:
time: 52.3 us; the launch traced here: 52.1 us
  Pallas kernels  51.5 us (98%)
  between operations  0.66 us (1%)
    pallas_call x1, Pallas kernels, body(): pl.pallas_call(functools.partial(kernel, dims), out_shape=tuple((V(*shape...  49.9 us
    pallas_call x1, Pallas kernels, body(): pl.pallas_call(write_out, out_shape=tuple((jax.ShapeDtypeStruct(*shape) f...  1.56 us

profile of v2, /device:TPU:0, one launch (start us, length us, event | category | flops | bytes accessed | tf_op | source)
XLA Modules:
  0.0 52.1 jit_solution(9317434375552030160)
XLA Ops:
  0.6 49.9 %shard_map.194 = (f32[1,1]{1,0:T(1,128)}, f32[2,2,64,128]{3,2,1,0:T(8,128)S(1)}, f32[12,128]{1,0:T(8,128)S(1)}, f32[4,128]{1,0:T(4,128)S(1)}, f32[2,2,64,128]{3,...) custom-call(f32[6,768]{1,0:T(8,128)} %coords_hbm.1, ...), custom_call_target="tpu_custom_call" | custom-call | tf_op jit(solution)/shard_map/pallas_call | solution.py:703
  50.6 1.6 %shard_map.195 = (f32[1,1]{1,0:T(1,128)}, f32[2,2,64,128]{3,2,1,0:T(8,128)}, f32[12,128]{1,0:T(8,128)}, f32[4,128]{1,0:T(4,128)}, f32[2,2,64,128]{3,2,1,0:T(8,12...) custom-call(f32[1,1]{1,0:T(1,128)} %get-tuple-element.33.refs_0_, ...), custom_call_target="tpu_custom_call" | custom-call | tf_op jit(solution)/shard_map/pallas_call | solution.py:772

commit v3 on v2

--- a/solution.py
+++ b/solution.py
@@ -109,22 +109,15 @@
     sgslot_g,
     sgtwo,
     sgslot_z,
-    arslot_g,
-    artwo,
-    arslot_z,
+    arslot,
     in_sem,
-    wz_send,
+    w_send,
     wz_recv,
-    wn_send,
     wn_recv,
-    wt_send,
-    wc_send,
     wc_recv,
-    gz_send,
+    g_send,
     gz_recv,
-    gn_send,
     gn_recv,
-    gc_send,
     gc_recv,
     s_send,
     s_recv,
@@ -146,18 +139,14 @@
     z_devices = [device(o, g, c) for o in far]
     g_devices = [device(a, o, c) for o in near]
     core_device = device(a, g, 1 - c)
-    group = [(o, 1 - c) for o in near]
-    q_devices = g_devices + [device(a, o, cc) for o, cc in group] + [core_device]
-    q_slots = [o * 2 + c for o in near] + [o * 2 + cc for o, cc in group] + [g * 2 + 1 - c]
-    NQ = 2 * G
-
-    S1 = 1
-    S2 = S1 + G - 1
-    S3 = S2 + A - 1
-    S4 = S3 + NQ - 1
-    S5 = S4 + n_t - 1
-
-    sends = []
+    q_devices = [device(a, partner(g, kg, G), partner(c, kc, 2)) for kg in range(G) for kc in range(2)][1:]
+    steps = [(ka, kg, kc) for ka in range(A) for kg in range(G) for kc in range(2)][1:]
+    steps.sort(key=lambda step: -(step[0] + bin(step[1]).count("1") + step[2] / 2))
+    everyone = [device(partner(a, ka, A), partner(g, kg, G), partner(c, kc, 2)) for ka, kg, kc in steps]
+    others = [d for d, step in zip(everyone, steps) if step[0] and (step[1] or step[2])]
+
+    WZ, WN, WT, WP, WC = range(5)
+    S_CORE, S_NEAR, S_FAR, S_ALL, S_PAR = range(5)
 
     def remote(src, dst, ssem, rsem, device_id):
         copy = pltpu.make_async_remote_copy(
@@ -169,7 +158,6 @@
             device_id_type=MESH,
         )
         copy.start()
-        sends.append(copy)
         return copy
 
     def arrived(copies):
@@ -216,35 +204,48 @@
     def plane(m, z):
         return wbuf.at[m, c, :, z]
 
-    def await_bytes(ref, rsem, d):
+    def await_bytes(ref, rsem):
         pltpu.make_async_remote_copy(
-            src_ref=ref, dst_ref=ref, send_sem=s_send.at[0], recv_sem=rsem, device_id=d, device_id_type=MESH
+            src_ref=ref,
+            dst_ref=ref,
+            send_sem=s_send.at[0],
+            recv_sem=rsem,
+            device_id=core_device,
+            device_id_type=MESH,
         ).wait_recv()
+
+    def await_sent(ref, ssem):
+        pltpu.make_async_remote_copy(
+            src_ref=ref,
+            dst_ref=ref,
+            send_sem=ssem,
+            recv_sem=s_recv.at[0],
+            device_id=core_device,
+            device_id_type=MESH,
+        ).wait_send()
 
     def w_far(m, ref):
         return [
-            remote(ref, ref, wz_send.at[m, k], wz_recv.at[m, k], d) for k, d in enumerate(z_devices)
+            remote(ref, ref, w_send.at[WZ], wz_recv.at[m, k], d) for k, d in enumerate(z_devices)
         ]
 
     def w_near(m, ref, j):
         return [
-            remote(ref, ref, wn_send.at[m, j, k], wn_recv.at[m, k], d) for k, d in enumerate(g_devices)
+            remote(ref, ref, w_send.at[WT if m == TURNED else WN], wn_recv.at[m, k], d)
+            for k, d in enumerate(g_devices)
         ]
 
     def w_far_turned(ref, j):
         for k, d in enumerate(z_devices):
-            remote(ref, ref, wt_send.at[j, k], wz_recv.at[TURNED, k], d)
+            remote(ref, ref, w_send.at[WP], wz_recv.at[TURNED, k], d)
 
     def w_core(m, ref, j):
-        remote(ref, ref, wc_send.at[m, j], wc_recv.at[m], core_device)
+        remote(ref, ref, w_send.at[WC], wc_recv.at[m], core_device)
 
     straight = [m for m in range(MATS) if m != TURNED]
-    sp_copies = []
     for k in range(1, n_t):
         o = (t + k) % n_t
-        sp_copies.append(
-            remote(spbuf.at[t], spbuf.at[t], s_send.at[S4 + k - 1], s_recv.at[S4 + k - 1], (dp, o))
-        )
+        remote(spbuf.at[t], spbuf.at[t], s_send.at[S_PAR], s_recv.at[S_PAR], (dp, o))
     first = {}
     for i, m in enumerate(straight):
         first[m] = w_far(m, piece(m, g, a))
@@ -294,7 +295,7 @@
     distance = jnp.sqrt(seps[0] * seps[0] + seps[1] * seps[1] + seps[2] * seps[2])
     units = [s / distance for s in seps]
 
-    arrived(sp_copies)
+    await_bytes(spbuf.at[pl.ds(0, n_t - 1)], s_recv.at[S_PAR])
 
     def small_row(i):
         return jnp.concatenate([spbuf[tt, i : i + 1, :] for tt in range(n_t)], 1)
@@ -356,19 +357,22 @@
     def fetch(m):
         if m == TURNED:
             for k in range(A - 1):
-                await_bytes(plane(m, far[k]), wz_recv.at[m, k], z_devices[k])
+                await_bytes(plane(m, far[k]), wz_recv.at[m, k])
                 w_core(m, plane(m, far[k]), k + 1)
         else:
             for k in range(G - 1):
-                await_bytes(line(m, near[k]), wn_recv.at[m, k], g_devices[k])
+                await_bytes(line(m, near[k]), wn_recv.at[m, k])
                 w_core(m, line(m, near[k]), k + 1)
 
     def fetched(m):
-        await_bytes(wbuf.at[m, c], wc_recv.at[m], core_device)
+        await_bytes(wbuf.at[m, c], wc_recv.at[m])
 
     for m in range(MATS):
         fetch(m)
         fetched(m)
+        if m == 0:
+            for d in others:
+                pl.semaphore_signal(barrier, inc=1, device_id=d, device_id_type=MESH)
         if m % 2 == 0:
             block_in(m // 2)
         else:
@@ -408,7 +412,7 @@
                 gsend[m, tt % 2, :, (tt // 2) * B + i] = block[:, i]
         return [
             remote(
-                gsend.at[m, 1 - c, z], gcore.at[m, z], gc_send.at[m, j], gc_recv.at[m, j], core_device
+                gsend.at[m, 1 - c, z], gcore.at[m, z], g_send.at[WC], gc_recv.at[m, j], core_device
             )
             for j, (z, k) in enumerate(pieces)
         ]
@@ -429,50 +433,43 @@
             core_sum(m, j)
             for k, o in enumerate(near):
                 remote(
-                    gone.at[m, z, o], gslot_n.at[m, j, k], gn_send.at[m, j, k], gn_recv.at[m, j], g_devices[k]
+                    gone.at[m, z, o], gslot_n.at[m, j, k], g_send.at[WN], gn_recv.at[m, j], g_devices[k]
                 )
 
     def start_far(m):
-        flying[m] = []
         for j, (z, k) in enumerate(pieces):
             if G > 1:
-                await_bytes(gslot_n.at[m, j], gn_recv.at[m, j], core_device)
+                await_bytes(gslot_n.at[m, j], gn_recv.at[m, j])
             total = slot_sum(gslot_n.at[m, j], G - 1, gone[m, z, g].astype(F32))
             if k is None:
                 gown[m] = total
             else:
                 gtwo[m, k] = total.astype(BF16)
-                flying[m].append(
-                    remote(gtwo.at[m, k], gslot_z.at[m, k], gz_send.at[m, k], gz_recv.at[m, k], z_devices[k])
-                )
+                remote(gtwo.at[m, k], gslot_z.at[m, k], g_send.at[WZ], gz_recv.at[m], z_devices[k])
 
     def finish(m):
         if m == TURNED:
+            await_bytes(tslot_n, gn_recv.at[m, 0])
             return slot_sum(tslot_n, G - 1, gown[m])
+        await_bytes(gslot_z.at[m], gz_recv.at[m])
         return slot_sum(gslot_z.at[m], A - 1, gown[m])
 
     def start_far_turned():
         m = TURNED
-        copies = []
         for j, (z, k) in enumerate(pieces):
             core_sum(m, j)
             if k is not None:
-                copies.append(
-                    remote(gone.at[m, z], tslot_z.at[k], gz_send.at[m, k], gz_recv.at[m, k], z_devices[k])
-                )
-        flying[m] = copies
+                remote(gone.at[m, z], tslot_z.at[k], g_send.at[WP], gz_recv.at[m], z_devices[k])
 
     def start_near_turned():
         m = TURNED
-        arrived(flying[m])
+        await_bytes(tslot_z, gz_recv.at[m])
         tback[...] = slot_sum(tslot_z, A - 1, gone[m, a].astype(F32))
         gown[m] = tback[g]
         tlow = gone.at[m, a]
         tlow[...] = tback[...].astype(BF16)
-        flying[m] = [
-            remote(tlow.at[o], tslot_n.at[k], gn_send.at[m, 0, k], gn_recv.at[m, k], g_devices[k])
-            for k, o in enumerate(near)
-        ]
+        for k, o in enumerate(near):
+            remote(tlow.at[o], tslot_n.at[k], g_send.at[WT], gn_recv.at[m, 0], g_devices[k])
 
     flying = {}
     bias_in = [None] * LAYERS
@@ -495,6 +492,8 @@
         gpre[0] = gz.astype(BF16)
         for k in range(1, 4):
             gpre[k] = (gh[k] * slope).astype(BF16)
+
+    def back_weight(l):
         flying[2 * l] = start_core(2 * l, tn(acts[l].reshape(M, D), gpre[...].reshape(M, D)))
 
     def back_through(l):
@@ -508,11 +507,13 @@
     back_out(1)
     back_in(1)
     start_near(3)
+    back_weight(1)
     back_through(1)
+    start_far_turned()
     back_out(0)
-    start_far_turned()
     back_in(0)
     start_near(1)
+    back_weight(0)
     back_through(0)
     start_near(0)
 
@@ -545,32 +546,28 @@
     ]
     for tt in range(n_t):
         sgsend[tt % 2, tt // 2] = jnp.concatenate([r[:, tt * cw : (tt + 1) * cw] for r in rows] + tail, 0)
-    sg = [remote(sgsend.at[1 - c], sgcore, s_send.at[0], s_recv.at[0], core_device)]
-    arrived(sg)
+    remote(sgsend.at[1 - c], sgcore, s_send.at[S_CORE], s_recv.at[S_CORE], core_device)
+    start_far(3)
+    await_bytes(sgcore, s_recv.at[S_CORE])
     sgone[...] = sgsend[c] + sgcore[...]
     sgslot_g[g] = sgone[y]
-    sg = [
-        remote(sgone.at[o // B], sgslot_g.at[g], s_send.at[S1 + k], s_recv.at[S1 + k], g_devices[k])
-        for k, o in enumerate(near)
-    ]
-
-    start_far(3)
+    for k, o in enumerate(near):
+        remote(sgone.at[o // B], sgslot_g.at[g], s_send.at[S_NEAR], s_recv.at[S_NEAR], g_devices[k])
+
+    start_far(1)
     start_near_turned()
-    start_far(1)
     start_far(0)
-    arrived(sg)
+    await_bytes(sgslot_g.at[pl.ds(0, G - 1)], s_recv.at[S_NEAR])
     sgtwo[...] = slot_sum(sgslot_g, G)
     sgslot_z[a] = sgtwo[...]
-    sg = [
-        remote(sgtwo, sgslot_z.at[a], s_send.at[S2 + k], s_recv.at[S2 + k], z_devices[k]) for k in range(A - 1)
-    ]
+    for d in z_devices:
+        remote(sgtwo, sgslot_z.at[a], s_send.at[S_FAR], s_recv.at[S_FAR], d)
 
     for copy in local[7:]:
         copy.wait()
     for m in (3, 1, TURNED, 0):
-        arrived(flying[m])
         grad_b[m // 2, m % 2] = finish(m)
-    arrived(sg)
+    await_bytes(sgslot_z.at[pl.ds(0, A - 1)], s_recv.at[S_FAR])
     sred[...] = slot_sum(sgslot_z, A)
     counted = sred[SMALL + 1 : SMALL + 2, 0:1]
     tile_rows = lax.broadcasted_iota(jnp.int32, (8, 128), 0)
@@ -594,23 +591,15 @@
     parts = jnp.where(
         tile_rows == MATS, jnp.sum(dir_small * dir_small, keepdims=True) / (A * B), parts
     )
-    me = g * 2 + c
-    arslot_g[me] = parts
-    ar = [
-        remote(arslot_g.at[me], arslot_g.at[me], s_send.at[S3 + k], s_recv.at[S3 + k], d)
-        for k, d in enumerate(q_devices)
-    ]
+    me = (a * G + g) * 2 + c
+    arslot[me] = parts
+    pl.semaphore_wait(barrier, len(others))
+    for d in everyone:
+        remote(arslot.at[me], arslot.at[me], s_send.at[S_ALL], s_recv.at[S_ALL], d)
     loss_b[...] = sred[SMALL : SMALL + 1, 0:1] / counted
     bias_b[...] = grad_s[7 : 7 + 2 * LAYERS, :]
-    arrived(ar)
-    artwo[...] = slot_sum(arslot_g, NQ)
-    arslot_z[a] = artwo[...]
-    ar = [
-        remote(artwo, arslot_z.at[a], s_send.at[S5 + k], s_recv.at[S5 + k], d)
-        for k, d in enumerate(z_devices)
-    ]
-    arrived(ar)
-    dir_sq = slot_sum(arslot_z, A)
+    await_bytes(arslot.at[pl.ds(0, len(everyone))], s_recv.at[S_ALL])
+    dir_sq = jnp.sum(arslot[...], axis=0)
 
     def rate_of(m):
         size = sred[SMALL + 2 : SMALL + 3, m : m + 1]
@@ -627,8 +616,18 @@
     master_s[...] = new
     average_s[...] = average_decay * asmall[...] + (1.0 - average_decay) * new
 
-    for copy in sends:
-        copy.wait_send()
+    straights, nears, fars = pl.ds(0, MATS - 1), pl.ds(0, G - 1), pl.ds(0, A - 1)
+    for sems in (w_send, g_send):
+        await_sent(gone.at[straights, fars, 0], sems.at[WZ])
+        await_sent(gone.at[straights, :, nears], sems.at[WN])
+        await_sent(gone.at[0, 0, nears], sems.at[WT])
+        await_sent(gone.at[0, fars], sems.at[WP])
+        await_sent(gone, sems.at[WC])
+    await_sent(sgcore, s_send.at[S_CORE])
+    await_sent(sgslot_g.at[nears], s_send.at[S_NEAR])
+    await_sent(sgslot_z.at[fars], s_send.at[S_FAR])
+    await_sent(arslot.at[pl.ds(0, len(everyone))], s_send.at[S_ALL])
+    await_sent(spbuf.at[pl.ds(0, n_t - 1)], s_send.at[S_PAR])
 
 
 def write_out(*refs):
@@ -744,25 +743,18 @@
             V((G, S, cw), F32),
             V((S, cw), F32),
             V((A, S, cw), F32),
-            V((2 * G, 8, 128), F32),
-            V((8, 128), F32),
-            V((A, 8, 128), F32),
+            V((2 * A * G, 8, 128), F32),
             pltpu.SemaphoreType.DMA((len(args),)),
+            DMA((5,)),
             DMA((MATS, A - 1)),
-            DMA((MATS, A - 1)),
-            DMA((MATS, A, G - 1)),
             DMA((MATS, G - 1)),
-            DMA((G, A - 1)),
-            DMA((MATS, max(A, G))),
             DMA((MATS,)),
-            DMA((MATS, A - 1)),
-            DMA((MATS, A - 1)),
-            DMA((MATS, A, G - 1)),
-            DMA((MATS, max(A, G - 1))),
+            DMA((5,)),
+            DMA((MATS,)),
             DMA((MATS, A)),
             DMA((MATS, A)),
-            pltpu.SemaphoreType.DMA((G + 2 * A + 2 * G + n_t,)),
-            pltpu.SemaphoreType.DMA((G + 2 * A + 2 * G + n_t,)),
+            DMA((5,)),
+            DMA((5,)),
         ],
         compiler_params=pltpu.CompilerParams(
             collective_id=0, has_side_effects=True, vmem_limit_bytes=60 << 20

time: 52.3 us -> 48.7 us (0.931)
  Pallas kernels: 51.5 us -> 47.8 us
    pallas_call x1, Pallas kernels: 49.9 us -> 46.3 us  [body(): pl.pallas_call(functools.partial(kernel, dims), out_shape=tuple((V(*shape...]
where the time goes in v3:
time: 48.7 us; the launch traced here: 48.5 us
  Pallas kernels  47.8 us (98%)
  between operations  0.66 us (1%)
    pallas_call x1, Pallas kernels, body(): pl.pallas_call(functools.partial(kernel, dims), out_shape=tuple((V(*shape...  46.3 us
    pallas_call x1, Pallas kernels, body(): pl.pallas_call(write_out, out_shape=tuple((jax.ShapeDtypeStruct(*shape) f...  1.56 us

profile of v3, /device:TPU:0, one launch (start us, length us, event | category | flops | bytes accessed | tf_op | source)
XLA Modules:
  0.0 48.5 jit_solution(5297097406142882727)
XLA Ops:
  0.6 46.3 %shard_map.194 = (f32[1,1]{1,0:T(1,128)}, f32[2,2,64,128]{3,2,1,0:T(8,128)S(1)}, f32[12,128]{1,0:T(8,128)S(1)}, f32[4,128]{1,0:T(4,128)S(1)}, f32[2,2,64,128]{3,...) custom-call(f32[6,768]{1,0:T(8,128)} %coords_hbm.1, ...), custom_call_target="tpu_custom_call" | custom-call | tf_op jit(solution)/shard_map/pallas_call | solution.py:702
  46.9 1.6 %shard_map.195 = (f32[1,1]{1,0:T(1,128)}, f32[2,2,64,128]{3,2,1,0:T(8,128)}, f32[12,128]{1,0:T(8,128)}, f32[4,128]{1,0:T(4,128)}, f32[2,2,64,128]{3,2,1,0:T(8,12...) custom-call(f32[1,1]{1,0:T(1,128)} %get-tuple-element.33.refs_0_, ...), custom_call_target="tpu_custom_call" | custom-call | tf_op jit(solution)/shard_map/pallas_call | solution.py:764

commit v4 on v3

--- a/solution.py
+++ b/solution.py
@@ -19,7 +19,9 @@
 spread_rate = 0.5
 norm_epsilon = 1e-12
 
-TURNED = 2
+MOVED = MATS - 1
+W_TURNED = 2
+G_TURNED = None
 
 
 def partner(i, k, size):
@@ -104,12 +106,18 @@
     tback,
     tslot_n,
     sgsend,
-    sgcore,
-    sgone,
+    psend,
+    pslot,
+    pdone,
     sgslot_g,
     sgtwo,
     sgslot_z,
     arslot,
+    qslot_z,
+    qslot_g,
+    vsend,
+    vslot_g,
+    vslot_z,
     in_sem,
     w_send,
     wz_recv,
@@ -139,14 +147,15 @@
     z_devices = [device(o, g, c) for o in far]
     g_devices = [device(a, o, c) for o in near]
     core_device = device(a, g, 1 - c)
-    q_devices = [device(a, partner(g, kg, G), partner(c, kc, 2)) for kg in range(G) for kc in range(2)][1:]
+    q_coords = [(partner(g, kg, G), partner(c, kc, 2)) for kg in range(G) for kc in range(2)][1:]
+    q_devices = [device(a, o, cc) for o, cc in q_coords]
     steps = [(ka, kg, kc) for ka in range(A) for kg in range(G) for kc in range(2)][1:]
     steps.sort(key=lambda step: -(step[0] + bin(step[1]).count("1") + step[2] / 2))
     everyone = [device(partner(a, ka, A), partner(g, kg, G), partner(c, kc, 2)) for ka, kg, kc in steps]
     others = [d for d, step in zip(everyone, steps) if step[0] and (step[1] or step[2])]
 
     WZ, WN, WT, WP, WC = range(5)
-    S_CORE, S_NEAR, S_FAR, S_ALL, S_PAR = range(5)
+    S_PROD, S_NEAR, S_FAR, S_ALL, S_PAR, S_QFAR, S_QNEAR, S_VNEAR, S_VFAR = range(9)
 
     def remote(src, dst, ssem, rsem, device_id):
         copy = pltpu.make_async_remote_copy(
@@ -163,6 +172,8 @@
     def arrived(copies):
         for copy in copies:
             copy.wait_recv()
+
+    nears, fars = pl.ds(0, G - 1), pl.ds(0, A - 1)
 
     local = []
     for i, (src, dst) in enumerate(
@@ -190,7 +201,7 @@
         pl.semaphore_signal(barrier, inc=1, device_id=d, device_id_type=MESH)
 
     local[0].wait()
-    for m in range(MATS):
+    for m in range(MOVED):
         wbuf[m, c, y, a, b] = master[m // 2, m % 2].astype(BF16)
     local[1].wait()
     pl.semaphore_wait(barrier, len(peers))
@@ -214,6 +225,12 @@
             device_id_type=MESH,
         ).wait_recv()
 
+    def slot_sum(ref, count_of, value=None):
+        for i in range(count_of):
+            term = ref[i].astype(F32)
+            value = term if value is None else value + term
+        return value
+
     def await_sent(ref, ssem):
         pltpu.make_async_remote_copy(
             src_ref=ref,
@@ -231,30 +248,30 @@
 
     def w_near(m, ref, j):
         return [
-            remote(ref, ref, w_send.at[WT if m == TURNED else WN], wn_recv.at[m, k], d)
+            remote(ref, ref, w_send.at[WT if m == W_TURNED else WN], wn_recv.at[m, k], d)
             for k, d in enumerate(g_devices)
         ]
 
     def w_far_turned(ref, j):
         for k, d in enumerate(z_devices):
-            remote(ref, ref, w_send.at[WP], wz_recv.at[TURNED, k], d)
+            remote(ref, ref, w_send.at[WP], wz_recv.at[W_TURNED, k], d)
 
     def w_core(m, ref, j):
         remote(ref, ref, w_send.at[WC], wc_recv.at[m], core_device)
 
-    straight = [m for m in range(MATS) if m != TURNED]
+    straight = [m for m in range(MOVED) if m != W_TURNED]
     for k in range(1, n_t):
         o = (t + k) % n_t
         remote(spbuf.at[t], spbuf.at[t], s_send.at[S_PAR], s_recv.at[S_PAR], (dp, o))
     first = {}
     for i, m in enumerate(straight):
         first[m] = w_far(m, piece(m, g, a))
-        if i == 0:
-            first[TURNED] = w_near(TURNED, piece(TURNED, g, a), 0)
+        if i == 0 and W_TURNED is not None:
+            first[W_TURNED] = w_near(W_TURNED, piece(W_TURNED, g, a), 0)
     for i, m in enumerate(straight):
         w_near(m, piece(m, g, a), 0)
-        if i == 0:
-            w_far_turned(piece(TURNED, g, a), 0)
+        if i == 0 and W_TURNED is not None:
+            w_far_turned(piece(W_TURNED, g, a), 0)
 
     for copy in local[2:7]:
         copy.wait()
@@ -300,6 +317,15 @@
     def small_row(i):
         return jnp.concatenate([spbuf[tt, i : i + 1, :] for tt in range(n_t)], 1)
 
+    out_row = small_row(7 + 2 * LAYERS)
+    last_low = master[LAYERS - 1, 1].astype(BF16).astype(F32)
+    feature = lax.broadcasted_iota(jnp.int32, (R, D), 1) - lax.broadcasted_iota(jnp.int32, (R, D), 0)
+    out_column = jnp.sum(jnp.where(feature == dp * R, out_row, 0.0), axis=1, keepdims=True)
+    q_part = jnp.sum(last_low * out_column, axis=0, keepdims=True)
+    qslot_z[a] = jnp.broadcast_to(q_part, (8, cw))
+    for d in z_devices:
+        remote(qslot_z.at[a], qslot_z.at[a], s_send.at[S_QFAR], s_recv.at[S_QFAR], d)
+
     first_rows = [small_row(j) for j in range(6)]
     z0 = small_row(6) + xs[0] * first_rows[0]
     for j in range(1, 6):
@@ -321,12 +347,18 @@
 
     def pass_on_turned():
         for k in range(G - 1):
-            first[TURNED][k].wait_recv()
-            w_far_turned(piece(TURNED, near[k], a), k + 1)
-        w_core(TURNED, plane(TURNED, a), 0)
+            first[W_TURNED][k].wait_recv()
+            w_far_turned(piece(W_TURNED, near[k], a), k + 1)
+        w_core(W_TURNED, plane(W_TURNED, a), 0)
 
     pass_on(straight[0])
-    pass_on_turned()
+    me_near = g * 2 + c
+    await_bytes(qslot_z.at[pl.ds(0, A - 1)], s_recv.at[S_QFAR])
+    qslot_g[me_near] = slot_sum(qslot_z, A)
+    for d in q_devices:
+        remote(qslot_g.at[me_near], qslot_g.at[me_near], s_send.at[S_QNEAR], s_recv.at[S_QNEAR], d)
+    if W_TURNED is not None:
+        pass_on_turned()
     for m in straight[1:]:
         pass_on(m)
 
@@ -355,7 +387,7 @@
                 acts[l + 1, s] = new.astype(BF16)
 
     def fetch(m):
-        if m == TURNED:
+        if m == W_TURNED:
             for k in range(A - 1):
                 await_bytes(plane(m, far[k]), wz_recv.at[m, k])
                 w_core(m, plane(m, far[k]), k + 1)
@@ -367,7 +399,7 @@
     def fetched(m):
         await_bytes(wbuf.at[m, c], wc_recv.at[m])
 
-    for m in range(MATS):
+    for m in range(MOVED):
         fetch(m)
         fetched(m)
         if m == 0:
@@ -377,9 +409,23 @@
             block_in(m // 2)
         else:
             block_out(m // 2)
-
-    out_row = small_row(7 + 2 * LAYERS)
-    proj = [jnp.sum(streams[s] * out_row, 1, keepdims=True) for s in range(4)]
+        if m == MOVED - 2:
+            proj_a = [jnp.sum(streams[s] * out_row, axis=1, keepdims=True) for s in range(4)]
+            bias_row = small_row(6 + 2 * LAYERS)
+            proj_a[0] = proj_a[0] + jnp.sum(bias_row * out_row, axis=1, keepdims=True)
+            await_bytes(qslot_g.at[pl.ds(0, 2 * G - 1)], s_recv.at[S_QNEAR])
+            q_row = []
+            for tt in range(n_t):
+                total = qslot_g[(tt // 2) * B * 2 + tt % 2, 0:1]
+                for i in range(1, B):
+                    total = total + qslot_g[((tt // 2) * B + i) * 2 + tt % 2, 0:1]
+                q_row.append(total)
+            q_row = jnp.concatenate(q_row, 1)
+
+    last = LAYERS - 1
+    proj = [
+        proj_a[s] + jnp.sum(hidden[last, s].astype(F32) * q_row, axis=1, keepdims=True) for s in range(4)
+    ]
     tau = proj[0]
     sign_tau = sign_of(tau)
     abs_tau = jnp.abs(tau)
@@ -392,15 +438,20 @@
     g_time = [2.0 * grad_time[k] * seed for k in range(3)]
     g_tau = sign_tau * (units[0] * g_time[0] + units[1] * g_time[1] + units[2] * g_time[2])
     g_proj = [g_tau] + [distance * sign_tau * g_time[k] for k in range(3)]
-    g_out_row = jnp.sum(
-        streams[0] * g_proj[0] + streams[1] * g_proj[1] + streams[2] * g_proj[2] + streams[3] * g_proj[3],
-        axis=0,
-        keepdims=True,
+    v_row = jnp.sum(
+        sum(hidden[last, s].astype(F32) * g_proj[s] for s in range(4)), axis=0, keepdims=True
     )
-    for s in range(4):
-        value = g_proj[s] * out_row
-        grad[s] = value
-        gbranch[s] = value.astype(BF16)
+    for tt in range(n_t):
+        vsend[tt % 2, tt // 2] = jnp.broadcast_to(v_row[:, tt * cw : (tt + 1) * cw], (8, cw))
+    vslot_g[me_near] = vsend[c, y]
+    for (o, cc), d in zip(q_coords, q_devices):
+        remote(vsend.at[cc, o // B], vslot_g.at[me_near], s_send.at[S_VNEAR], s_recv.at[S_VNEAR], d)
+
+    def v_far():
+        await_bytes(vslot_g.at[pl.ds(0, 2 * G - 1)], s_recv.at[S_VNEAR])
+        vslot_z[a] = slot_sum(vslot_g, 2 * G)
+        for d in z_devices:
+            remote(vslot_z.at[a], vslot_z.at[a], s_send.at[S_VFAR], s_recv.at[S_VFAR], d)
 
     pieces = [(far[k], k) for k in reversed(range(A - 1))] + [(a, None)]
 
@@ -422,12 +473,6 @@
         flying[m][j].wait_recv()
         gone[m, z] = (gsend[m, c, z].astype(F32) + gcore[m, z].astype(F32)).astype(BF16)
 
-    def slot_sum(ref, count_of, value=None):
-        for i in range(count_of):
-            term = ref[i].astype(F32)
-            value = term if value is None else value + term
-        return value
-
     def start_near(m):
         for j, (z, _) in enumerate(pieces):
             core_sum(m, j)
@@ -448,21 +493,21 @@
                 remote(gtwo.at[m, k], gslot_z.at[m, k], g_send.at[WZ], gz_recv.at[m], z_devices[k])
 
     def finish(m):
-        if m == TURNED:
+        if m == G_TURNED:
             await_bytes(tslot_n, gn_recv.at[m, 0])
             return slot_sum(tslot_n, G - 1, gown[m])
         await_bytes(gslot_z.at[m], gz_recv.at[m])
         return slot_sum(gslot_z.at[m], A - 1, gown[m])
 
     def start_far_turned():
-        m = TURNED
+        m = G_TURNED
         for j, (z, k) in enumerate(pieces):
             core_sum(m, j)
             if k is not None:
                 remote(gone.at[m, z], tslot_z.at[k], g_send.at[WP], gz_recv.at[m], z_devices[k])
 
     def start_near_turned():
-        m = TURNED
+        m = G_TURNED
         await_bytes(tslot_z, gz_recv.at[m])
         tback[...] = slot_sum(tslot_z, A - 1, gone[m, a].astype(F32))
         gown[m] = tback[g]
@@ -472,8 +517,28 @@
             remote(tlow.at[o], tslot_n.at[k], g_send.at[WT], gn_recv.at[m, 0], g_devices[k])
 
     flying = {}
+
+    def start_first(m):
+        if m == G_TURNED:
+            start_far_turned()
+        else:
+            start_near(m)
+
     bias_in = [None] * LAYERS
     bias_out = [None] * LAYERS
+
+    def back_last():
+        z = pre[last, 0] + small_row(7 + last)
+        e = jnp.exp(jnp.minimum(z, 0.0))
+        slope = jnp.where(z > 0, 1.0, e)
+        curve = jnp.where(z > 0, 0.0, e)
+        mixed = g_proj[1] * pre[last, 1] + g_proj[2] * pre[last, 2] + g_proj[3] * pre[last, 3]
+        gz = q_row * (g_proj[0] * slope + curve * mixed)
+        bias_in[last] = jnp.sum(gz, axis=0, keepdims=True)
+        gpre[0] = gz.astype(BF16)
+        slope = slope * q_row
+        for k in range(1, 4):
+            gpre[k] = (g_proj[k] * slope).astype(BF16)
 
     def back_out(l):
         bias_out[l] = jnp.sum(grad[0], axis=0, keepdims=True)
@@ -499,23 +564,29 @@
     def back_through(l):
         back = nt(gpre[...].reshape(M, D), weight(2 * l)).reshape(4, Pn, D)
         for s in range(4):
-            value = grad[s] + back[s]
+            value = (out_row * g_proj[s] if l == last else grad[s]) + back[s]
             grad[s] = value
             if l > 0:
                 gbranch[s] = value.astype(BF16)
 
-    back_out(1)
-    back_in(1)
-    start_near(3)
+    back_last()
     back_weight(1)
+    tau_sum = jnp.sum(g_proj[0], axis=0, keepdims=True)
+    bias_out[last] = out_row * tau_sum
+    g_out_row = bias_row * tau_sum + jnp.sum(
+        streams[0] * g_proj[0] + streams[1] * g_proj[1] + streams[2] * g_proj[2] + streams[3] * g_proj[3],
+        axis=0,
+        keepdims=True,
+    )
     back_through(1)
-    start_far_turned()
     back_out(0)
+    start_first(2)
     back_in(0)
-    start_near(1)
     back_weight(0)
+    start_first(1)
+    v_far()
     back_through(0)
-    start_near(0)
+    start_first(0)
 
     z0 = inner[...]
     e0 = jnp.exp(jnp.minimum(z0, 0.0))
@@ -546,29 +617,67 @@
     ]
     for tt in range(n_t):
         sgsend[tt % 2, tt // 2] = jnp.concatenate([r[:, tt * cw : (tt + 1) * cw] for r in rows] + tail, 0)
-    remote(sgsend.at[1 - c], sgcore, s_send.at[S_CORE], s_recv.at[S_CORE], core_device)
-    start_far(3)
-    await_bytes(sgcore, s_recv.at[S_CORE])
-    sgone[...] = sgsend[c] + sgcore[...]
-    sgslot_g[g] = sgone[y]
-    for k, o in enumerate(near):
-        remote(sgone.at[o // B], sgslot_g.at[g], s_send.at[S_NEAR], s_recv.at[S_NEAR], g_devices[k])
-
+    sgslot_g[me_near] = sgsend[c, y]
+    for (o, cc), d in zip(q_coords, q_devices):
+        remote(sgsend.at[cc, o // B], sgslot_g.at[me_near], s_send.at[S_NEAR], s_recv.at[S_NEAR], d)
+
+    await_bytes(vslot_z.at[fars], s_recv.at[S_VFAR])
+    v_part = slot_sum(vslot_z, A)[0:1]
+    product = jnp.sum(last_low * v_part, axis=1, keepdims=True)
+    place = lax.broadcasted_iota(jnp.int32, (R, cw), 1) - lax.broadcasted_iota(jnp.int32, (R, cw), 0)
+    product_row = jnp.sum(jnp.where(place == (dp * R) % cw, product, 0.0), axis=0, keepdims=True)
+    psend[...] = jnp.broadcast_to(product_row, (8, cw))
+    column = (dp * R) // cw
+    mine_too = column == t
+    slot = (dp % (cw // R)) * n_t + t
+    pl.semaphore_wait(barrier, len(others))
+    for k in range(1, A * B):
+        remote(
+            psend, pslot.at[slot], s_send.at[S_PROD], s_recv.at[S_PROD], (partner(dp, k, A * B), column)
+        )
+
+    @pl.when(mine_too)
+    def _():
+        pslot[slot] = psend[...]
+
+    @pl.when(jnp.logical_not(mine_too))
+    def _():
+        remote(psend, pslot.at[slot], s_send.at[S_PROD], s_recv.at[S_PROD], (dp, column))
+
+    def await_products(wait, ref, count_of, sems):
+        @pl.when(mine_too)
+        def _():
+            wait(ref.at[pl.ds(0, count_of - 1)], sems.at[S_PROD])
+
+        @pl.when(jnp.logical_not(mine_too))
+        def _():
+            wait(ref.at[pl.ds(0, count_of)], sems.at[S_PROD])
+
+    if G_TURNED is None:
+        start_far(2)
     start_far(1)
-    start_near_turned()
+    if G_TURNED is not None:
+        start_near_turned()
     start_far(0)
-    await_bytes(sgslot_g.at[pl.ds(0, G - 1)], s_recv.at[S_NEAR])
-    sgtwo[...] = slot_sum(sgslot_g, G)
+    await_bytes(sgslot_g.at[pl.ds(0, 2 * G - 1)], s_recv.at[S_NEAR])
+    sgtwo[...] = slot_sum(sgslot_g, 2 * G)
     sgslot_z[a] = sgtwo[...]
     for d in z_devices:
         remote(sgtwo, sgslot_z.at[a], s_send.at[S_FAR], s_recv.at[S_FAR], d)
 
     for copy in local[7:]:
         copy.wait()
-    for m in (3, 1, TURNED, 0):
+    grad_b[last, 1] = out_column * v_part
+    for m in (1, 2, 0):
         grad_b[m // 2, m % 2] = finish(m)
     await_bytes(sgslot_z.at[pl.ds(0, A - 1)], s_recv.at[S_FAR])
     sred[...] = slot_sum(sgslot_z, A)
+    slots = (cw // R) * n_t
+    await_products(await_bytes, pslot, slots, s_recv)
+    head_row = sred[SMALL - 1 : SMALL]
+    for i in range(slots):
+        head_row = head_row + pslot[i, 0:1]
+    sred[SMALL - 1 : SMALL] = head_row
     counted = sred[SMALL + 1 : SMALL + 2, 0:1]
     tile_rows = lax.broadcasted_iota(jnp.int32, (8, 128), 0)
     parts = jnp.zeros((8, 128), F32)
@@ -593,7 +702,6 @@
     )
     me = (a * G + g) * 2 + c
     arslot[me] = parts
-    pl.semaphore_wait(barrier, len(others))
     for d in everyone:
         remote(arslot.at[me], arslot.at[me], s_send.at[S_ALL], s_recv.at[S_ALL], d)
     loss_b[...] = sred[SMALL : SMALL + 1, 0:1] / counted
@@ -616,15 +724,20 @@
     master_s[...] = new
     average_s[...] = average_decay * asmall[...] + (1.0 - average_decay) * new
 
-    straights, nears, fars = pl.ds(0, MATS - 1), pl.ds(0, G - 1), pl.ds(0, A - 1)
-    for sems in (w_send, g_send):
+    for sems, turned in ((w_send, W_TURNED), (g_send, G_TURNED)):
+        straights = pl.ds(0, MOVED if turned is None else MOVED - 1)
         await_sent(gone.at[straights, fars, 0], sems.at[WZ])
         await_sent(gone.at[straights, :, nears], sems.at[WN])
-        await_sent(gone.at[0, 0, nears], sems.at[WT])
-        await_sent(gone.at[0, fars], sems.at[WP])
+        if turned is not None:
+            await_sent(gone.at[0, 0, nears], sems.at[WT])
+            await_sent(gone.at[0, fars], sems.at[WP])
         await_sent(gone, sems.at[WC])
-    await_sent(sgcore, s_send.at[S_CORE])
-    await_sent(sgslot_g.at[nears], s_send.at[S_NEAR])
+    await_sent(qslot_z.at[fars], s_send.at[S_QFAR])
+    await_sent(vslot_z.at[fars], s_send.at[S_VFAR])
+    await_sent(qslot_g.at[pl.ds(0, 2 * G - 1)], s_send.at[S_QNEAR])
+    await_sent(vslot_g.at[pl.ds(0, 2 * G - 1)], s_send.at[S_VNEAR])
+    await_sent(sgslot_g.at[pl.ds(0, 2 * G - 1)], s_send.at[S_NEAR])
+    await_products(await_sent, pdone, A * B, s_send)
     await_sent(sgslot_z.at[fars], s_send.at[S_FAR])
     await_sent(arslot.at[pl.ds(0, len(everyone))], s_send.at[S_ALL])
     await_sent(spbuf.at[pl.ds(0, n_t - 1)], s_send.at[S_PAR])
@@ -718,7 +831,7 @@
             V((n_t, SMALL, cw), F32),
             V((PB, 128), F32),
             V((S, cw), F32),
-            V((MATS, 2, C, A, B, R, cw), BF16),
+            V((MOVED, 2, C, A, B, R, cw), BF16),
             V((4, Pn, D), F32),
             V((LAYERS, 4, Pn, D), BF16),
             V((LAYERS, 4, Pn, D), F32),
@@ -727,34 +840,40 @@
             V((4, Pn, D), BF16),
             V((4, Pn, D), BF16),
             V((Pn, D), F32),
-            V((MATS, 2, A, G, R, cw), BF16),
-            V((MATS, A, G, R, cw), BF16),
-            V((MATS, A, G, R, cw), BF16),
-            V((MATS, A, G - 1, R, cw), BF16),
-            V((MATS, A - 1, R, cw), BF16),
-            V((MATS, A - 1, R, cw), BF16),
-            V((MATS, R, cw), F32),
+            V((MOVED, 2, A, G, R, cw), BF16),
+            V((MOVED, A, G, R, cw), BF16),
+            V((MOVED, A, G, R, cw), BF16),
+            V((MOVED, A, G - 1, R, cw), BF16),
+            V((MOVED, A - 1, R, cw), BF16),
+            V((MOVED, A - 1, R, cw), BF16),
+            V((MOVED, R, cw), F32),
             V((A - 1, G, R, cw), BF16),
             V((G, R, cw), F32),
             V((G - 1, R, cw), BF16),
             V((2, C, S, cw), F32),
-            V((C, S, cw), F32),
-            V((C, S, cw), F32),
-            V((G, S, cw), F32),
+            V((8, cw), F32),
+            V(((cw // R) * n_t, 8, cw), F32),
+            V((n_dp, 8, cw), F32),
+            V((2 * G, S, cw), F32),
             V((S, cw), F32),
             V((A, S, cw), F32),
             V((2 * A * G, 8, 128), F32),
+            V((A, 8, cw), F32),
+            V((2 * G, 8, cw), F32),
+            V((2, C, 8, cw), F32),
+            V((2 * G, 8, cw), F32),
+            V((A, 8, cw), F32),
             pltpu.SemaphoreType.DMA((len(args),)),
             DMA((5,)),
-            DMA((MATS, A - 1)),
-            DMA((MATS, G - 1)),
-            DMA((MATS,)),
+            DMA((MOVED, A - 1)),
+            DMA((MOVED, G - 1)),
+            DMA((MOVED,)),
             DMA((5,)),
-            DMA((MATS,)),
-            DMA((MATS, A)),
-            DMA((MATS, A)),
-            DMA((5,)),
-            DMA((5,)),
+            DMA((MOVED,)),
+            DMA((MOVED, A)),
+            DMA((MOVED, A)),
+            DMA((9,)),
+            DMA((9,)),
         ],
         compiler_params=pltpu.CompilerParams(
             collective_id=0, has_side_effects=True, vmem_limit_bytes=60 << 20

time: 48.7 us -> 46.8 us (0.961)
  Pallas kernels: 47.8 us -> 46 us
    pallas_call x1, Pallas kernels: 46.3 us -> 44.5 us  [body(): pl.pallas_call(functools.partial(kernel, dims), out_shape=tuple((V(*shape...]
where the time goes in v4:
time: 46.8 us; the launch traced here: 46.7 us
  Pallas kernels  46 us (98%)
  between operations  0.66 us (1%)
    pallas_call x1, Pallas kernels, body(): pl.pallas_call(functools.partial(kernel, dims), out_shape=tuple((V(*shape...  44.5 us
    pallas_call x1, Pallas kernels, body(): pl.pallas_call(write_out, out_shape=tuple((jax.ShapeDtypeStruct(*shape) f...  1.56 us

profile of v4, /device:TPU:0, one launch (start us, length us, event | category | flops | bytes accessed | tf_op | source)
XLA Modules:
  0.0 46.7 jit_solution(11773067618462208429)
XLA Ops:
  0.6 44.5 %shard_map.194 = (f32[1,1]{1,0:T(1,128)}, f32[2,2,64,128]{3,2,1,0:T(8,128)S(1)}, f32[12,128]{1,0:T(8,128)S(1)}, f32[4,128]{1,0:T(4,128)S(1)}, f32[2,2,64,128]{3,...) custom-call(f32[6,768]{1,0:T(8,128)} %coords_hbm.1, ...), custom_call_target="tpu_custom_call" | custom-call | tf_op jit(solution)/shard_map/pallas_call | solution.py:815
  45.1 1.6 %shard_map.195 = (f32[1,1]{1,0:T(1,128)}, f32[2,2,64,128]{3,2,1,0:T(8,128)}, f32[12,128]{1,0:T(8,128)}, f32[4,128]{1,0:T(4,128)}, f32[2,2,64,128]{3,2,1,0:T(8,12...) custom-call(f32[1,1]{1,0:T(1,128)} %get-tuple-element.33.refs_0_, ...), custom_call_target="tpu_custom_call" | custom-call | tf_op jit(solution)/shard_map/pallas_call | solution.py:883

commit v5 on v4

--- a/solution.py
+++ b/solution.py
@@ -20,8 +20,8 @@
 norm_epsilon = 1e-12
 
 MOVED = MATS - 1
-W_TURNED = 2
-G_TURNED = None
+W_TURNED = (0, 1)
+G_TURNED = (1, 0)
 
 
 def partner(i, k, size):
@@ -103,7 +103,7 @@
     gslot_z,
     gown,
     tslot_z,
-    tback,
+    tlow,
     tslot_n,
     sgsend,
     psend,
@@ -122,10 +122,12 @@
     w_send,
     wz_recv,
     wn_recv,
+    wt_recv,
     wc_recv,
     g_send,
     gz_recv,
     gn_recv,
+    gt_recv,
     gc_recv,
     s_send,
     s_recv,
@@ -154,7 +156,14 @@
     everyone = [device(partner(a, ka, A), partner(g, kg, G), partner(c, kc, 2)) for ka, kg, kc in steps]
     others = [d for d, step in zip(everyone, steps) if step[0] and (step[1] or step[2])]
 
-    WZ, WN, WT, WP, WC = range(5)
+    WZ, WO, WN, WX, WT, WP, WC = range(7)
+    FARTHEST = G - 2
+    w_turned = W_TURNED if G > 2 else ()
+    g_turned = G_TURNED if G > 2 else ()
+
+    def plain_near(m, turned):
+        return range(G - 2 if m in turned else G - 1)
+
     S_PROD, S_NEAR, S_FAR, S_ALL, S_PAR, S_QFAR, S_QNEAR, S_VNEAR, S_VFAR = range(9)
 
     def remote(src, dst, ssem, rsem, device_id):
@@ -246,32 +255,20 @@
             remote(ref, ref, w_send.at[WZ], wz_recv.at[m, k], d) for k, d in enumerate(z_devices)
         ]
 
-    def w_near(m, ref, j):
-        return [
-            remote(ref, ref, w_send.at[WT if m == W_TURNED else WN], wn_recv.at[m, k], d)
-            for k, d in enumerate(g_devices)
-        ]
-
-    def w_far_turned(ref, j):
-        for k, d in enumerate(z_devices):
-            remote(ref, ref, w_send.at[WP], wz_recv.at[W_TURNED, k], d)
-
-    def w_core(m, ref, j):
+    def w_near(m, ref, ks, ssem):
+        for k in ks:
+            remote(ref, ref, w_send.at[ssem], wn_recv.at[m, k], g_devices[k])
+
+    def w_core(m, ref):
         remote(ref, ref, w_send.at[WC], wc_recv.at[m], core_device)
 
-    straight = [m for m in range(MOVED) if m != W_TURNED]
     for k in range(1, n_t):
         o = (t + k) % n_t
         remote(spbuf.at[t], spbuf.at[t], s_send.at[S_PAR], s_recv.at[S_PAR], (dp, o))
     first = {}
-    for i, m in enumerate(straight):
+    for m in range(MOVED):
         first[m] = w_far(m, piece(m, g, a))
-        if i == 0 and W_TURNED is not None:
-            first[W_TURNED] = w_near(W_TURNED, piece(W_TURNED, g, a), 0)
-    for i, m in enumerate(straight):
-        w_near(m, piece(m, g, a), 0)
-        if i == 0 and W_TURNED is not None:
-            w_far_turned(piece(W_TURNED, g, a), 0)
+        w_near(m, piece(m, g, a), reversed(range(G - 1)), WO)
 
     for copy in local[2:7]:
         copy.wait()
@@ -342,24 +339,22 @@
     def pass_on(m):
         for k in range(A - 1):
             first[m][k].wait_recv()
-            w_near(m, piece(m, g, far[k]), k + 1)
-        w_core(m, line(m, g), 0)
-
-    def pass_on_turned():
-        for k in range(G - 1):
-            first[W_TURNED][k].wait_recv()
-            w_far_turned(piece(W_TURNED, near[k], a), k + 1)
-        w_core(W_TURNED, plane(W_TURNED, a), 0)
-
-    pass_on(straight[0])
+            w_near(m, piece(m, g, far[k]), plain_near(m, w_turned), WX if m in w_turned else WN)
+        w_core(m, line(m, g))
+        if m in w_turned:
+            o = near[FARTHEST]
+            ref = piece(m, o, a)
+            await_bytes(ref, wn_recv.at[m, FARTHEST])
+            for d in z_devices:
+                remote(ref, ref, w_send.at[WT], wt_recv.at[m], d)
+
+    pass_on(0)
     me_near = g * 2 + c
-    await_bytes(qslot_z.at[pl.ds(0, A - 1)], s_recv.at[S_QFAR])
+    await_bytes(qslot_z.at[fars], s_recv.at[S_QFAR])
     qslot_g[me_near] = slot_sum(qslot_z, A)
     for d in q_devices:
         remote(qslot_g.at[me_near], qslot_g.at[me_near], s_send.at[S_QNEAR], s_recv.at[S_QNEAR], d)
-    if W_TURNED is not None:
-        pass_on_turned()
-    for m in straight[1:]:
+    for m in range(1, MOVED):
         pass_on(m)
 
     def weight(m):
@@ -387,14 +382,12 @@
                 acts[l + 1, s] = new.astype(BF16)
 
     def fetch(m):
-        if m == W_TURNED:
-            for k in range(A - 1):
-                await_bytes(plane(m, far[k]), wz_recv.at[m, k])
-                w_core(m, plane(m, far[k]), k + 1)
-        else:
-            for k in range(G - 1):
+        for k in range(G - 1):
+            if m in w_turned and k == FARTHEST:
+                await_bytes(wbuf.at[m, c, 0, fars, 0], wt_recv.at[m])
+            else:
                 await_bytes(line(m, near[k]), wn_recv.at[m, k])
-                w_core(m, line(m, near[k]), k + 1)
+            w_core(m, line(m, near[k]))
 
     def fetched(m):
         await_bytes(wbuf.at[m, c], wc_recv.at[m])
@@ -474,55 +467,53 @@
         gone[m, z] = (gsend[m, c, z].astype(F32) + gcore[m, z].astype(F32)).astype(BF16)
 
     def start_near(m):
-        for j, (z, _) in enumerate(pieces):
+        for j, (z, kz) in enumerate(pieces):
             core_sum(m, j)
-            for k, o in enumerate(near):
+            for k in plain_near(m, g_turned):
                 remote(
-                    gone.at[m, z, o], gslot_n.at[m, j, k], g_send.at[WN], gn_recv.at[m, j], g_devices[k]
+                    gone.at[m, z, near[k]],
+                    gslot_n.at[m, j, k],
+                    g_send.at[WX if m in g_turned else WN],
+                    gn_recv.at[m, j],
+                    g_devices[k],
                 )
+            if m in g_turned and kz is not None:
+                remote(
+                    gone.at[m, z, near[FARTHEST]],
+                    tslot_z.at[m, kz],
+                    g_send.at[WT],
+                    gt_recv.at[m, 0],
+                    z_devices[kz],
+                )
 
     def start_far(m):
+        count_of = len(plain_near(m, g_turned))
         for j, (z, k) in enumerate(pieces):
-            if G > 1:
-                await_bytes(gslot_n.at[m, j], gn_recv.at[m, j])
-            total = slot_sum(gslot_n.at[m, j], G - 1, gone[m, z, g].astype(F32))
+            if count_of:
+                await_bytes(gslot_n.at[m, j, pl.ds(0, count_of)], gn_recv.at[m, j])
+            total = slot_sum(gslot_n.at[m, j], count_of, gone[m, z, g].astype(F32))
             if k is None:
                 gown[m] = total
             else:
                 gtwo[m, k] = total.astype(BF16)
                 remote(gtwo.at[m, k], gslot_z.at[m, k], g_send.at[WZ], gz_recv.at[m], z_devices[k])
 
+    def start_turned(m):
+        if m in g_turned:
+            await_bytes(tslot_z.at[m], gt_recv.at[m, 0])
+            total = slot_sum(tslot_z.at[m], A - 1, gone[m, a, near[FARTHEST]].astype(F32))
+            tlow[m] = total.astype(BF16)
+            remote(tlow.at[m], tslot_n.at[m], g_send.at[WP], gt_recv.at[m, 1], g_devices[FARTHEST])
+
     def finish(m):
-        if m == G_TURNED:
-            await_bytes(tslot_n, gn_recv.at[m, 0])
-            return slot_sum(tslot_n, G - 1, gown[m])
         await_bytes(gslot_z.at[m], gz_recv.at[m])
-        return slot_sum(gslot_z.at[m], A - 1, gown[m])
-
-    def start_far_turned():
-        m = G_TURNED
-        for j, (z, k) in enumerate(pieces):
-            core_sum(m, j)
-            if k is not None:
-                remote(gone.at[m, z], tslot_z.at[k], g_send.at[WP], gz_recv.at[m], z_devices[k])
-
-    def start_near_turned():
-        m = G_TURNED
-        await_bytes(tslot_z, gz_recv.at[m])
-        tback[...] = slot_sum(tslot_z, A - 1, gone[m, a].astype(F32))
-        gown[m] = tback[g]
-        tlow = gone.at[m, a]
-        tlow[...] = tback[...].astype(BF16)
-        for k, o in enumerate(near):
-            remote(tlow.at[o], tslot_n.at[k], g_send.at[WT], gn_recv.at[m, 0], g_devices[k])
+        total = slot_sum(gslot_z.at[m], A - 1, gown[m])
+        if m in g_turned:
+            await_bytes(tslot_n.at[m], gt_recv.at[m, 1])
+            total = total + tslot_n[m].astype(F32)
+        return total
 
     flying = {}
-
-    def start_first(m):
-        if m == G_TURNED:
-            start_far_turned()
-        else:
-            start_near(m)
 
     bias_in = [None] * LAYERS
     bias_out = [None] * LAYERS
@@ -580,13 +571,13 @@
     )
     back_through(1)
     back_out(0)
-    start_first(2)
+    start_near(2)
     back_in(0)
     back_weight(0)
-    start_first(1)
+    start_near(1)
     v_far()
     back_through(0)
-    start_first(0)
+    start_near(0)
 
     z0 = inner[...]
     e0 = jnp.exp(jnp.minimum(z0, 0.0))
@@ -653,12 +644,12 @@
         def _():
             wait(ref.at[pl.ds(0, count_of)], sems.at[S_PROD])
 
-    if G_TURNED is None:
-        start_far(2)
+    start_far(2)
+    start_turned(2)
     start_far(1)
-    if G_TURNED is not None:
-        start_near_turned()
+    start_turned(1)
     start_far(0)
+    start_turned(0)
     await_bytes(sgslot_g.at[pl.ds(0, 2 * G - 1)], s_recv.at[S_NEAR])
     sgtwo[...] = slot_sum(sgslot_g, 2 * G)
     sgslot_z[a] = sgtwo[...]
@@ -724,14 +715,19 @@
     master_s[...] = new
     average_s[...] = average_decay * asmall[...] + (1.0 - average_decay) * new
 
-    for sems, turned in ((w_send, W_TURNED), (g_send, G_TURNED)):
-        straights = pl.ds(0, MOVED if turned is None else MOVED - 1)
-        await_sent(gone.at[straights, fars, 0], sems.at[WZ])
-        await_sent(gone.at[straights, :, nears], sems.at[WN])
-        if turned is not None:
-            await_sent(gone.at[0, 0, nears], sems.at[WT])
-            await_sent(gone.at[0, fars], sems.at[WP])
+    for sems, turned, passed in ((w_send, w_turned, A - 1), (g_send, g_turned, A)):
+        few, many = pl.ds(0, len(turned)), pl.ds(0, MOVED - len(turned))
+        all_passed = pl.ds(0, passed)
+        await_sent(gone.at[:, fars, 0], sems.at[WZ])
+        if len(turned) < MOVED:
+            await_sent(gone.at[many, all_passed, nears], sems.at[WN])
+        if turned:
+            await_sent(gone.at[few, all_passed, pl.ds(0, G - 2)], sems.at[WX])
+            await_sent(gone.at[few, fars, 0], sems.at[WT])
         await_sent(gone, sems.at[WC])
+    await_sent(gone.at[:, 0, nears], w_send.at[WO])
+    if g_turned:
+        await_sent(gone.at[pl.ds(0, len(g_turned)), 0, 0], g_send.at[WP])
     await_sent(qslot_z.at[fars], s_send.at[S_QFAR])
     await_sent(vslot_z.at[fars], s_send.at[S_VFAR])
     await_sent(qslot_g.at[pl.ds(0, 2 * G - 1)], s_send.at[S_QNEAR])
@@ -847,9 +843,9 @@
             V((MOVED, A - 1, R, cw), BF16),
             V((MOVED, A - 1, R, cw), BF16),
             V((MOVED, R, cw), F32),
-            V((A - 1, G, R, cw), BF16),
-            V((G, R, cw), F32),
-            V((G - 1, R, cw), BF16),
+            V((MOVED, A - 1, R, cw), BF16),
+            V((MOVED, R, cw), BF16),
+            V((MOVED, R, cw), BF16),
             V((2, C, S, cw), F32),
             V((8, cw), F32),
             V(((cw // R) * n_t, 8, cw), F32),
@@ -864,13 +860,15 @@
             V((2 * G, 8, cw), F32),
             V((A, 8, cw), F32),
             pltpu.SemaphoreType.DMA((len(args),)),
-            DMA((5,)),
+            DMA((7,)),
             DMA((MOVED, A - 1)),
             DMA((MOVED, G - 1)),
             DMA((MOVED,)),
-            DMA((5,)),
+            DMA((MOVED,)),
+            DMA((7,)),
             DMA((MOVED,)),
             DMA((MOVED, A)),
+            DMA((MOVED, 2)),
             DMA((MOVED, A)),
             DMA((9,)),
             DMA((9,)),

time: 46.8 us -> 44.7 us (0.955)
  Pallas kernels: 46 us -> 43.9 us
    pallas_call x1, Pallas kernels: 44.5 us -> 42.3 us  [body(): pl.pallas_call(functools.partial(kernel, dims), out_shape=tuple((V(*shape...]
where the time goes in v5:
time: 44.7 us; the launch traced here: 44.6 us
  Pallas kernels  43.9 us (98%)
  between operations  0.66 us (1%)
    pallas_call x1, Pallas kernels, body(): pl.pallas_call(functools.partial(kernel, dims), out_shape=tuple((V(*shape...  42.3 us
    pallas_call x1, Pallas kernels, body(): pl.pallas_call(write_out, out_shape=tuple((jax.ShapeDtypeStruct(*shape) f...  1.56 us

profile of v5, /device:TPU:0, one launch (start us, length us, event | category | flops | bytes accessed | tf_op | source)
XLA Modules:
  0.0 44.6 jit_solution(11205412108763953203)
XLA Ops:
  0.6 42.3 %shard_map.194 = (f32[1,1]{1,0:T(1,128)}, f32[2,2,64,128]{3,2,1,0:T(8,128)S(1)}, f32[12,128]{1,0:T(8,128)S(1)}, f32[4,128]{1,0:T(4,128)S(1)}, f32[2,2,64,128]{3,...) custom-call(f32[6,768]{1,0:T(8,128)} %coords_hbm.1, ...), custom_call_target="tpu_custom_call" | custom-call | tf_op jit(solution)/shard_map/pallas_call | solution.py:811
  43.0 1.6 %shard_map.195 = (f32[1,1]{1,0:T(1,128)}, f32[2,2,64,128]{3,2,1,0:T(8,128)}, f32[12,128]{1,0:T(8,128)}, f32[4,128]{1,0:T(4,128)}, f32[2,2,64,128]{3,2,1,0:T(8,12...) custom-call(f32[1,1]{1,0:T(1,128)} %get-tuple-element.33.refs_0_, ...), custom_call_target="tpu_custom_call" | custom-call | tf_op jit(solution)/shard_map/pallas_call | solution.py:881

commit v6 on v5

--- a/solution.py
+++ b/solution.py
@@ -21,7 +21,7 @@
 
 MOVED = MATS - 1
 W_TURNED = (0, 1)
-G_TURNED = (1, 0)
+G_TURNED = (2, 1, 0)
 
 
 def partner(i, k, size):
@@ -348,14 +348,13 @@
             for d in z_devices:
                 remote(ref, ref, w_send.at[WT], wt_recv.at[m], d)
 
-    pass_on(0)
+    for m in range(MOVED):
+        pass_on(m)
     me_near = g * 2 + c
     await_bytes(qslot_z.at[fars], s_recv.at[S_QFAR])
     qslot_g[me_near] = slot_sum(qslot_z, A)
     for d in q_devices:
         remote(qslot_g.at[me_near], qslot_g.at[me_near], s_send.at[S_QNEAR], s_recv.at[S_QNEAR], d)
-    for m in range(1, MOVED):
-        pass_on(m)
 
     def weight(m):
         return jnp.concatenate([wbuf[m, tt % 2, tt // 2].reshape(D, cw) for tt in range(n_t)], 1)
@@ -575,8 +574,8 @@
     back_in(0)
     back_weight(0)
     start_near(1)
+    back_through(0)
     v_far()
-    back_through(0)
     start_near(0)
 
     z0 = inner[...]

time: 44.7 us -> 44.2 us (0.989)
  Pallas kernels: 43.9 us -> 43.4 us
    pallas_call x1, Pallas kernels: 42.3 us -> 41.9 us  [body(): pl.pallas_call(functools.partial(kernel, dims), out_shape=tuple((V(*shape...]
where the time goes in v6:
time: 44.2 us; the launch traced here: 44.1 us
  Pallas kernels  43.4 us (98%)
  between operations  0.66 us (1%)
    pallas_call x1, Pallas kernels, body(): pl.pallas_call(functools.partial(kernel, dims), out_shape=tuple((V(*shape...  41.9 us
    pallas_call x1, Pallas kernels, body(): pl.pallas_call(write_out, out_shape=tuple((jax.ShapeDtypeStruct(*shape) f...  1.56 us

profile of v6, /device:TPU:0, one launch (start us, length us, event | category | flops | bytes accessed | tf_op | source)
XLA Modules:
  0.0 44.1 jit_solution(10085549797872418758)
XLA Ops:
  0.6 41.9 %shard_map.194 = (f32[1,1]{1,0:T(1,128)}, f32[2,2,64,128]{3,2,1,0:T(8,128)S(1)}, f32[12,128]{1,0:T(8,128)S(1)}, f32[4,128]{1,0:T(4,128)S(1)}, f32[2,2,64,128]{3,...) custom-call(f32[6,768]{1,0:T(8,128)} %coords_hbm.1, ...), custom_call_target="tpu_custom_call" | custom-call | tf_op jit(solution)/shard_map/pallas_call | solution.py:810
  42.5 1.6 %shard_map.195 = (f32[1,1]{1,0:T(1,128)}, f32[2,2,64,128]{3,2,1,0:T(8,128)}, f32[12,128]{1,0:T(8,128)}, f32[4,128]{1,0:T(4,128)}, f32[2,2,64,128]{3,2,1,0:T(8,12...) custom-call(f32[1,1]{1,0:T(1,128)} %get-tuple-element.33.refs_0_, ...), custom_call_target="tpu_custom_call" | custom-call | tf_op jit(solution)/shard_map/pallas_call | solution.py:880

commit v7 on v6

--- a/solution.py
+++ b/solution.py
@@ -109,6 +109,7 @@
     psend,
     pslot,
     pdone,
+    sized,
     sgslot_g,
     sgtwo,
     sgslot_z,
@@ -156,7 +157,6 @@
     everyone = [device(partner(a, ka, A), partner(g, kg, G), partner(c, kc, 2)) for ka, kg, kc in steps]
     others = [d for d, step in zip(everyone, steps) if step[0] and (step[1] or step[2])]
 
-    WZ, WO, WN, WX, WT, WP, WC = range(7)
     FARTHEST = G - 2
     w_turned = W_TURNED if G > 2 else ()
     g_turned = G_TURNED if G > 2 else ()
@@ -252,15 +252,15 @@
 
     def w_far(m, ref):
         return [
-            remote(ref, ref, w_send.at[WZ], wz_recv.at[m, k], d) for k, d in enumerate(z_devices)
+            remote(ref, ref, w_send.at[0], wz_recv.at[m, k], d) for k, d in enumerate(z_devices)
         ]
 
-    def w_near(m, ref, ks, ssem):
+    def w_near(m, ref, ks):
         for k in ks:
-            remote(ref, ref, w_send.at[ssem], wn_recv.at[m, k], g_devices[k])
+            remote(ref, ref, w_send.at[0], wn_recv.at[m, k], g_devices[k])
 
     def w_core(m, ref):
-        remote(ref, ref, w_send.at[WC], wc_recv.at[m], core_device)
+        remote(ref, ref, w_send.at[0], wc_recv.at[m], core_device)
 
     for k in range(1, n_t):
         o = (t + k) % n_t
@@ -268,7 +268,7 @@
     first = {}
     for m in range(MOVED):
         first[m] = w_far(m, piece(m, g, a))
-        w_near(m, piece(m, g, a), reversed(range(G - 1)), WO)
+        w_near(m, piece(m, g, a), reversed(range(G - 1)))
 
     for copy in local[2:7]:
         copy.wait()
@@ -319,7 +319,9 @@
     feature = lax.broadcasted_iota(jnp.int32, (R, D), 1) - lax.broadcasted_iota(jnp.int32, (R, D), 0)
     out_column = jnp.sum(jnp.where(feature == dp * R, out_row, 0.0), axis=1, keepdims=True)
     q_part = jnp.sum(last_low * out_column, axis=0, keepdims=True)
-    qslot_z[a] = jnp.broadcast_to(q_part, (8, cw))
+    count = jnp.sum(mask, axis=0, keepdims=True)
+    row_of_8 = lax.broadcasted_iota(jnp.int32, (8, cw), 0)
+    qslot_z[a] = jnp.where(row_of_8 == 0, q_part, count)
     for d in z_devices:
         remote(qslot_z.at[a], qslot_z.at[a], s_send.at[S_QFAR], s_recv.at[S_QFAR], d)
 
@@ -339,14 +341,14 @@
     def pass_on(m):
         for k in range(A - 1):
             first[m][k].wait_recv()
-            w_near(m, piece(m, g, far[k]), plain_near(m, w_turned), WX if m in w_turned else WN)
+            w_near(m, piece(m, g, far[k]), plain_near(m, w_turned))
         w_core(m, line(m, g))
         if m in w_turned:
             o = near[FARTHEST]
             ref = piece(m, o, a)
             await_bytes(ref, wn_recv.at[m, FARTHEST])
             for d in z_devices:
-                remote(ref, ref, w_send.at[WT], wt_recv.at[m], d)
+                remote(ref, ref, w_send.at[0], wt_recv.at[m], d)
 
     for m in range(MOVED):
         pass_on(m)
@@ -413,6 +415,7 @@
                     total = total + qslot_g[((tt // 2) * B + i) * 2 + tt % 2, 0:1]
                 q_row.append(total)
             q_row = jnp.concatenate(q_row, 1)
+            counted = slot_sum(qslot_g, 2 * G)[1:2, 0:1]
 
     last = LAYERS - 1
     proj = [
@@ -425,7 +428,6 @@
     square = grad_time[0] * grad_time[0] + grad_time[1] * grad_time[1] + grad_time[2] * grad_time[2]
     error = square - truth * truth
     total_err = jnp.sum(mask * jnp.abs(error), axis=0, keepdims=True)
-    count = jnp.sum(mask, axis=0, keepdims=True)
     seed = mask * sign_of(error)
     g_time = [2.0 * grad_time[k] * seed for k in range(3)]
     g_tau = sign_tau * (units[0] * g_time[0] + units[1] * g_time[1] + units[2] * g_time[2])
@@ -453,26 +455,22 @@
             block = low[:, tt * cw : (tt + 1) * cw].reshape(A, B, R, cw)
             for i in range(B):
                 gsend[m, tt % 2, :, (tt // 2) * B + i] = block[:, i]
-        return [
-            remote(
-                gsend.at[m, 1 - c, z], gcore.at[m, z], g_send.at[WC], gc_recv.at[m, j], core_device
-            )
-            for j, (z, k) in enumerate(pieces)
-        ]
+        for z, _ in pieces:
+            remote(gsend.at[m, 1 - c, z], gcore.at[m, z], g_send.at[0], gc_recv.at[m], core_device)
 
     def core_sum(m, j):
         z = pieces[j][0]
-        flying[m][j].wait_recv()
         gone[m, z] = (gsend[m, c, z].astype(F32) + gcore[m, z].astype(F32)).astype(BF16)
 
     def start_near(m):
+        await_bytes(gcore.at[m], gc_recv.at[m])
         for j, (z, kz) in enumerate(pieces):
             core_sum(m, j)
             for k in plain_near(m, g_turned):
                 remote(
                     gone.at[m, z, near[k]],
                     gslot_n.at[m, j, k],
-                    g_send.at[WX if m in g_turned else WN],
+                    g_send.at[0],
                     gn_recv.at[m, j],
                     g_devices[k],
                 )
@@ -480,7 +478,7 @@
                 remote(
                     gone.at[m, z, near[FARTHEST]],
                     tslot_z.at[m, kz],
-                    g_send.at[WT],
+                    g_send.at[0],
                     gt_recv.at[m, 0],
                     z_devices[kz],
                 )
@@ -495,14 +493,14 @@
                 gown[m] = total
             else:
                 gtwo[m, k] = total.astype(BF16)
-                remote(gtwo.at[m, k], gslot_z.at[m, k], g_send.at[WZ], gz_recv.at[m], z_devices[k])
+                remote(gtwo.at[m, k], gslot_z.at[m, k], g_send.at[0], gz_recv.at[m], z_devices[k])
 
     def start_turned(m):
         if m in g_turned:
             await_bytes(tslot_z.at[m], gt_recv.at[m, 0])
             total = slot_sum(tslot_z.at[m], A - 1, gone[m, a, near[FARTHEST]].astype(F32))
             tlow[m] = total.astype(BF16)
-            remote(tlow.at[m], tslot_n.at[m], g_send.at[WP], gt_recv.at[m, 1], g_devices[FARTHEST])
+            remote(tlow.at[m], tslot_n.at[m], g_send.at[0], gt_recv.at[m, 1], g_devices[FARTHEST])
 
     def finish(m):
         await_bytes(gslot_z.at[m], gz_recv.at[m])
@@ -511,8 +509,6 @@
             await_bytes(tslot_n.at[m], gt_recv.at[m, 1])
             total = total + tslot_n[m].astype(F32)
         return total
-
-    flying = {}
 
     bias_in = [None] * LAYERS
     bias_out = [None] * LAYERS
@@ -533,7 +529,7 @@
     def back_out(l):
         bias_out[l] = jnp.sum(grad[0], axis=0, keepdims=True)
         gb = gbranch[...].reshape(M, D)
-        flying[2 * l + 1] = start_core(2 * l + 1, tn(gb, hidden[l].reshape(M, D)))
+        start_core(2 * l + 1, tn(gb, hidden[l].reshape(M, D)))
 
     def back_in(l):
         gb = gbranch[...].reshape(M, D)
@@ -549,7 +545,7 @@
             gpre[k] = (gh[k] * slope).astype(BF16)
 
     def back_weight(l):
-        flying[2 * l] = start_core(2 * l, tn(acts[l].reshape(M, D), gpre[...].reshape(M, D)))
+        start_core(2 * l, tn(acts[l].reshape(M, D), gpre[...].reshape(M, D)))
 
     def back_through(l):
         back = nt(gpre[...].reshape(M, D), weight(2 * l)).reshape(4, Pn, D)
@@ -576,7 +572,6 @@
     start_near(1)
     back_through(0)
     v_far()
-    start_near(0)
 
     z0 = inner[...]
     e0 = jnp.exp(jnp.minimum(z0, 0.0))
@@ -601,15 +596,36 @@
     weight_sq = jnp.where(lanes == MATS, jnp.sum(own_small * own_small, keepdims=True) / (A * B), weight_sq)
     tail = [
         jnp.broadcast_to(total_err, (1, cw)),
-        jnp.broadcast_to(count, (1, cw)),
         weight_sq,
-        jnp.zeros((1, cw), F32),
+        jnp.zeros((2, cw), F32),
     ]
     for tt in range(n_t):
         sgsend[tt % 2, tt // 2] = jnp.concatenate([r[:, tt * cw : (tt + 1) * cw] for r in rows] + tail, 0)
     sgslot_g[me_near] = sgsend[c, y]
     for (o, cc), d in zip(q_coords, q_devices):
         remote(sgsend.at[cc, o // B], sgslot_g.at[me_near], s_send.at[S_NEAR], s_recv.at[S_NEAR], d)
+    start_near(0)
+
+    for copy in local[7:]:
+        copy.wait()
+    tile_rows = lax.broadcasted_iota(jnp.int32, (8, 128), 0)
+
+    def step(gradient, momentum):
+        new = momentum_coef * momentum + gradient
+        return new, gradient + momentum_coef * new
+
+    def settle(m, total):
+        at = (m // 2, m % 2)
+        gr = total / counted
+        new, direction = step(gr, moment[at])
+        grad_b[at] = gr
+        moment_b[at] = new
+        return jnp.where(tile_rows == m, jnp.sum(direction * direction, keepdims=True), 0.0)
+
+    start_far(2)
+    start_turned(2)
+    start_far(1)
+    start_turned(1)
 
     await_bytes(vslot_z.at[fars], s_recv.at[S_VFAR])
     v_part = slot_sum(vslot_z, A)[0:1]
@@ -643,10 +659,6 @@
         def _():
             wait(ref.at[pl.ds(0, count_of)], sems.at[S_PROD])
 
-    start_far(2)
-    start_turned(2)
-    start_far(1)
-    start_turned(1)
     start_far(0)
     start_turned(0)
     await_bytes(sgslot_g.at[pl.ds(0, 2 * G - 1)], s_recv.at[S_NEAR])
@@ -655,40 +667,23 @@
     for d in z_devices:
         remote(sgtwo, sgslot_z.at[a], s_send.at[S_FAR], s_recv.at[S_FAR], d)
 
-    for copy in local[7:]:
-        copy.wait()
-    grad_b[last, 1] = out_column * v_part
-    for m in (1, 2, 0):
-        grad_b[m // 2, m % 2] = finish(m)
-    await_bytes(sgslot_z.at[pl.ds(0, A - 1)], s_recv.at[S_FAR])
-    sred[...] = slot_sum(sgslot_z, A)
+    parts = settle(MATS - 1, out_column * v_part)
+    for m in (2, 1, 0):
+        parts = parts + settle(m, finish(m))
     slots = (cw // R) * n_t
     await_products(await_bytes, pslot, slots, s_recv)
+    await_bytes(sgslot_z.at[fars], s_recv.at[S_FAR])
+    sred[...] = slot_sum(sgslot_z, A)
     head_row = sred[SMALL - 1 : SMALL]
     for i in range(slots):
         head_row = head_row + pslot[i, 0:1]
     sred[SMALL - 1 : SMALL] = head_row
-    counted = sred[SMALL + 1 : SMALL + 2, 0:1]
-    tile_rows = lax.broadcasted_iota(jnp.int32, (8, 128), 0)
-    parts = jnp.zeros((8, 128), F32)
-
-    def step(gradient, momentum):
-        new = momentum_coef * momentum + gradient
-        return new, gradient + momentum_coef * new
-
-    for m in range(MATS):
-        at = (m // 2, m % 2)
-        gr = grad_b[at] / counted
-        new, direction = step(gr, moment[at])
-        grad_b[at] = gr
-        moment_b[at] = new
-        parts = jnp.where(tile_rows == m, jnp.sum(direction * direction, keepdims=True), parts)
     gr = sred[0:SMALL, :] / counted
     new, dir_small = step(gr, msmall[...])
     grad_s[...] = gr
     moment_s[...] = new
-    parts = jnp.where(
-        tile_rows == MATS, jnp.sum(dir_small * dir_small, keepdims=True) / (A * B), parts
+    parts = parts + jnp.where(
+        tile_rows == MATS, jnp.sum(dir_small * dir_small, keepdims=True) / (A * B), 0.0
     )
     me = (a * G + g) * 2 + c
     arslot[me] = parts
@@ -700,7 +695,7 @@
     dir_sq = jnp.sum(arslot[...], axis=0)
 
     def rate_of(m):
-        size = sred[SMALL + 2 : SMALL + 3, m : m + 1]
+        size = sred[SMALL + 1 : SMALL + 2, m : m + 1]
         return spread_rate * jnp.sqrt(size) / jnp.sqrt(dir_sq[m : m + 1, 0:1] + norm_epsilon)
 
     for m in range(MATS):
@@ -714,19 +709,11 @@
     master_s[...] = new
     average_s[...] = average_decay * asmall[...] + (1.0 - average_decay) * new
 
-    for sems, turned, passed in ((w_send, w_turned, A - 1), (g_send, g_turned, A)):
-        few, many = pl.ds(0, len(turned)), pl.ds(0, MOVED - len(turned))
-        all_passed = pl.ds(0, passed)
-        await_sent(gone.at[:, fars, 0], sems.at[WZ])
-        if len(turned) < MOVED:
-            await_sent(gone.at[many, all_passed, nears], sems.at[WN])
-        if turned:
-            await_sent(gone.at[few, all_passed, pl.ds(0, G - 2)], sems.at[WX])
-            await_sent(gone.at[few, fars, 0], sems.at[WT])
-        await_sent(gone, sems.at[WC])
-    await_sent(gone.at[:, 0, nears], w_send.at[WO])
-    if g_turned:
-        await_sent(gone.at[pl.ds(0, len(g_turned)), 0, 0], g_send.at[WP])
+    n_w, n_g = len(w_turned), len(g_turned)
+    gathered = MOVED * (A - 1 + G - 1 + A * G) + (A - 1) * (MOVED * (G - 1) - n_w) + n_w * (A - 1)
+    scattered = MOVED * (A - 1 + A * G) + A * (MOVED * (G - 1) - n_g) + n_g * A
+    await_sent(sized.at[pl.ds(0, gathered)], w_send.at[0])
+    await_sent(sized.at[pl.ds(0, scattered)], g_send.at[0])
     await_sent(qslot_z.at[fars], s_send.at[S_QFAR])
     await_sent(vslot_z.at[fars], s_send.at[S_VFAR])
     await_sent(qslot_g.at[pl.ds(0, 2 * G - 1)], s_send.at[S_QNEAR])
@@ -849,6 +836,7 @@
             V((8, cw), F32),
             V(((cw // R) * n_t, 8, cw), F32),
             V((n_dp, 8, cw), F32),
+            V((MOVED * A * (2 * G + 1), R, cw), BF16),
             V((2 * G, S, cw), F32),
             V((S, cw), F32),
             V((A, S, cw), F32),
@@ -859,16 +847,16 @@
             V((2 * G, 8, cw), F32),
             V((A, 8, cw), F32),
             pltpu.SemaphoreType.DMA((len(args),)),
-            DMA((7,)),
+            DMA((1,)),
             DMA((MOVED, A - 1)),
             DMA((MOVED, G - 1)),
             DMA((MOVED,)),
             DMA((MOVED,)),
-            DMA((7,)),
+            DMA((1,)),
             DMA((MOVED,)),
             DMA((MOVED, A)),
             DMA((MOVED, 2)),
-            DMA((MOVED, A)),
+            DMA((MOVED,)),
             DMA((9,)),
             DMA((9,)),
         ],

time: 44.2 us -> 44 us (level)
  no operation moved by 1% of the time
where the time goes in v7:
time: 44 us; the launch traced here: 43.8 us
  Pallas kernels  43.2 us (98%)
  between operations  0.66 us (2%)
    pallas_call x1, Pallas kernels, body(): pl.pallas_call(functools.partial(kernel, dims), out_shape=tuple((V(*shape...  41.6 us
    pallas_call x1, Pallas kernels, body(): pl.pallas_call(write_out, out_shape=tuple((jax.ShapeDtypeStruct(*shape) f...  1.56 us

profile of v7, /device:TPU:0, one launch (start us, length us, event | category | flops | bytes accessed | tf_op | source)
XLA Modules:
  0.0 43.8 jit_solution(11059204675098537481)
XLA Ops:
  0.6 41.6 %shard_map.194 = (f32[1,1]{1,0:T(1,128)}, f32[2,2,64,128]{3,2,1,0:T(8,128)S(1)}, f32[12,128]{1,0:T(8,128)S(1)}, f32[4,128]{1,0:T(4,128)S(1)}, f32[2,2,64,128]{3,...) custom-call(f32[6,768]{1,0:T(8,128)} %coords_hbm.1, ...), custom_call_target="tpu_custom_call" | custom-call | tf_op jit(solution)/shard_map/pallas_call | solution.py:797
  42.3 1.6 %shard_map.195 = (f32[1,1]{1,0:T(1,128)}, f32[2,2,64,128]{3,2,1,0:T(8,128)}, f32[12,128]{1,0:T(8,128)}, f32[4,128]{1,0:T(4,128)}, f32[2,2,64,128]{3,2,1,0:T(8,12...) custom-call(f32[1,1]{1,0:T(1,128)} %get-tuple-element.33.refs_0_, ...), custom_call_target="tpu_custom_call" | custom-call | tf_op jit(solution)/shard_map/pallas_call | solution.py:868

commit v8 on v7

--- a/solution.py
+++ b/solution.py
@@ -150,7 +150,9 @@
     z_devices = [device(o, g, c) for o in far]
     g_devices = [device(a, o, c) for o in near]
     core_device = device(a, g, 1 - c)
-    q_coords = [(partner(g, kg, G), partner(c, kc, 2)) for kg in range(G) for kc in range(2)][1:]
+    q_steps = [(kg, kc) for kg in range(G) for kc in range(2)][1:]
+    q_steps.sort(key=lambda step: -(bin(step[0]).count("1") + step[1] / 2))
+    q_coords = [(partner(g, kg, G), partner(c, kc, 2)) for kg, kc in q_steps]
     q_devices = [device(a, o, cc) for o, cc in q_coords]
     steps = [(ka, kg, kc) for ka in range(A) for kg in range(G) for kc in range(2)][1:]
     steps.sort(key=lambda step: -(step[0] + bin(step[1]).count("1") + step[2] / 2))
@@ -252,8 +254,8 @@
 
     def w_far(m, ref):
         return [
-            remote(ref, ref, w_send.at[0], wz_recv.at[m, k], d) for k, d in enumerate(z_devices)
-        ]
+            remote(ref, ref, w_send.at[0], wz_recv.at[m, k], z_devices[k]) for k in reversed(range(A - 1))
+        ][::-1]
 
     def w_near(m, ref, ks):
         for k in ks:
@@ -322,7 +324,7 @@
     count = jnp.sum(mask, axis=0, keepdims=True)
     row_of_8 = lax.broadcasted_iota(jnp.int32, (8, cw), 0)
     qslot_z[a] = jnp.where(row_of_8 == 0, q_part, count)
-    for d in z_devices:
+    for d in reversed(z_devices):
         remote(qslot_z.at[a], qslot_z.at[a], s_send.at[S_QFAR], s_recv.at[S_QFAR], d)
 
     first_rows = [small_row(j) for j in range(6)]
@@ -347,7 +349,7 @@
             o = near[FARTHEST]
             ref = piece(m, o, a)
             await_bytes(ref, wn_recv.at[m, FARTHEST])
-            for d in z_devices:
+            for d in reversed(z_devices):
                 remote(ref, ref, w_send.at[0], wt_recv.at[m], d)
 
     for m in range(MOVED):
@@ -444,7 +446,7 @@
     def v_far():
         await_bytes(vslot_g.at[pl.ds(0, 2 * G - 1)], s_recv.at[S_VNEAR])
         vslot_z[a] = slot_sum(vslot_g, 2 * G)
-        for d in z_devices:
+        for d in reversed(z_devices):
             remote(vslot_z.at[a], vslot_z.at[a], s_send.at[S_VFAR], s_recv.at[S_VFAR], d)
 
     pieces = [(far[k], k) for k in reversed(range(A - 1))] + [(a, None)]
@@ -637,7 +639,7 @@
     mine_too = column == t
     slot = (dp % (cw // R)) * n_t + t
     pl.semaphore_wait(barrier, len(others))
-    for k in range(1, A * B):
+    for k in reversed(range(1, A * B)):
         remote(
             psend, pslot.at[slot], s_send.at[S_PROD], s_recv.at[S_PROD], (partner(dp, k, A * B), column)
         )
@@ -664,7 +666,7 @@
     await_bytes(sgslot_g.at[pl.ds(0, 2 * G - 1)], s_recv.at[S_NEAR])
     sgtwo[...] = slot_sum(sgslot_g, 2 * G)
     sgslot_z[a] = sgtwo[...]
-    for d in z_devices:
+    for d in reversed(z_devices):
         remote(sgtwo, sgslot_z.at[a], s_send.at[S_FAR], s_recv.at[S_FAR], d)
 
     parts = settle(MATS - 1, out_column * v_part)

time: 44 us -> 43.7 us (level)
  no operation moved by 1% of the time
where the time goes in v8:
time: 43.7 us; the launch traced here: 43.5 us
  Pallas kernels  42.9 us (98%)
  between operations  0.66 us (2%)
    pallas_call x1, Pallas kernels, body(): pl.pallas_call(functools.partial(kernel, dims), out_shape=tuple((V(*shape...  41.3 us
    pallas_call x1, Pallas kernels, body(): pl.pallas_call(write_out, out_shape=tuple((jax.ShapeDtypeStruct(*shape) f...  1.56 us

profile of v8, /device:TPU:0, one launch (start us, length us, event | category | flops | bytes accessed | tf_op | source)
XLA Modules:
  0.0 43.5 jit_solution(11872302733633189162)
XLA Ops:
  0.6 41.3 %shard_map.194 = (f32[1,1]{1,0:T(1,128)}, f32[2,2,64,128]{3,2,1,0:T(8,128)S(1)}, f32[12,128]{1,0:T(8,128)S(1)}, f32[4,128]{1,0:T(4,128)S(1)}, f32[2,2,64,128]{3,...) custom-call(f32[6,768]{1,0:T(8,128)} %coords_hbm.1, ...), custom_call_target="tpu_custom_call" | custom-call | tf_op jit(solution)/shard_map/pallas_call | solution.py:799
  42.0 1.6 %shard_map.195 = (f32[1,1]{1,0:T(1,128)}, f32[2,2,64,128]{3,2,1,0:T(8,128)}, f32[12,128]{1,0:T(8,128)}, f32[4,128]{1,0:T(4,128)}, f32[2,2,64,128]{3,2,1,0:T(8,12...) custom-call(f32[1,1]{1,0:T(1,128)} %get-tuple-element.33.refs_0_, ...), custom_call_target="tpu_custom_call" | custom-call | tf_op jit(solution)/shard_map/pallas_call | solution.py:870

commit v9 on v8

--- a/solution.py
+++ b/solution.py
@@ -24,13 +24,13 @@
 G_TURNED = (2, 1, 0)
 
 
-def partner(i, k, size):
-    bit = 1
+def partners(i, size):
+    values, bit = [i], 1
     while bit < size:
-        if (k // bit) % 2:
-            i = i + bit - 2 * bit * ((i // bit) % 2)
+        change = bit - 2 * bit * lax.rem(lax.div(i, bit), 2)
+        values = values + [value + change for value in values]
         bit *= 2
-    return i
+    return values
 
 
 def nn(left, right):
@@ -138,25 +138,26 @@
     G = C * B
     dp = lax.axis_index("dp")
     t = lax.axis_index("tensor")
-    a, b = dp // B, dp % B
-    y, c = t // 2, t % 2
+    a, b = lax.div(dp, B), lax.rem(dp, B)
+    y, c = lax.div(t, 2), lax.rem(t, 2)
     g = y * B + b
+    in_a, in_g, in_c, in_dp = partners(a, A), partners(g, G), partners(c, 2), partners(dp, A * B)
 
     def device(a_, g_, c_):
-        return (a_ * B + g_ % B, (g_ // B) * 2 + c_)
-
-    far = [partner(a, k, A) for k in range(1, A)]
-    near = [partner(g, k, G) for k in range(1, G)]
+        return (a_ * B + lax.rem(g_, B), lax.div(g_, B) * 2 + c_)
+
+    far = [in_a[k] for k in range(1, A)]
+    near = [in_g[k] for k in range(1, G)]
     z_devices = [device(o, g, c) for o in far]
     g_devices = [device(a, o, c) for o in near]
     core_device = device(a, g, 1 - c)
     q_steps = [(kg, kc) for kg in range(G) for kc in range(2)][1:]
     q_steps.sort(key=lambda step: -(bin(step[0]).count("1") + step[1] / 2))
-    q_coords = [(partner(g, kg, G), partner(c, kc, 2)) for kg, kc in q_steps]
+    q_coords = [(in_g[kg], in_c[kc]) for kg, kc in q_steps]
     q_devices = [device(a, o, cc) for o, cc in q_coords]
     steps = [(ka, kg, kc) for ka in range(A) for kg in range(G) for kc in range(2)][1:]
     steps.sort(key=lambda step: -(step[0] + bin(step[1]).count("1") + step[2] / 2))
-    everyone = [device(partner(a, ka, A), partner(g, kg, G), partner(c, kc, 2)) for ka, kg, kc in steps]
+    everyone = [device(in_a[ka], in_g[kg], in_c[kc]) for ka, kg, kc in steps]
     others = [d for d, step in zip(everyone, steps) if step[0] and (step[1] or step[2])]
 
     FARTHEST = G - 2
@@ -218,10 +219,10 @@
     pl.semaphore_wait(barrier, len(peers))
 
     def piece(m, o, z):
-        return wbuf.at[m, c, o // B, z, o % B]
+        return wbuf.at[m, c, lax.div(o, B), z, lax.rem(o, B)]
 
     def line(m, o):
-        return wbuf.at[m, c, o // B, :, o % B]
+        return wbuf.at[m, c, lax.div(o, B), :, lax.rem(o, B)]
 
     def plane(m, z):
         return wbuf.at[m, c, :, z]
@@ -441,7 +442,7 @@
         vsend[tt % 2, tt // 2] = jnp.broadcast_to(v_row[:, tt * cw : (tt + 1) * cw], (8, cw))
     vslot_g[me_near] = vsend[c, y]
     for (o, cc), d in zip(q_coords, q_devices):
-        remote(vsend.at[cc, o // B], vslot_g.at[me_near], s_send.at[S_VNEAR], s_recv.at[S_VNEAR], d)
+        remote(vsend.at[cc, lax.div(o, B)], vslot_g.at[me_near], s_send.at[S_VNEAR], s_recv.at[S_VNEAR], d)
 
     def v_far():
         await_bytes(vslot_g.at[pl.ds(0, 2 * G - 1)], s_recv.at[S_VNEAR])
@@ -605,7 +606,7 @@
         sgsend[tt % 2, tt // 2] = jnp.concatenate([r[:, tt * cw : (tt + 1) * cw] for r in rows] + tail, 0)
     sgslot_g[me_near] = sgsend[c, y]
     for (o, cc), d in zip(q_coords, q_devices):
-        remote(sgsend.at[cc, o // B], sgslot_g.at[me_near], s_send.at[S_NEAR], s_recv.at[S_NEAR], d)
+        remote(sgsend.at[cc, lax.div(o, B)], sgslot_g.at[me_near], s_send.at[S_NEAR], s_recv.at[S_NEAR], d)
     start_near(0)
 
     for copy in local[7:]:
@@ -641,7 +642,7 @@
     pl.semaphore_wait(barrier, len(others))
     for k in reversed(range(1, A * B)):
         remote(
-            psend, pslot.at[slot], s_send.at[S_PROD], s_recv.at[S_PROD], (partner(dp, k, A * B), column)
+            psend, pslot.at[slot], s_send.at[S_PROD], s_recv.at[S_PROD], (in_dp[k], column)
         )
 
     @pl.when(mine_too)

time: 43.7 us -> 43.6 us (level)
  no operation moved by 1% of the time
where the time goes in v9:
time: 43.6 us; the launch traced here: 43.5 us
  Pallas kernels  42.8 us (98%)
  between operations  0.66 us (2%)
    pallas_call x1, Pallas kernels, body(): pl.pallas_call(functools.partial(kernel, dims), out_shape=tuple((V(*shape...  41.3 us
    pallas_call x1, Pallas kernels, body(): pl.pallas_call(write_out, out_shape=tuple((jax.ShapeDtypeStruct(*shape) f...  1.56 us

profile of v9, /device:TPU:0, one launch (start us, length us, event | category | flops | bytes accessed | tf_op | source)
XLA Modules:
  0.0 43.5 jit_solution(11948564294153528811)
XLA Ops:
  0.6 41.3 %shard_map.194 = (f32[1,1]{1,0:T(1,128)}, f32[2,2,64,128]{3,2,1,0:T(8,128)S(1)}, f32[12,128]{1,0:T(8,128)S(1)}, f32[4,128]{1,0:T(4,128)S(1)}, f32[2,2,64,128]{3,...) custom-call(f32[6,768]{1,0:T(8,128)} %coords_hbm.1, ...), custom_call_target="tpu_custom_call" | custom-call | tf_op jit(solution)/shard_map/pallas_call | solution.py:800
  41.9 1.6 %shard_map.195 = (f32[1,1]{1,0:T(1,128)}, f32[2,2,64,128]{3,2,1,0:T(8,128)}, f32[12,128]{1,0:T(8,128)}, f32[4,128]{1,0:T(4,128)}, f32[2,2,64,128]{3,2,1,0:T(8,12...) custom-call(f32[1,1]{1,0:T(1,128)} %get-tuple-element.33.refs_0_, ...), custom_call_target="tpu_custom_call" | custom-call | tf_op jit(solution)/shard_map/pallas_call | solution.py:871

commit v10 on v9

--- a/solution.py
+++ b/solution.py
@@ -271,6 +271,7 @@
     first = {}
     for m in range(MOVED):
         first[m] = w_far(m, piece(m, g, a))
+    for m in range(MOVED):
         w_near(m, piece(m, g, a), reversed(range(G - 1)))
 
     for copy in local[2:7]:

time: 43.6 us -> 43.7 us (level)
  no operation moved by 1% of the time
where the time goes in v10:
time: 43.7 us; the launch traced here: 43.5 us
  Pallas kernels  42.8 us (98%)
  between operations  0.66 us (2%)
    pallas_call x1, Pallas kernels, body(): pl.pallas_call(functools.partial(kernel, dims), out_shape=tuple((V(*shape...  41.3 us
    pallas_call x1, Pallas kernels, body(): pl.pallas_call(write_out, out_shape=tuple((jax.ShapeDtypeStruct(*shape) f...  1.56 us

profile of v10, /device:TPU:0, one launch (start us, length us, event | category | flops | bytes accessed | tf_op | source)
XLA Modules:
  0.0 43.5 jit_solution(4134534165135470696)
XLA Ops:
  0.6 41.3 %shard_map.194 = (f32[1,1]{1,0:T(1,128)}, f32[2,2,64,128]{3,2,1,0:T(8,128)S(1)}, f32[12,128]{1,0:T(8,128)S(1)}, f32[4,128]{1,0:T(4,128)S(1)}, f32[2,2,64,128]{3,...) custom-call(f32[6,768]{1,0:T(8,128)} %coords_hbm.1, ...), custom_call_target="tpu_custom_call" | custom-call | tf_op jit(solution)/shard_map/pallas_call | solution.py:801
  41.9 1.6 %shard_map.195 = (f32[1,1]{1,0:T(1,128)}, f32[2,2,64,128]{3,2,1,0:T(8,128)}, f32[12,128]{1,0:T(8,128)}, f32[4,128]{1,0:T(4,128)}, f32[2,2,64,128]{3,2,1,0:T(8,12...) custom-call(f32[1,1]{1,0:T(1,128)} %get-tuple-element.33.refs_0_, ...), custom_call_target="tpu_custom_call" | custom-call | tf_op jit(solution)/shard_map/pallas_call | solution.py:872

commit v11 on v9

--- a/solution.py
+++ b/solution.py
@@ -435,15 +435,6 @@
     g_time = [2.0 * grad_time[k] * seed for k in range(3)]
     g_tau = sign_tau * (units[0] * g_time[0] + units[1] * g_time[1] + units[2] * g_time[2])
     g_proj = [g_tau] + [distance * sign_tau * g_time[k] for k in range(3)]
-    v_row = jnp.sum(
-        sum(hidden[last, s].astype(F32) * g_proj[s] for s in range(4)), axis=0, keepdims=True
-    )
-    for tt in range(n_t):
-        vsend[tt % 2, tt // 2] = jnp.broadcast_to(v_row[:, tt * cw : (tt + 1) * cw], (8, cw))
-    vslot_g[me_near] = vsend[c, y]
-    for (o, cc), d in zip(q_coords, q_devices):
-        remote(vsend.at[cc, lax.div(o, B)], vslot_g.at[me_near], s_send.at[S_VNEAR], s_recv.at[S_VNEAR], d)
-
     def v_far():
         await_bytes(vslot_g.at[pl.ds(0, 2 * G - 1)], s_recv.at[S_VNEAR])
         vslot_z[a] = slot_sum(vslot_g, 2 * G)
@@ -560,6 +551,15 @@
 
     back_last()
     back_weight(1)
+    v_row = jnp.sum(
+        sum(hidden[last, s].astype(F32) * g_proj[s] for s in range(4)), axis=0, keepdims=True
+    )
+    for tt in range(n_t):
+        vsend[tt % 2, tt // 2] = jnp.broadcast_to(v_row[:, tt * cw : (tt + 1) * cw], (8, cw))
+    vslot_g[me_near] = vsend[c, y]
+    for (o, cc), d in zip(q_coords, q_devices):
+        remote(vsend.at[cc, lax.div(o, B)], vslot_g.at[me_near], s_send.at[S_VNEAR], s_recv.at[S_VNEAR], d)
+
     tau_sum = jnp.sum(g_proj[0], axis=0, keepdims=True)
     bias_out[last] = out_row * tau_sum
     g_out_row = bias_row * tau_sum + jnp.sum(

time: 43.6 us -> 43.5 us (level)
  no operation moved by 1% of the time
where the time goes in v11:
time: 43.5 us; the launch traced here: 43.3 us
  Pallas kernels  42.7 us (98%)
  between operations  0.66 us (2%)
    pallas_call x1, Pallas kernels, body(): pl.pallas_call(functools.partial(kernel, dims), out_shape=tuple((V(*shape...  41.1 us
    pallas_call x1, Pallas kernels, body(): pl.pallas_call(write_out, out_shape=tuple((jax.ShapeDtypeStruct(*shape) f...  1.56 us

profile of v11, /device:TPU:0, one launch (start us, length us, event | category | flops | bytes accessed | tf_op | source)
XLA Modules:
  0.0 43.3 jit_solution(12707871370789941061)
XLA Ops:
  0.6 41.1 %shard_map.194 = (f32[1,1]{1,0:T(1,128)}, f32[2,2,64,128]{3,2,1,0:T(8,128)S(1)}, f32[12,128]{1,0:T(8,128)S(1)}, f32[4,128]{1,0:T(4,128)S(1)}, f32[2,2,64,128]{3,...) custom-call(f32[6,768]{1,0:T(8,128)} %coords_hbm.1, ...), custom_call_target="tpu_custom_call" | custom-call | tf_op jit(solution)/shard_map/pallas_call | solution.py:800
  41.8 1.6 %shard_map.195 = (f32[1,1]{1,0:T(1,128)}, f32[2,2,64,128]{3,2,1,0:T(8,128)}, f32[12,128]{1,0:T(8,128)}, f32[4,128]{1,0:T(4,128)}, f32[2,2,64,128]{3,2,1,0:T(8,12...) custom-call(f32[1,1]{1,0:T(1,128)} %get-tuple-element.33.refs_0_, ...), custom_call_target="tpu_custom_call" | custom-call | tf_op jit(solution)/shard_map/pallas_call | solution.py:871
